TPU v7x, 128 devices: a whole 4x4x4 slice. The times are simulated.
128 devices in a mesh: gx: 2 (over z_lo), gy: 4 (over x), mem: 16 (over z_hi, y, core).
Axes of the slice: x: 4, y: 4, z: 4 (z_hi: 2, z_lo: 2; z = z_hi * 2 + z_lo), core: 2. Of those that a mesh axis runs over, the one named last changes fastest.
Arguments:
- prior_members: float32 [8, 512, 128, 512], P(None, 'mem', 'gx', 'gy'), may hold values from -30 to 30
- courant_x: float32 [128, 512], P('gx', 'gy'), may hold values from -0.4 to 0.4
- courant_y: float32 [128, 512], P('gx', 'gy'), may hold values from -0.4 to 0.4
- diffusion: float32 [128, 512], P('gx', 'gy'), may hold values from 0.01 to 0.05
- report_level: int32 [32, 4, 256], P('gx', 'gy'), may hold values from 0 to 3
- report_cell: int32 [32, 4, 256], P('gx', 'gy'), may hold values from 0 to 511
- report_value: float32 [32, 4, 256], P('gx', 'gy'), may hold values from -6 to 6
- report_precision: float32 [32, 4, 256], P('gx', 'gy'), may hold values from 0.5 to 4
- report_class: int32 [32, 4, 256], P('gx', 'gy'), may hold values from 0 to 7
- report_count: int32 [32, 4], P('gx', 'gy'), may hold values from 64 to 256, as said below
Outputs:
- analysis: float32 [8, 512, 128, 512], P(None, 'mem', 'gx', 'gy')
Inputs may be any that keep to these rules, and one draw needn't show every extreme that they name: A tile uses observation slots 0 to report_count - 1; some tile uses all 256.
All inputs are finite; a program needn't handle non-finite values.
Results may differ from a plain program's by a relative error of at most 0.0003.
Values sent between devices are 32-bit elements; how exact they have to be, the bound alone decides.
No kernel may reach another device: no remote copies, remote signals or barrier semaphores. Data moves between devices by JAX's collectives and lax.ppermute only.
A program may use at most 192 MiB of HBM per device.

v0:
```python
import functools

import jax
import jax.numpy as jnp
from jax import lax
from jax.experimental import pallas as pl
from jax.experimental.pallas import tpu as pltpu
from jax.sharding import PartitionSpec as P

NEWTON = 8
LANES = 128
VMEM_LIMIT = 58 * 1024 * 1024
PACK_LIMIT = 58 * 1024 * 1024


def iota(shape, dim):
    return lax.broadcasted_iota(jnp.int32, shape, dim)


HEIGHT = 4
SPREAD = 32
PITCH = 8
CHIPS = ((0, 0), (1, 0), (0, 2), (1, 1), (0, 3), (1, 3), (0, 1), (1, 2))
OFFSETS = tuple(chip + (core,) for chip in CHIPS for core in range(2))
COUNT = len(OFFSETS)
EARLY, LATE = 5, 7
GROUPS = ((0,), (1, 2), (3, 4), (5, 6), (7,))


def shifted(index, offset, sign=1):
    z, y, core = index // 8, index // 2 % 4, index % 2
    dz, dy, dc = offset
    return (z + dz) % 2 * 8 + (y + sign * dy + 4) % 4 * 2 + (core + dc) % 2


def pair_spec(piece):
    return pl.BlockSpec((2, 1, piece, LANES), lambda i: (0, i, 0, 0))


def piece_specs(pieces):
    def spec(array, lead):
        return pl.BlockSpec((1, 1) + array.shape[2:], lambda i: (lead, i, 0, 0))

    return [spec(*p) for p in pieces]


def arrays(pieces):
    return [p[0] for p in pieces]


def pack_kernel(first, fields, rows, members, x_ref, cx_ref, cy_ref, df_ref, *refs):
    edge_ref, row_ref, corner_ref, held, sems = refs[-5:]
    step = pl.program_id(0)
    pitch = rows + PITCH
    picked = (0, 1, rows - 2, rows - 1)
    groups = rows // SPREAD

    def copy(field):
        return pltpu.make_async_copy(
            x_ref.at[first + field], held.at[field, :, pl.ds(0, rows), :], sems.at[field]
        )

    @pl.when(step == 0)
    def _():
        for field in range(fields):
            copy(field).start()

    def gather(read, tall):
        lane = iota((tall, LANES), 1)
        packed = []
        for group in range(groups):
            parts = [jnp.zeros((tall, LANES), jnp.float32) for _ in range(4)]
            for i in range(SPREAD):
                moved = pltpu.roll(read(group * SPREAD + i), (4 * i + 2) % LANES, 1)
                parts[i % 4] = jnp.where(lane // 4 == i, moved, parts[i % 4])
            packed.append((parts[0] + parts[1]) + (parts[2] + parts[3]))
            edge_ref[0, group, 0:tall, :] = packed[group]
        corner_ref[0, 0:tall, :] = jnp.where(lane < LANES // 2, packed[0], packed[-1])

    for field in range(fields):

        @pl.when(step == field)
        def _():
            copy(field).wait()
            flat = held.at[field].reshape(members * pitch, LANES)

            def read(row):
                value = flat[pl.ds(row, members, stride=pitch), :]
                if row in picked:
                    row_ref[0, picked.index(row)] = value
                return value

            gather(read, members)

    @pl.when(step == fields)
    def _():
        sub = iota((8, LANES), 0)
        row_ref[0] = jnp.zeros((4, members, LANES), jnp.float32)
        edge_ref[0] = jnp.zeros((groups, members, LANES), jnp.float32)
        corner_ref[0] = jnp.zeros((members, LANES), jnp.float32)

        def read(row):
            at = slice(row, row + 1)
            value = jnp.where(
                sub == 0, cx_ref[at, :], jnp.where(sub == 1, cy_ref[at, :], df_ref[at, :])
            )
            if row in picked:
                row_ref[0, picked.index(row), 0:8, :] = value
            return value

        gather(read, 8)


def pack(x, coefficients, first, fields, after=()):
    _, members, rows, _ = x.shape
    small = pl.BlockSpec((rows, LANES), lambda i: (0, 0))
    groups = rows // SPREAD
    return pl.pallas_call(
        functools.partial(pack_kernel, first, fields, rows, members),
        grid=(fields + 1,),
        in_specs=[pl.BlockSpec(memory_space=pl.ANY), small, small, small]
        + [pl.BlockSpec(memory_space=pl.ANY) for _ in after],
        out_specs=[
            pl.BlockSpec((1, groups, members, LANES), lambda i: (i, 0, 0, 0)),
            pl.BlockSpec((1, 4, members, LANES), lambda i: (i, 0, 0, 0)),
            pl.BlockSpec((1, members, LANES), lambda i: (i, 0, 0)),
        ],
        out_shape=[
            jax.ShapeDtypeStruct((fields + 1, groups, members, LANES), jnp.float32),
            jax.ShapeDtypeStruct((fields + 1, 4, members, LANES), jnp.float32),
            jax.ShapeDtypeStruct((fields + 1, members, LANES), jnp.float32),
        ],
        scratch_shapes=[
            pltpu.VMEM((fields, members, rows + PITCH, LANES), jnp.float32),
            pltpu.SemaphoreType.DMA((fields,)),
        ],
        compiler_params=pltpu.CompilerParams(vmem_limit_bytes=PACK_LIMIT),
        cost_estimate=pl.CostEstimate(
            flops=fields * members * rows * LANES * 2,
            bytes_accessed=fields * members * rows * LANES * 8,
            transcendentals=0,
        ),
        name="pack_edges",
    )(x, *coefficients, *after)


def exchange(packed):
    edge, row, corner = packed
    nx, ny = lax.axis_size("gx"), lax.axis_size("gy")
    right = [(i, (i + 1) % ny) for i in range(ny)]
    left = [(i, (i - 1) % ny) for i in range(ny)]

    def diagonal(step):
        return [
            (a * ny + b, ((a + 1) % nx) * ny + (b + step) % ny) for a in range(nx) for b in range(ny)
        ]

    return (
        lax.ppermute(row, "gx", [(i, (i + 1) % nx) for i in range(nx)]),
        lax.ppermute(edge, "gy", right),
        lax.ppermute(edge, "gy", left),
        lax.ppermute(corner, ("gx", "gy"), diagonal(1)),
        lax.ppermute(corner, ("gx", "gy"), diagonal(-1)),
    )


def weights_of(cx, cy, spread):
    plus_x, minus_x = jnp.maximum(cx, 0.0), jnp.minimum(cx, 0.0)
    plus_y, minus_y = jnp.maximum(cy, 0.0), jnp.minimum(cy, 0.0)
    centre = 1.0 - (plus_x - minus_x) - (plus_y - minus_y) - 4.0 * spread
    return centre, plus_x + spread, spread - minus_x, plus_y + spread, spread - minus_y


def stencil(k, centre, west, east, south, north):
    return k[0] * centre + k[1] * west + k[2] * east + k[3] * south + k[4] * north


def forecast_kernel(first, fields, rows, members, dest_ref, x_hbm, cx_ref, cy_ref, df_ref, own_ref, left_ref, right_ref, left_k_ref, right_k_ref, row_ref, row_k_ref, dl_ref, dr_ref, *refs):
    out_refs = refs[: len(CHIPS)]
    k_main, k_edge, k_row, edge_s, first_s, x_s, second_s, beside_s, held, sems = refs[len(CHIPS) :]
    step = pl.program_id(0)
    pitch = rows + PITCH

    def copy(field):
        slot = lax.rem(field, 2)
        return pltpu.make_async_copy(
            x_hbm.at[first + field], held.at[slot, :, pl.ds(0, rows), :], sems.at[slot]
        )

    @pl.when(step == 0)
    def _():
        copy(step).start()

    @pl.when(step + 1 < fields)
    def _():
        copy(step + 1).start()

    copy(step).wait()
    flat = held.at[lax.rem(step, 2)].reshape(members * pitch, LANES)
    for row in range(rows):
        x_s[row] = flat[pl.ds(row, members, stride=pitch), :]
    lane = iota((members, LANES), 1)
    from_left = lane % 4 < 2
    groups = rows // SPREAD

    @pl.when(pl.program_id(0) == 0)
    def _():
        for i, w in enumerate(weights_of(cx_ref[...], cy_ref[...], df_ref[...])):
            k_main[i] = w
        for group in range(groups):
            both = jnp.where(from_left[0:8], left_k_ref[0, group, 0:8, :], right_k_ref[0, group, 0:8, :])
            for i, w in enumerate(weights_of(*[both[j : j + 1, :] for j in range(3)])):
                k_edge[group, i : i + 1, :] = w
        for side, at in ((0, 3), (1, 0)):
            for i, w in enumerate(weights_of(*[row_k_ref[0, at, j : j + 1, :] for j in range(3)])):
                k_row[side, i : i + 1, :] = w

    edges = [jnp.where(from_left, left_ref[0, g], right_ref[0, g]) for g in range(groups)]
    corner = jnp.where(from_left, dl_ref[0], dr_ref[0])
    chain = [corner] + edges + [corner]
    up = [pltpu.roll(v, 4, 1) for v in chain]
    down = [pltpu.roll(v, LANES - 4, 1) for v in chain]
    for group, edge in enumerate(edges):
        own = own_ref[0, group]
        edge_s[0, group] = edge
        edge_s[1, group] = stencil(
            [k_edge[group, i : i + 1, :] for i in range(5)],
            edge,
            jnp.where(lane < 4, up[group], up[group + 1]),
            jnp.where(lane >= LANES - 4, down[group + 2], down[group + 1]),
            pltpu.roll(jnp.where(lane % 4 == 0, edge, own), 1, 1),
            pltpu.roll(jnp.where(lane % 4 == 3, edge, own), LANES - 1, 1),
        )

    def sides(centre, beside):
        return (
            pltpu.roll(jnp.where(lane == LANES - 1, beside, centre), 1, 1),
            pltpu.roll(jnp.where(lane == 0, beside, centre), LANES - 1, 1),
        )

    for side, (centre, west, east, turn, at) in enumerate(
        (
            (row_ref[0, 3], row_ref[0, 2], x_s[0], 2, 0),
            (row_ref[0, 0], x_s[rows - 1], row_ref[0, 1], LANES - 2, rows + 1),
        )
    ):
        k = [k_row[side, i : i + 1, :] for i in range(5)]
        first_s[at] = stencil(k, centre, west, east, *sides(centre, pltpu.roll(corner, turn, 1)))

    def lay_sides(stage):
        for row in range(rows):
            turn = (126 - row % SPREAD * 4) % LANES
            beside_s[row] = pltpu.roll(edge_s[stage, row // SPREAD], turn, 1)

    def one(row, centre, west, east):
        k = [k_main[i, row : row + 1, :] for i in range(5)]
        return stencil(k, centre, west, east, *sides(centre, beside_s[row]))

    lay_sides(0)
    for row in range(rows):
        west = row_ref[0, 3] if row == 0 else x_s[row - 1]
        east = row_ref[0, 0] if row == rows - 1 else x_s[row + 1]
        first_s[row + 1] = one(row, x_s[row], west, east)
    lay_sides(1)
    for row in range(rows):
        second_s[row] = one(row, first_s[row + 1], first_s[row], first_s[row + 2])
    for i in range(COUNT):
        base = dest_ref[i] * HEIGHT
        for r in range(HEIGHT):
            out_refs[i // 2][i % 2, 0, r * members : (r + 1) * members, :] = second_s[base + r]


def forecast(x, coefficients, edge, moved, moved_k, dest, first, fields):
    _, members, rows, _ = x.shape
    row, left, right, corner_l, corner_r = moved
    row_k, left_k, right_k = moved_k
    last = row_k.shape[0] - 1
    groups = rows // SPREAD
    small = pl.BlockSpec((rows, LANES), lambda i: (0, 0))
    edge_spec = pl.BlockSpec((1, groups, members, LANES), lambda i: (i, 0, 0, 0))
    edge_last = pl.BlockSpec((1, groups, members, LANES), lambda i: (last, 0, 0, 0))
    corner_spec = pl.BlockSpec((1, members, LANES), lambda i: (i, 0, 0))
    piece = HEIGHT * members
    return pl.pallas_call(
        functools.partial(forecast_kernel, first, fields, rows, members),
        grid=(fields,),
        in_specs=[
            pl.BlockSpec(memory_space=pltpu.SMEM),
            pl.BlockSpec(memory_space=pl.ANY),
            small,
            small,
            small,
            edge_spec,
            edge_spec,
            edge_spec,
            edge_last,
            edge_last,
            pl.BlockSpec((1, 4, members, LANES), lambda i: (i, 0, 0, 0)),
            pl.BlockSpec((1, 4, members, LANES), lambda i: (last, 0, 0, 0)),
            corner_spec,
            corner_spec,
        ],
        out_specs=[pair_spec(piece)] * len(CHIPS),
        out_shape=[jax.ShapeDtypeStruct((2, fields, piece, LANES), jnp.float32)] * len(CHIPS),
        scratch_shapes=[
            pltpu.VMEM((5, rows, LANES), jnp.float32),
            pltpu.VMEM((groups, 8, LANES), jnp.float32),
            pltpu.VMEM((2, 8, LANES), jnp.float32),
            pltpu.VMEM((2, groups, members, LANES), jnp.float32),
            pltpu.VMEM((rows + 2, members, LANES), jnp.float32),
            pltpu.VMEM((rows, members, LANES), jnp.float32),
            pltpu.VMEM((rows, members, LANES), jnp.float32),
            pltpu.VMEM((rows, members, LANES), jnp.float32),
            pltpu.VMEM((2, members, rows + PITCH, LANES), jnp.float32),
            pltpu.SemaphoreType.DMA((2,)),
        ],
        compiler_params=pltpu.CompilerParams(vmem_limit_bytes=PACK_LIMIT),
        cost_estimate=pl.CostEstimate(
            flops=fields * rows * members * LANES * 18,
            bytes_accessed=fields * rows * members * LANES * 8,
            transcendentals=0,
        ),
        name="forecast",
    )(dest, x, *coefficients, edge, left, right, left_k, right_k, row, row_k, corner_l, corner_r)


def halves(value):
    high = value.astype(jnp.bfloat16)
    return high, (value - high.astype(jnp.float32)).astype(jnp.bfloat16)


def dot(a, b):
    return jnp.dot(a, b, preferred_element_type=jnp.float32)


def tile_rows(refs, r):
    tall = refs[0].shape[2] // HEIGHT
    return jnp.concatenate([ref[0, 0, r * tall : (r + 1) * tall, :] for ref in refs], axis=0)


def sample_kernel(place_ref, *refs):
    step = pl.program_id(0)
    x_refs, out_ref = refs[:COUNT], refs[-1]
    slots = place_ref.shape[1]
    cells = HEIGHT * LANES
    x = jnp.concatenate([tile_rows(x_refs, r) for r in range(HEIGHT)], axis=1)
    chosen = (iota((cells, slots), 0) + step * cells == place_ref[0:1, :]).astype(jnp.bfloat16)
    high = x.astype(jnp.bfloat16)
    middle, low = halves(x - high.astype(jnp.float32))
    got = dot(high, chosen) + dot(middle, chosen) + dot(low, chosen)

    @pl.when(step == 0)
    def _():
        out_ref[...] = got

    @pl.when(step > 0)
    def _():
        out_ref[...] += got


def sample(pieces, place, after):
    _, fields, piece, _ = pieces[0][0].shape
    members = COUNT * piece // HEIGHT
    slots = place.shape[1]
    return pl.pallas_call(
        sample_kernel,
        grid=(fields,),
        in_specs=[pl.BlockSpec((1, slots), lambda i: (0, 0))]
        + piece_specs(pieces)
        + [pl.BlockSpec(memory_space=pl.ANY) for _ in after],
        out_specs=pl.BlockSpec((members, slots), lambda i: (0, 0)),
        out_shape=jax.ShapeDtypeStruct((members, slots), jnp.float32),
        compiler_params=pltpu.CompilerParams(vmem_limit_bytes=VMEM_LIMIT),
        cost_estimate=pl.CostEstimate(
            flops=fields * members * HEIGHT * LANES * slots * 6,
            bytes_accessed=fields * members * HEIGHT * LANES * 4,
            transcendentals=0,
        ),
        name="sample",
    )(place, *arrays(pieces), *after)


def transform_kernel(mix_ref, *refs):
    x_refs, out_refs, (high_s, low_s) = refs[:COUNT], refs[COUNT:-2], refs[-2:]

    @pl.when(pl.program_id(0) == 0)
    def _():
        high_s[...], low_s[...] = halves(mix_ref[...])

    tall = x_refs[0].shape[2] // HEIGHT
    members = COUNT * tall
    for half in range(HEIGHT // 2):
        x = jnp.concatenate([tile_rows(x_refs, 2 * half + i) for i in range(2)], axis=1)
        centre = jnp.sum(x, axis=0, keepdims=True) / members
        high, low = halves(x - centre)
        result = dot(high_s[...], high) + (dot(high_s[...], low) + dot(low_s[...], high)) + centre
        for i in range(2):
            at = (2 * half + i) * tall
            for o in range(COUNT):
                out_refs[o // 2][o % 2, 0, at : at + tall, :] = result[
                    o * tall : (o + 1) * tall, i * LANES : (i + 1) * LANES
                ]


def transform(pieces, mixing_t):
    _, fields, piece, _ = pieces[0][0].shape
    members = mixing_t.shape[0]
    return pl.pallas_call(
        transform_kernel,
        grid=(fields,),
        in_specs=[pl.BlockSpec((members, members), lambda i: (0, 0))] + piece_specs(pieces),
        out_specs=[pair_spec(piece)] * len(CHIPS),
        out_shape=[jax.ShapeDtypeStruct((2, fields, piece, LANES), jnp.float32)] * len(CHIPS),
        scratch_shapes=[
            pltpu.VMEM((members, members), jnp.bfloat16),
            pltpu.VMEM((members, members), jnp.bfloat16),
        ],
        compiler_params=pltpu.CompilerParams(vmem_limit_bytes=VMEM_LIMIT),
        cost_estimate=pl.CostEstimate(
            flops=fields * members * members * HEIGHT * LANES * 6,
            bytes_accessed=fields * members * HEIGHT * LANES * 8,
            transcendentals=0,
        ),
        name="transform",
    )(mixing_t, *arrays(pieces))


def unpack_kernel(members, rows, dest_ref, *refs):
    x_refs, out_ref, held = refs[:COUNT], refs[-2], refs[-1]
    pitch = rows + 4
    for i in range(COUNT):
        base = dest_ref[i] * HEIGHT
        for r in range(HEIGHT):
            held[pl.ds(base + r, members, stride=pitch), :] = x_refs[i][0, 0, r * members : (r + 1) * members, :]
    for m in range(members):
        out_ref[0, m * rows : (m + 1) * rows, :] = held[m * pitch : m * pitch + rows, :]


def unpack(pieces, so_far, dest, first, total, members, rows):
    _, fields, piece, _ = pieces[0][0].shape
    flat = members * rows
    more = () if so_far is None else (so_far,)
    return pl.pallas_call(
        functools.partial(unpack_kernel, members, rows),
        grid=(fields,),
        in_specs=[pl.BlockSpec(memory_space=pltpu.SMEM)]
        + piece_specs(pieces)
        + [pl.BlockSpec(memory_space=pl.ANY) for _ in more],
        out_specs=pl.BlockSpec((1, flat, LANES), lambda i: (first + i, 0, 0)),
        out_shape=jax.ShapeDtypeStruct((total, flat, LANES), jnp.float32),
        scratch_shapes=[pltpu.VMEM((members * (rows + 4), LANES), jnp.float32)],
        input_output_aliases={COUNT + 1: 0} if more else {},
        compiler_params=pltpu.CompilerParams(vmem_limit_bytes=VMEM_LIMIT),
        cost_estimate=pl.CostEstimate(
            flops=0, bytes_accessed=fields * flat * LANES * 8, transcendentals=0
        ),
        name="unpack",
    )(dest, *arrays(pieces), *more)


def hop(value, offset, sign):
    return lax.ppermute(value, "mem", [(i, shifted(i, offset, sign)) for i in range(COUNT)])


def travel(sent, sign, skip=0):
    return [
        value if chip == (0, 0) else hop(value, chip + (0,), sign)
        for value, chip in zip(sent, CHIPS[skip:])
    ]


def trade(arrived, group):
    return hop(jnp.concatenate([arrived[o][1:2] for o in group], axis=0), (0, 0, 1), 1)


def settled(arrived, traded):
    pieces = []
    for group, value in zip(GROUPS, traded):
        for at, o in enumerate(group):
            pieces += [(arrived[o], 0), (value, at)]
    return pieces


def spread_out(sent, sign):
    arrived = travel(sent, sign)
    return settled(arrived, [trade(arrived, group) for group in GROUPS])


def dot3(a, b, dims=(1, 0)):
    (ah, al), (bh, bl) = halves(a), halves(b)

    def one(u, v):
        return lax.dot_general(
            u, v, (((dims[0],), (dims[1],)), ((), ())), preferred_element_type=jnp.float32
        )

    return one(ah, bh) + (one(ah, bl) + one(al, bh))


def mixing_kernel(count_ref, raw_ref, value_ref, precision_ref, class_ref, out_ref):
    members, slots = raw_ref.shape
    raw = raw_ref[...]
    centre_obs = jnp.sum(raw, axis=0, keepdims=True) / members
    usable = iota((1, slots), 1) < count_ref[0]
    weight = jnp.where(usable, precision_ref[...] / (1.0 + class_ref[...].astype(jnp.float32)), 0.0)
    root_weight = jnp.sqrt(weight)
    spread = (raw - centre_obs) * root_weight
    small = dot3(spread, spread, (0, 0))
    inflation = members - 1.0
    scale = jnp.sqrt(
        inflation * inflation * members
        + 2.0 * inflation * jnp.sum(spread * spread, keepdims=True)
        + jnp.sum(small * small, keepdims=True)
    )
    eye = (iota((slots, slots), 0) == iota((slots, slots), 1)).astype(jnp.float32)
    start = inflation / scale
    y, z = start, jnp.ones_like(start)
    root_y = start * eye + small / scale
    factor = 1.5 * eye - 0.5 * root_y
    p = 1.5 - 0.5 * y
    root_z, part_z, z = factor, -0.5 * eye, p
    root_y, y = dot3(root_y, factor), y * p
    for iteration in range(1, NEWTON):
        both = dot3(jnp.concatenate([root_z, part_z], axis=0), root_y)
        part = z * (start * part_z + root_z) + both[slots:]
        factor = 1.5 * eye - 0.5 * both[:slots]
        p = 1.5 - 0.5 * z * y
        both = dot3(jnp.concatenate([factor, -0.5 * part], axis=0), root_z)
        if iteration + 1 < NEWTON:
            root_y, y = dot3(root_y, factor), y * p
        root_z, part_z, z = both[:slots], p * part_z + both[slots:], z * p
    driven = jnp.broadcast_to(root_weight * (value_ref[...] - centre_obs), (8, slots))
    driven = dot3(dot3(driven, root_z), root_z)
    shift = dot3(driven, spread, (1, 1))[0:1] / scale
    gain = jnp.sqrt(inflation / scale)
    low_rank = dot3(dot3(spread, part_z * (gain / scale)), spread, (1, 1))
    whole = iota((members, members), 0) == iota((members, members), 1)
    out_ref[...] = low_rank + jnp.where(whole, gain * z, 0.0) + shift


def mixing_transposed(raw_values, report_value, report_precision, report_class, slot_count):
    members, slots = raw_values.shape
    row = pl.BlockSpec((1, slots), lambda: (0, 0))
    return pl.pallas_call(
        mixing_kernel,
        in_specs=[
            pl.BlockSpec(memory_space=pltpu.SMEM),
            pl.BlockSpec((members, slots), lambda: (0, 0)),
            row,
            row,
            row,
        ],
        out_specs=pl.BlockSpec((members, members), lambda: (0, 0)),
        out_shape=jax.ShapeDtypeStruct((members, members), jnp.float32),
        compiler_params=pltpu.CompilerParams(vmem_limit_bytes=VMEM_LIMIT),
        cost_estimate=pl.CostEstimate(
            flops=NEWTON * 5 * 6 * slots**3, bytes_accessed=4 * members * members, transcendentals=0
        ),
        name="mixing",
    )(
        slot_count.reshape(1),
        raw_values,
        report_value[None, :],
        report_precision[None, :],
        report_class[None, :],
    )


def own_row(table, tile):
    flat_table = table.reshape((table.shape[0] * table.shape[1],) + table.shape[2:])
    return lax.dynamic_index_in_dim(flat_table, tile, 0, keepdims=False)


def on_device(
    prior_members,
    courant_x,
    courant_y,
    diffusion,
    report_level,
    report_cell,
    report_value,
    report_precision,
    report_class,
    report_count,
):
    total, members, rows, _ = prior_members.shape
    coefficients = (courant_x, courant_y, diffusion)
    tile = lax.axis_index("mem")
    dest = jnp.stack([shifted(tile, o) for o in OFFSETS]).astype(jnp.int32)
    half = total // 2

    def fields_sent(packed, moved, moved_k, first):
        return list(
            forecast(prior_members, coefficients, packed[0], moved, moved_k, dest, first, half)
        )

    packed = pack(prior_members, coefficients, 0, half)
    moved_k = exchange(packed)
    sent = fields_sent(packed, moved_k, moved_k[:3], 0)
    arrived = travel(sent[:EARLY], 1)
    traded = [trade(arrived, GROUPS[0])]
    later = pack(prior_members, coefficients, half, half, traded)
    later, sent[EARLY:] = lax.optimization_barrier((later, sent[EARLY:]))
    moved = exchange(later)
    following = fields_sent(later, moved, moved_k[:3], half)
    following, sent[LATE:] = lax.optimization_barrier((following, sent[LATE:]))
    arrived += travel(sent[EARLY:], 1, EARLY)
    traded += [trade(arrived, group) for group in GROUPS[1:]]
    sent = following
    traded, sent[EARLY:] = lax.optimization_barrier((traded, sent[EARLY:]))
    gathered = settled(arrived, traded)

    level, cell = own_row(report_level, tile), own_row(report_cell, tile)
    place = (level * (HEIGHT * LANES) + cell)[None, :]
    mixing_t = mixing_transposed(
        sample(gathered, place, sent[:1]),
        own_row(report_value, tile),
        own_row(report_precision, tile),
        own_row(report_class, tile),
        own_row(report_count, tile),
    )
    mixing_t, sent[EARLY:] = lax.optimization_barrier((mixing_t, sent[EARLY:]))
    analysed = list(transform(gathered, mixing_t))
    analysed, sent[LATE:] = lax.optimization_barrier((analysed, sent[LATE:]))
    gathered = spread_out(sent, 1)

    arrived = travel(analysed[:EARLY], -1)
    traded = [trade(arrived, GROUPS[0])]
    ready = list(transform(gathered, mixing_t))
    ready, analysed[EARLY:] = lax.optimization_barrier((ready, analysed[EARLY:]))
    arrived += travel(analysed[EARLY:], -1, EARLY)
    traded += [trade(arrived, group) for group in GROUPS[1:]]
    traded, ready[EARLY:] = lax.optimization_barrier((traded, ready[EARLY:]))
    returned = [settled(arrived, traded), spread_out(ready, -1)]
    result = unpack(returned[0], None, dest, 0, total, members, rows)
    result = unpack(returned[1], result, dest, half, total, members, rows)
    return result.reshape(prior_members.shape)


def solution(mesh):
    in_specs = (
        P(None, "mem", "gx", "gy"),
        P("gx", "gy"),
        P("gx", "gy"),
        P("gx", "gy"),
        P("gx", "gy", None),
        P("gx", "gy", None),
        P("gx", "gy", None),
        P("gx", "gy", None),
        P("gx", "gy", None),
        P("gx", "gy"),
    )
    out_specs = P(None, "mem", "gx", "gy")
    return jax.shard_map(
        on_device, mesh=mesh, in_specs=in_specs, out_specs=out_specs, check_vma=False
    )
```

profile of v0, /device:TPU:1, one launch (start us, length us, event | category | flops | bytes accessed | tf_op | source)
XLA Modules:
  0.0 311.1 jit_solution(5652010035172512067)
XLA Ops:
  0.0 4.8 %pack_edges.2 = (f32[5,2,32,128]{3,2,1,0:T(8,128)}, f32[5,4,32,128]{3,2,1,0:T(8,128)}, f32[5,32,128]{2,1,0:T(8,128)}) custom-call(f32[8,32,64,128]{3,2,1,0:T(8,128)} %x_hbm.3, f32[64,128]{1,0:T(8,128)} %cx_ref.7, f32[64,128]{1,0:T(8,128)} %cy_ref.7, f32[64,128]{1,0:T(8,128)} %df_ref.7), custom_call_target="tpu_custom_call" | custom-call | flops 2097152 | bytes 8388608 | tf_op jit(solution)/shard_map/pack_edges/pallas_call | solution.py:118
  19.6 12.4 %forecast.2 = (f32[2,4,128,128]{3,2,1,0:T(8,128)}, f32[2,4,128,128]{3,2,1,0:T(8,128)}, f32[2,4,128,128]{3,2,1,0:T(8,128)}, f32[2,4,128,128]{3,2,1,0:T(8,128)}, f...) custom-call(s32[16]{0:T(128)} %stack.67.dest_ref, ...), custom_call_target="tpu_custom_call" | custom-call | flops 18874368 | bytes 8388608 | tf_op jit(solution)/shard_map/forecast/pallas_call | solution.py:284
  40.0 4.8 %pack_edges.3 = (f32[5,2,32,128]{3,2,1,0:T(8,128)}, f32[5,4,32,128]{3,2,1,0:T(8,128)}, f32[5,32,128]{2,1,0:T(8,128)}) custom-call(f32[8,32,64,128]{3,2,1,0:T(8,128)} %x_hbm.3, f32[64,128]{1,0:T(8,128)} %cx_ref.7, f32[64,128]{1,0:T(8,128)} %cy_ref.7, f32[64,128]{1,0:T(8,128)} %df_ref.7, f32[1,4,128,128]{3,2,1,0:T(8,128)} %copy-done.38), custom_call_target="tpu_custom_call" | custom-call | flops 2097152 | bytes 8388608 | tf_op jit(solution)/shard_map/pack_edges/pallas_call | solution.py:118
  57.1 4.2 %collective-permute-done.15.left_ref = f32[5,2,32,128]{3,2,1,0:T(8,128)S(1)} collective-permute-done((f32[5,2,32,128]{3,2,1,0:T(8,128)}, f32[5,2,32,128]{3,2,1,0:T(8,128)S(1)}, u32[]{:S(2)}, u32[]{:S(2)}) %collective-permute-start.15) | collective-permute-done | bytes 163872 | tf_op jit(solution)/shard_map/ppermute | solution.py:160
  66.0 12.4 %forecast.3 = (f32[2,4,128,128]{3,2,1,0:T(8,128)}, f32[2,4,128,128]{3,2,1,0:T(8,128)}, f32[2,4,128,128]{3,2,1,0:T(8,128)}, f32[2,4,128,128]{3,2,1,0:T(8,128)}, f...) custom-call(s32[16]{0:T(128)} %stack.67.dest_ref, ...), custom_call_target="tpu_custom_call" | custom-call | flops 18874368 | bytes 8388608 | tf_op jit(solution)/shard_map/forecast/pallas_call | solution.py:284
  78.4 9.6 %collective-permute-start.20 = (f32[2,4,128,128]{3,2,1,0:T(8,128)S(1)}, f32[2,4,128,128]{3,2,1,0:T(8,128)S(1)}, u32[]{:S(2)}, u32[]{:S(2)}) collective-permute-start(f32[2,4,128,128]{3,2,1,0:T(8,128)S(1)} %copy-done.58), channel_id=1, source_target_pairs={{0,12},{1,13},{2,14},{3,15},{4,8},{5,9},{6,10},{7,11},{8,4},{9,5},... | collective-permute-start | bytes 1572872 | tf_op jit(solution)/shard_map/ppermute | solution.py:462
  88.1 3.8 %collective-permute-start.23 = (f32[2,4,128,128]{3,2,1,0:T(8,128)}, f32[2,4,128,128]{3,2,1,0:T(8,128)}, u32[]{:S(2)}, u32[]{:S(2)}) collective-permute-start(f32[2,4,128,128]{3,2,1,0:T(8,128)} %get-tuple-element.140), channel_id=1, source_target_pairs={{0,8},{1,9},{2,10},{3,11},{4,12},{5,13},{6,14},{7,15},{8,0},{9,1},... | collective-permute-start | bytes 1572872 | tf_op jit(solution)/shard_map/ppermute | solution.py:462
  92.7 19.8 %collective-permute-start.8 = (f32[2,4,128,128]{3,2,1,0:T(8,128)}, f32[2,4,128,128]{3,2,1,0:T(8,128)S(1)}, u32[]{:S(2)}, u32[]{:S(2)}) collective-permute-start(f32[2,4,128,128]{3,2,1,0:T(8,128)} %pad_maximum_fusion), channel_id=1, source_target_pairs={{0,1},{1,0},{2,3},{3,2},{4,5},{5,4},{6,7},{7,6},{8,9},{9,8},{10,11... | collective-permute-start | bytes 1572872 | tf_op jit(solution)/shard_map/ppermute | solution.py:462
  116.7 3.6 %collective-permute-start.21 = (f32[1,4,128,128]{3,2,1,0:T(8,128)S(1)}, f32[1,4,128,128]{3,2,1,0:T(8,128)S(1)}, u32[]{:S(2)}, u32[]{:S(2)}) collective-permute-start(f32[1,4,128,128]{3,2,1,0:T(8,128)S(1)} %slice.134), channel_id=1, source_target_pairs={{0,1},{1,0},{2,3},{3,2},{4,5},{5,4},{6,7},{7,6},{8,9},{9,8},{10,11... | collective-permute-start | bytes 786440 | tf_op jit(solution)/shard_map/ppermute | solution.py:462
  133.9 5.3 %sample.1.raw_ref = f32[512,256]{1,0:T(8,128)} custom-call(s32[1,256]{1,0:T(1,128)} %fusion.5.place_ref, f32[2,4,128,128]{3,2,1,0:T(8,128)} %get-tuple-element.101.refs_0_, f32[1,4,128,128]{3,2,1,0:T(8,128)} %copy-done.38, f32[2,4,128,128]{3,2,1,0:T(8,128)} %copy-done.19, f32[2,4,128,128]{3,2,1,0:T(8,128)} %copy-done.6, f32[2,4,128,128]{3,2,1,0:T(8,128)} %copy-done.22, ...), custom_call_target="tpu_custom_call" | custom-call | flops 1610612736 | bytes 4194304 | tf_op jit(solution)/shard_map/sample/pallas_call | solution.py:365
  139.2 11.4 %mixing.1.mix_ref = f32[512,512]{1,0:T(8,128)} custom-call(s32[1]{0:T(128)} %bitcast.16.count_ref, f32[512,256]{1,0:T(8,128)} %sample.1.raw_ref, f32[1,256]{1,0:T(1,128)} %get-tuple-element.191.value_ref, f32[1,256]{1,0:T(1,128)} %get-tuple-element.192.precision_ref, s32[1,256]{1,0:T(1,128)} %fusion.4.class_ref), custom_call_target="tpu_custom_call" | custom-call | flops 4026531840 | bytes 1048576 | tf_op jit(solution)/shard_map/mixing/pallas_call | solution.py:544
  153.8 10.1 %collective-permute-start.30 = (f32[2,4,128,128]{3,2,1,0:T(8,128)S(1)}, f32[2,4,128,128]{3,2,1,0:T(8,128)S(1)}, u32[]{:S(2)}, u32[]{:S(2)}) collective-permute-start(f32[2,4,128,128]{3,2,1,0:T(8,128)S(1)} %copy-done.55), channel_id=1, source_target_pairs={{0,2},{1,3},{2,4},{3,5},{4,6},{5,7},{6,0},{7,1},{8,10},{9,11},{10,... | collective-permute-start | bytes 1572872 | tf_op jit(solution)/shard_map/ppermute | solution.py:462
  163.9 7.8 %transform.2 = (f32[2,4,128,128]{3,2,1,0:T(8,128)}, f32[2,4,128,128]{3,2,1,0:T(8,128)}, f32[2,4,128,128]{3,2,1,0:T(8,128)}, f32[2,4,128,128]{3,2,1,0:T(8,128)}, ...) custom-call(f32[512,512]{1,0:T(8,128)} %mixing.1.mix_ref, ...), custom_call_target="tpu_custom_call" | custom-call | flops 3221225472 | bytes 8388608 | tf_op jit(solution)/shard_map/transform/pallas_call | solution.py:408
  177.5 12.6 %collective-permute-start.31 = (f32[2,4,128,128]{3,2,1,0:T(8,128)S(1)}, f32[2,4,128,128]{3,2,1,0:T(8,128)}, u32[]{:S(2)}, u32[]{:S(2)}) collective-permute-start(f32[2,4,128,128]{3,2,1,0:T(8,128)S(1)} %pad_maximum_fusion.5), channel_id=1, source_target_pairs={{0,1},{1,0},{2,3},{3,2},{4,5},{5,4},{6,7},{7,6},{8,9},{9,8},{10,11... | collective-permute-start | bytes 1572872 | tf_op jit(solution)/shard_map/ppermute | solution.py:462
  196.8 7.8 %transform.3 = (f32[2,4,128,128]{3,2,1,0:T(8,128)}, f32[2,4,128,128]{3,2,1,0:T(8,128)}, f32[2,4,128,128]{3,2,1,0:T(8,128)}, f32[2,4,128,128]{3,2,1,0:T(8,128)}, ...) custom-call(f32[512,512]{1,0:T(8,128)} %mixing.1.mix_ref, ...), custom_call_target="tpu_custom_call" | custom-call | flops 3221225472 | bytes 8388608 | tf_op jit(solution)/shard_map/transform/pallas_call | solution.py:408
  211.6 7.0 %collective-permute-done.45.refs_6_ = f32[2,4,128,128]{3,2,1,0:T(8,128)S(1)} collective-permute-done((f32[2,4,128,128]{3,2,1,0:T(8,128)}, f32[2,4,128,128]{3,2,1,0:T(8,128)S(1)}, u32[]{:S(2)}, u32[]{:S(2)}) %collective-permute-start.45) | collective-permute-done | bytes 524320 | tf_op jit(solution)/shard_map/ppermute | solution.py:462
  221.5 12.6 %collective-permute-done.48.refs_10_ = f32[2,4,128,128]{3,2,1,0:T(8,128)S(1)} collective-permute-done((f32[2,4,128,128]{3,2,1,0:T(8,128)}, f32[2,4,128,128]{3,2,1,0:T(8,128)S(1)}, u32[]{:S(2)}, u32[]{:S(2)}) %collective-permute-start.48) | collective-permute-done | bytes 524320 | tf_op jit(solution)/shard_map/ppermute | solution.py:462
  235.6 7.8 %collective-permute-done.51.refs_14_ = f32[2,4,128,128]{3,2,1,0:T(8,128)S(1)} collective-permute-done((f32[2,4,128,128]{3,2,1,0:T(8,128)S(1)}, f32[2,4,128,128]{3,2,1,0:T(8,128)S(1)}, u32[]{:S(2)}, u32[]{:S(2)}) %collective-permute-start.51) | collective-permute-done | bytes 524320 | tf_op jit(solution)/shard_map/ppermute | solution.py:462
  250.8 6.2 %collective-permute-done.35.refs_2_ = f32[2,4,128,128]{3,2,1,0:T(8,128)S(1)} collective-permute-done((f32[2,4,128,128]{3,2,1,0:T(8,128)}, f32[2,4,128,128]{3,2,1,0:T(8,128)S(1)}, u32[]{:S(2)}, u32[]{:S(2)}) %collective-permute-start.35) | collective-permute-done | bytes 524320 | tf_op jit(solution)/shard_map/ppermute | solution.py:462
  264.2 8.1 %collective-permute-done.38.refs_6_ = f32[2,4,128,128]{3,2,1,0:T(8,128)S(1)} collective-permute-done((f32[2,4,128,128]{3,2,1,0:T(8,128)}, f32[2,4,128,128]{3,2,1,0:T(8,128)S(1)}, u32[]{:S(2)}, u32[]{:S(2)}) %collective-permute-start.38) | collective-permute-done | bytes 524320 | tf_op jit(solution)/shard_map/ppermute | solution.py:462
  275.3 11.0 %collective-permute-done.53.refs_10_ = f32[2,4,128,128]{3,2,1,0:T(8,128)S(1)} collective-permute-done((f32[2,4,128,128]{3,2,1,0:T(8,128)}, f32[2,4,128,128]{3,2,1,0:T(8,128)S(1)}, u32[]{:S(2)}, u32[]{:S(2)}) %collective-permute-start.53) | collective-permute-done | bytes 524320 | tf_op jit(solution)/shard_map/ppermute | solution.py:462
  288.8 8.2 %collective-permute-done.56.refs_14_ = f32[2,4,128,128]{3,2,1,0:T(8,128)S(1)} collective-permute-done((f32[2,4,128,128]{3,2,1,0:T(8,128)S(1)}, f32[2,4,128,128]{3,2,1,0:T(8,128)S(1)}, u32[]{:S(2)}, u32[]{:S(2)}) %collective-permute-start.56) | collective-permute-done | bytes 524320 | tf_op jit(solution)/shard_map/ppermute | solution.py:462
  299.4 4.8 %unpack.2.refs_16_ = f32[8,2048,128]{2,1,0:T(8,128)} custom-call(s32[16]{0:T(128)} %stack.67.dest_ref, f32[2,4,128,128]{3,2,1,0:T(8,128)} %get-tuple-element.172.refs_0_, f32[1,4,128,128]{3,2,1,0:T(8,128)} %copy-done.40, f32[2,4,128,128]{3,2,1,0:T(8,128)} %copy-done.16, f32[2,4,128,128]{3,2,1,0:T(8,128)} %copy-done.3, f32[2,4,128,128]{3,2,1,0:T(8,128)} %copy-done.18, ...), custom_call_target="tpu_custom_call" | custom-call | bytes 8388608 | tf_op jit(solution)/shard_map/unpack/pallas_call | solution.py:443
  306.0 4.8 %unpack.3 = f32[8,2048,128]{2,1,0:T(8,128)} custom-call(s32[16]{0:T(128)} %stack.67.dest_ref, f32[2,4,128,128]{3,2,1,0:T(8,128)} %get-tuple-element.167.refs_0_, f32[1,4,128,128]{3,2,1,0:T(8,128)} %collective-permute-done.34.refs_1_, f32[2,4,128,128]{3,2,1,0:T(8,128)} %copy-done.30, f32[2,4,128,128]{3,2,1,0:T(8,128)} %copy-done.9, ...), custom_call_target="tpu_custom_call", output_to_operand_aliasing={{}: (17, {})} | custom-call | bytes 8388608 | tf_op jit(solution)/shard_map/unpack/pallas_call | solution.py:443
  (281 shorter events, 108.9 us)
Async XLA Ops:
  35.7 27.1 %collective-permute-start.6 = (f32[2,4,128,128]{3,2,1,0:T(8,128)}, f32[2,4,128,128]{3,2,1,0:T(8,128)S(1)}, u32[]{:S(2)}, u32[]{:S(2)}) collective-permute-start(f32[2,4,128,128]{3,2,1,0:T(8,128)} %get-tuple-element.102), channel_id=1, source_target_pairs={{0,8},{1,9},{2,10},{3,11},{4,12},{5,13},{6,14},{7,15},{8,0},{9,1},... | collective-permute-start | bytes 1572872 | tf_op jit(solution)/shard_map/ppermute | solution.py:462
  46.6 31.8 %collective-permute-start.7 = (f32[2,4,128,128]{3,2,1,0:T(8,128)}, f32[2,4,128,128]{3,2,1,0:T(8,128)S(1)}, u32[]{:S(2)}, u32[]{:S(2)}) collective-permute-start(f32[2,4,128,128]{3,2,1,0:T(8,128)} %get-tuple-element.103), channel_id=1, source_target_pairs={{0,4},{1,5},{2,6},{3,7},{4,0},{5,1},{6,2},{7,3},{8,12},{9,13},{10,... | collective-permute-start | bytes 1572872 | tf_op jit(solution)/shard_map/ppermute | solution.py:462
  55.4 32.6 %collective-permute-start.9 = (f32[2,4,128,128]{3,2,1,0:T(8,128)}, f32[2,4,128,128]{3,2,1,0:T(8,128)S(1)}, u32[]{:S(2)}, u32[]{:S(2)}) collective-permute-start(f32[2,4,128,128]{3,2,1,0:T(8,128)} %get-tuple-element.104), channel_id=1, source_target_pairs={{0,10},{1,11},{2,12},{3,13},{4,14},{5,15},{6,8},{7,9},{8,2},{9,3},... | collective-permute-start | bytes 1572872 | tf_op jit(solution)/shard_map/ppermute | solution.py:462
  61.3 31.4 %collective-permute-start.10 = (f32[2,4,128,128]{3,2,1,0:T(8,128)S(1)}, f32[2,4,128,128]{3,2,1,0:T(8,128)S(1)}, u32[]{:S(2)}, u32[]{:S(2)}) collective-permute-start(f32[2,4,128,128]{3,2,1,0:T(8,128)S(1)} %copy-done.60), channel_id=1, source_target_pairs={{0,6},{1,7},{2,0},{3,1},{4,2},{5,3},{6,4},{7,5},{8,14},{9,15},{10,... | collective-permute-start | bytes 1572872 | tf_op jit(solution)/shard_map/ppermute | solution.py:462
  62.8 50.5 %collective-permute-start.12 = (f32[2,4,128,128]{3,2,1,0:T(8,128)S(1)}, f32[2,4,128,128]{3,2,1,0:T(8,128)S(1)}, u32[]{:S(2)}, u32[]{:S(2)}) collective-permute-start(f32[2,4,128,128]{3,2,1,0:T(8,128)S(1)} %copy-done.59), channel_id=1, source_target_pairs={{0,14},{1,15},{2,8},{3,9},{4,10},{5,11},{6,12},{7,13},{8,6},{9,7},... | collective-permute-start | bytes 1572872 | tf_op jit(solution)/shard_map/ppermute | solution.py:462
  64.3 49.2 %collective-permute-start.13 = (f32[2,4,128,128]{3,2,1,0:T(8,128)}, f32[2,4,128,128]{3,2,1,0:T(8,128)S(1)}, u32[]{:S(2)}, u32[]{:S(2)}) collective-permute-start(f32[2,4,128,128]{3,2,1,0:T(8,128)} %get-tuple-element.113), channel_id=1, source_target_pairs={{0,2},{1,3},{2,4},{3,5},{4,6},{5,7},{6,0},{7,1},{8,10},{9,11},{10,... | collective-permute-start | bytes 1572872 | tf_op jit(solution)/shard_map/ppermute | solution.py:462
  78.4 36.1 %collective-permute-start.20 = (f32[2,4,128,128]{3,2,1,0:T(8,128)S(1)}, f32[2,4,128,128]{3,2,1,0:T(8,128)S(1)}, u32[]{:S(2)}, u32[]{:S(2)}) collective-permute-start(f32[2,4,128,128]{3,2,1,0:T(8,128)S(1)} %copy-done.58), channel_id=1, source_target_pairs={{0,12},{1,13},{2,14},{3,15},{4,8},{5,9},{6,10},{7,11},{8,4},{9,5},... | collective-permute-start | bytes 1572872 | tf_op jit(solution)/shard_map/ppermute | solution.py:462
  88.1 28.7 %collective-permute-start.23 = (f32[2,4,128,128]{3,2,1,0:T(8,128)}, f32[2,4,128,128]{3,2,1,0:T(8,128)}, u32[]{:S(2)}, u32[]{:S(2)}) collective-permute-start(f32[2,4,128,128]{3,2,1,0:T(8,128)} %get-tuple-element.140), channel_id=1, source_target_pairs={{0,8},{1,9},{2,10},{3,11},{4,12},{5,13},{6,14},{7,15},{8,0},{9,1},... | collective-permute-start | bytes 1572872 | tf_op jit(solution)/shard_map/ppermute | solution.py:462
  92.7 36.9 %collective-permute-start.8 = (f32[2,4,128,128]{3,2,1,0:T(8,128)}, f32[2,4,128,128]{3,2,1,0:T(8,128)S(1)}, u32[]{:S(2)}, u32[]{:S(2)}) collective-permute-start(f32[2,4,128,128]{3,2,1,0:T(8,128)} %pad_maximum_fusion), channel_id=1, source_target_pairs={{0,1},{1,0},{2,3},{3,2},{4,5},{5,4},{6,7},{7,6},{8,9},{9,8},{10,11... | collective-permute-start | bytes 1572872 | tf_op jit(solution)/shard_map/ppermute | solution.py:462
  128.5 44.6 %collective-permute-start.26 = (f32[2,4,128,128]{3,2,1,0:T(8,128)}, f32[2,4,128,128]{3,2,1,0:T(8,128)S(1)}, u32[]{:S(2)}, u32[]{:S(2)}) collective-permute-start(f32[2,4,128,128]{3,2,1,0:T(8,128)} %get-tuple-element.142), channel_id=1, source_target_pairs={{0,10},{1,11},{2,12},{3,13},{4,14},{5,15},{6,8},{7,9},{8,2},{9,3},... | collective-permute-start | bytes 1572872 | tf_op jit(solution)/shard_map/ppermute | solution.py:462
  129.7 46.8 %collective-permute-start.27 = (f32[2,4,128,128]{3,2,1,0:T(8,128)}, f32[2,4,128,128]{3,2,1,0:T(8,128)S(1)}, u32[]{:S(2)}, u32[]{:S(2)}) collective-permute-start(f32[2,4,128,128]{3,2,1,0:T(8,128)} %get-tuple-element.143), channel_id=1, source_target_pairs={{0,6},{1,7},{2,0},{3,1},{4,2},{5,3},{6,4},{7,5},{8,14},{9,15},{10,... | collective-permute-start | bytes 1572872 | tf_op jit(solution)/shard_map/ppermute | solution.py:462
  150.6 26.7 %collective-permute-start.29 = (f32[2,4,128,128]{3,2,1,0:T(8,128)}, f32[2,4,128,128]{3,2,1,0:T(8,128)S(1)}, u32[]{:S(2)}, u32[]{:S(2)}) collective-permute-start(f32[2,4,128,128]{3,2,1,0:T(8,128)} %get-tuple-element.144), channel_id=1, source_target_pairs={{0,14},{1,15},{2,8},{3,9},{4,10},{5,11},{6,12},{7,13},{8,6},{9,7},... | collective-permute-start | bytes 1572872 | tf_op jit(solution)/shard_map/ppermute | solution.py:462
  193.8 24.7 %collective-permute-start.45 = (f32[2,4,128,128]{3,2,1,0:T(8,128)}, f32[2,4,128,128]{3,2,1,0:T(8,128)S(1)}, u32[]{:S(2)}, u32[]{:S(2)}) collective-permute-start(f32[2,4,128,128]{3,2,1,0:T(8,128)} %get-tuple-element.175), channel_id=1, source_target_pairs={{0,14},{1,15},{2,8},{3,9},{4,10},{5,11},{6,12},{7,13},{8,6},{9,7},... | collective-permute-start | bytes 1572872 | tf_op jit(solution)/shard_map/ppermute | solution.py:462
  204.6 29.5 %collective-permute-start.48 = (f32[2,4,128,128]{3,2,1,0:T(8,128)}, f32[2,4,128,128]{3,2,1,0:T(8,128)S(1)}, u32[]{:S(2)}, u32[]{:S(2)}) collective-permute-start(f32[2,4,128,128]{3,2,1,0:T(8,128)} %get-tuple-element.177), channel_id=1, source_target_pairs={{0,10},{1,11},{2,12},{3,13},{4,14},{5,15},{6,8},{7,9},{8,2},{9,3},... | collective-permute-start | bytes 1572872 | tf_op jit(solution)/shard_map/ppermute | solution.py:462
  207.2 27.5 %collective-permute-start.49 = (f32[2,4,128,128]{3,2,1,0:T(8,128)S(1)}, f32[2,4,128,128]{3,2,1,0:T(8,128)S(1)}, u32[]{:S(2)}, u32[]{:S(2)}) collective-permute-start(f32[2,4,128,128]{3,2,1,0:T(8,128)S(1)} %copy-done.57), channel_id=1, source_target_pairs={{0,6},{1,7},{2,0},{3,1},{4,2},{5,3},{6,4},{7,5},{8,14},{9,15},{10,... | collective-permute-start | bytes 1572872 | tf_op jit(solution)/shard_map/ppermute | solution.py:462
  208.5 34.9 %collective-permute-start.51 = (f32[2,4,128,128]{3,2,1,0:T(8,128)S(1)}, f32[2,4,128,128]{3,2,1,0:T(8,128)S(1)}, u32[]{:S(2)}, u32[]{:S(2)}) collective-permute-start(f32[2,4,128,128]{3,2,1,0:T(8,128)S(1)} %copy-done.54), channel_id=1, source_target_pairs={{0,12},{1,13},{2,14},{3,15},{4,8},{5,9},{6,10},{7,11},{8,4},{9,5},... | collective-permute-start | bytes 1572872 | tf_op jit(solution)/shard_map/ppermute | solution.py:462
  218.6 25.2 %collective-permute-start.41 = (f32[1,4,128,128]{3,2,1,0:T(8,128)S(1)}, f32[1,4,128,128]{3,2,1,0:T(8,128)S(1)}, u32[]{:S(2)}, u32[]{:S(2)}) collective-permute-start(f32[1,4,128,128]{3,2,1,0:T(8,128)S(1)} %slice.117), channel_id=1, source_target_pairs={{0,1},{1,0},{2,3},{3,2},{4,5},{5,4},{6,7},{7,6},{8,9},{9,8},{10,11... | collective-permute-start | bytes 786440 | tf_op jit(solution)/shard_map/ppermute | solution.py:462
  220.7 24.7 %collective-permute-start.44 = (f32[2,4,128,128]{3,2,1,0:T(8,128)S(1)}, f32[2,4,128,128]{3,2,1,0:T(8,128)S(1)}, u32[]{:S(2)}, u32[]{:S(2)}) collective-permute-start(f32[2,4,128,128]{3,2,1,0:T(8,128)S(1)} %pad_maximum_fusion.8), channel_id=1, source_target_pairs={{0,1},{1,0},{2,3},{3,2},{4,5},{5,4},{6,7},{7,6},{8,9},{9,8},{10,11... | collective-permute-start | bytes 1572872 | tf_op jit(solution)/shard_map/ppermute | solution.py:462
  246.8 25.6 %collective-permute-start.38 = (f32[2,4,128,128]{3,2,1,0:T(8,128)}, f32[2,4,128,128]{3,2,1,0:T(8,128)S(1)}, u32[]{:S(2)}, u32[]{:S(2)}) collective-permute-start(f32[2,4,128,128]{3,2,1,0:T(8,128)} %get-tuple-element.170), channel_id=1, source_target_pairs={{0,14},{1,15},{2,8},{3,9},{4,10},{5,11},{6,12},{7,13},{8,6},{9,7},... | collective-permute-start | bytes 1572872 | tf_op jit(solution)/shard_map/ppermute | solution.py:462
  249.6 36.8 %collective-permute-start.53 = (f32[2,4,128,128]{3,2,1,0:T(8,128)}, f32[2,4,128,128]{3,2,1,0:T(8,128)S(1)}, u32[]{:S(2)}, u32[]{:S(2)}) collective-permute-start(f32[2,4,128,128]{3,2,1,0:T(8,128)} %get-tuple-element.183), channel_id=1, source_target_pairs={{0,10},{1,11},{2,12},{3,13},{4,14},{5,15},{6,8},{7,9},{8,2},{9,3},... | collective-permute-start | bytes 1572872 | tf_op jit(solution)/shard_map/ppermute | solution.py:462
  257.0 29.4 %collective-permute-start.54 = (f32[2,4,128,128]{3,2,1,0:T(8,128)}, f32[2,4,128,128]{3,2,1,0:T(8,128)S(1)}, u32[]{:S(2)}, u32[]{:S(2)}) collective-permute-start(f32[2,4,128,128]{3,2,1,0:T(8,128)} %get-tuple-element.184), channel_id=1, source_target_pairs={{0,6},{1,7},{2,0},{3,1},{4,2},{5,3},{6,4},{7,5},{8,14},{9,15},{10,... | collective-permute-start | bytes 1572872 | tf_op jit(solution)/shard_map/ppermute | solution.py:462
  260.7 36.3 %collective-permute-start.56 = (f32[2,4,128,128]{3,2,1,0:T(8,128)S(1)}, f32[2,4,128,128]{3,2,1,0:T(8,128)S(1)}, u32[]{:S(2)}, u32[]{:S(2)}) collective-permute-start(f32[2,4,128,128]{3,2,1,0:T(8,128)S(1)} %copy-done.56), channel_id=1, source_target_pairs={{0,12},{1,13},{2,14},{3,15},{4,8},{5,9},{6,10},{7,11},{8,4},{9,5},... | collective-permute-start | bytes 1572872 | tf_op jit(solution)/shard_map/ppermute | solution.py:462
  272.4 31.9 %collective-permute-start.37 = (f32[2,4,128,128]{3,2,1,0:T(8,128)}, f32[2,4,128,128]{3,2,1,0:T(8,128)S(1)}, u32[]{:S(2)}, u32[]{:S(2)}) collective-permute-start(f32[2,4,128,128]{3,2,1,0:T(8,128)} %pad_maximum_fusion.6), channel_id=1, source_target_pairs={{0,1},{1,0},{2,3},{3,2},{4,5},{5,4},{6,7},{7,6},{8,9},{9,8},{10,11... | collective-permute-start | bytes 1572872 | tf_op jit(solution)/shard_map/ppermute | solution.py:462
  274.7 29.6 %collective-permute-start.40 = (f32[2,4,128,128]{3,2,1,0:T(8,128)}, f32[2,4,128,128]{3,2,1,0:T(8,128)S(1)}, u32[]{:S(2)}, u32[]{:S(2)}) collective-permute-start(f32[2,4,128,128]{3,2,1,0:T(8,128)} %pad_maximum_fusion.7), channel_id=1, source_target_pairs={{0,1},{1,0},{2,3},{3,2},{4,5},{5,4},{6,7},{7,6},{8,9},{9,8},{10,11... | collective-permute-start | bytes 1572872 | tf_op jit(solution)/shard_map/ppermute | solution.py:462
  (99 other events, 2006.7 us)
where the time goes:
time: 316 us; the launch traced here: 311 us
  starting transfers between devices  126 us (40%)
  waiting for transfers between devices  83.5 us (26%)
  Pallas kernels  76.5 us (24%)
  local copies, waits for them, and re-layouts  17 us (5%)
  other arithmetic  6.72 us (2%)
    ppermute x48, starting transfers between devices, hop(): lax.ppermute(value, 'mem', [(i, shifted(i, offset, sign)) for i in range(...  115 us
    ppermute x48, waiting for transfers between devices, hop(): lax.ppermute(value, 'mem', [(i, shifted(i, offset, sign)) for i in range(...  70.4 us
    pallas_call x2, Pallas kernels, forecast(): pl.pallas_call(functools.partial(forecast_kernel, first, fields, rows, me...  24.8 us
    pallas_call x2, Pallas kernels, transform(): pl.pallas_call(transform_kernel, grid=(fields,), in_specs=[pl.BlockSpec((...  15.6 us
    pallas_call x1, Pallas kernels, mixing_transposed(): pl.pallas_call(mixing_kernel, in_specs=[pl.BlockSpec(memory_space=pltpu.S...  11.4 us
    pallas_call x2, Pallas kernels, pack(): pl.pallas_call(functools.partial(pack_kernel, first, fields, rows, member...  9.68 us
    pallas_call x2, Pallas kernels, unpack(): pl.pallas_call(functools.partial(unpack_kernel, members, rows), grid=(fie...  9.65 us
    unnamed x130, local copies, waits for them, and re-layouts  8.04 us
  transfers between devices with their start and end apart: 58, of which 16 were waited for; matrix products, arithmetic and copies ran while one was open for 5% of the time, Pallas kernels for 18%

commit v1 on v0

--- a/solution.py
+++ b/solution.py
@@ -9,8 +9,8 @@
 
 NEWTON = 8
 LANES = 128
-VMEM_LIMIT = 58 * 1024 * 1024
-PACK_LIMIT = 58 * 1024 * 1024
+VMEM_LIMIT = 60 * 1024 * 1024
+PACK_LIMIT = 60 * 1024 * 1024
 
 
 def iota(shape, dim):
@@ -176,8 +176,8 @@
 
 
 def forecast_kernel(first, fields, rows, members, dest_ref, x_hbm, cx_ref, cy_ref, df_ref, own_ref, left_ref, right_ref, left_k_ref, right_k_ref, row_ref, row_k_ref, dl_ref, dr_ref, *refs):
-    out_refs = refs[: len(CHIPS)]
-    k_main, k_edge, k_row, edge_s, first_s, x_s, second_s, beside_s, held, sems = refs[len(CHIPS) :]
+    k_main, k_edge, k_row, edge_s, first_s, x_s, second_s, beside_s, held, sems = refs[-10:]
+    out_refs = refs[-10 - len(CHIPS) : -10]
     step = pl.program_id(0)
     pitch = rows + PITCH
 
@@ -270,16 +270,15 @@
             out_refs[i // 2][i % 2, 0, r * members : (r + 1) * members, :] = second_s[base + r]
 
 
-def forecast(x, coefficients, edge, moved, moved_k, dest, first, fields):
+def forecast(x, coefficients, edge, moved, dest, first, fields, after):
     _, members, rows, _ = x.shape
     row, left, right, corner_l, corner_r = moved
-    row_k, left_k, right_k = moved_k
-    last = row_k.shape[0] - 1
+    last = row.shape[0] - 1
     groups = rows // SPREAD
     small = pl.BlockSpec((rows, LANES), lambda i: (0, 0))
-    edge_spec = pl.BlockSpec((1, groups, members, LANES), lambda i: (i, 0, 0, 0))
+    edge_spec = pl.BlockSpec((1, groups, members, LANES), lambda i: (first + i, 0, 0, 0))
     edge_last = pl.BlockSpec((1, groups, members, LANES), lambda i: (last, 0, 0, 0))
-    corner_spec = pl.BlockSpec((1, members, LANES), lambda i: (i, 0, 0))
+    corner_spec = pl.BlockSpec((1, members, LANES), lambda i: (first + i, 0, 0))
     piece = HEIGHT * members
     return pl.pallas_call(
         functools.partial(forecast_kernel, first, fields, rows, members),
@@ -295,11 +294,12 @@
             edge_spec,
             edge_last,
             edge_last,
-            pl.BlockSpec((1, 4, members, LANES), lambda i: (i, 0, 0, 0)),
+            pl.BlockSpec((1, 4, members, LANES), lambda i: (first + i, 0, 0, 0)),
             pl.BlockSpec((1, 4, members, LANES), lambda i: (last, 0, 0, 0)),
             corner_spec,
             corner_spec,
-        ],
+        ]
+        + [pl.BlockSpec(memory_space=pl.ANY) for _ in after],
         out_specs=[pair_spec(piece)] * len(CHIPS),
         out_shape=[jax.ShapeDtypeStruct((2, fields, piece, LANES), jnp.float32)] * len(CHIPS),
         scratch_shapes=[
@@ -321,7 +321,7 @@
             transcendentals=0,
         ),
         name="forecast",
-    )(dest, x, *coefficients, edge, left, right, left_k, right_k, row, row_k, corner_l, corner_r)
+    )(dest, x, *coefficients, edge, left, right, left, right, row, row, corner_l, corner_r, *after)
 
 
 def halves(value):
@@ -589,21 +589,18 @@
     dest = jnp.stack([shifted(tile, o) for o in OFFSETS]).astype(jnp.int32)
     half = total // 2
 
-    def fields_sent(packed, moved, moved_k, first):
+    def fields_sent(first, after=()):
         return list(
-            forecast(prior_members, coefficients, packed[0], moved, moved_k, dest, first, half)
+            forecast(prior_members, coefficients, packed[0], moved, dest, first, half, after)
         )
 
-    packed = pack(prior_members, coefficients, 0, half)
-    moved_k = exchange(packed)
-    sent = fields_sent(packed, moved_k, moved_k[:3], 0)
+    packed = pack(prior_members, coefficients, 0, total)
+    moved = exchange(packed)
+    sent = fields_sent(0)
     arrived = travel(sent[:EARLY], 1)
     traded = [trade(arrived, GROUPS[0])]
-    later = pack(prior_members, coefficients, half, half, traded)
-    later, sent[EARLY:] = lax.optimization_barrier((later, sent[EARLY:]))
-    moved = exchange(later)
-    following = fields_sent(later, moved, moved_k[:3], half)
-    following, sent[LATE:] = lax.optimization_barrier((following, sent[LATE:]))
+    following = fields_sent(half, sent[:1])
+    following, sent[EARLY:] = lax.optimization_barrier((following, sent[EARLY:]))
     arrived += travel(sent[EARLY:], 1, EARLY)
     traded += [trade(arrived, group) for group in GROUPS[1:]]
     sent = following

time: 316 us -> 292 us (0.924)
  starting transfers between devices: 126 us -> 85.9 us
  waiting for transfers between devices: 83.5 us -> 105 us
    ppermute x48, starting transfers between devices: 115 us -> 78.4 us  [hop(): lax.ppermute(value, 'mem', [(i, shifted(i, offset, sign)) for i in range(...]
    ppermute x48, waiting for transfers between devices: 70.4 us -> 91.5 us  [hop(): lax.ppermute(value, 'mem', [(i, shifted(i, offset, sign)) for i in range(...]
    ppermute x2 -> x1, waiting for transfers between devices: 0.01 us -> 5.17 us  [exchange(): lax.ppermute(row, 'gx', [(i, (i + 1) % nx) for i in range(nx)])]
    ppermute x2 -> x1, waiting for transfers between devices: 4.24 us -> 0.01 us  [exchange(): lax.ppermute(edge, 'gy', right)]
    pallas_call x2 -> x1, Pallas kernels: 9.68 us -> 6.93 us  [pack(): pl.pallas_call(functools.partial(pack_kernel, first, fields, rows, member...]
    unnamed x130 -> x112, local copies, waits for them, and re-layouts: 8.04 us -> 6.83 us
  transfers between devices with their start and end apart: 58 -> 53, of which waited for: 16 -> 16; matrix products, arithmetic and copies ran while one was open for 5% -> 6% of each run, Pallas kernels for 18% -> 17%
where the time goes in v1:
time: 292 us; the launch traced here: 290 us
  waiting for transfers between devices  105 us (36%)
  starting transfers between devices  85.9 us (29%)
  Pallas kernels  74 us (25%)
  local copies, waits for them, and re-layouts  16.8 us (6%)
  other arithmetic  6.81 us (2%)
    ppermute x48, waiting for transfers between devices, hop(): lax.ppermute(value, 'mem', [(i, shifted(i, offset, sign)) for i in range(...  91.5 us
    ppermute x48, starting transfers between devices, hop(): lax.ppermute(value, 'mem', [(i, shifted(i, offset, sign)) for i in range(...  78.4 us
    pallas_call x2, Pallas kernels, forecast(): pl.pallas_call(functools.partial(forecast_kernel, first, fields, rows, me...  24.9 us
    pallas_call x2, Pallas kernels, transform(): pl.pallas_call(transform_kernel, grid=(fields,), in_specs=[pl.BlockSpec((...  15.8 us
    pallas_call x1, Pallas kernels, mixing_transposed(): pl.pallas_call(mixing_kernel, in_specs=[pl.BlockSpec(memory_space=pltpu.S...  11.4 us
    pallas_call x2, Pallas kernels, unpack(): pl.pallas_call(functools.partial(unpack_kernel, members, rows), grid=(fie...  9.65 us
    pallas_call x1, Pallas kernels, pack(): pl.pallas_call(functools.partial(pack_kernel, first, fields, rows, member...  6.93 us
    slice x32, local copies, waits for them, and re-layouts, trade(): arrived[o][1:2]  6.85 us
  transfers between devices with their start and end apart: 53, of which 16 were waited for; matrix products, arithmetic and copies ran while one was open for 6% of the time, Pallas kernels for 17%

profile of v1, /device:TPU:1, one launch (start us, length us, event | category | flops | bytes accessed | tf_op | source)
XLA Modules:
  0.0 290.0 jit_solution(6512908404028426653)
XLA Ops:
  0.0 6.9 %pack_edges.1 = (f32[9,2,32,128]{3,2,1,0:T(8,128)}, f32[9,4,32,128]{3,2,1,0:T(8,128)}, f32[9,32,128]{2,1,0:T(8,128)}) custom-call(f32[8,32,64,128]{3,2,1,0:T(8,128)} %x_hbm.3, f32[64,128]{1,0:T(8,128)} %cx_ref.5, f32[64,128]{1,0:T(8,128)} %cy_ref.5, f32[64,128]{1,0:T(8,128)} %df_ref.5), custom_call_target="tpu_custom_call" | custom-call | flops 4194304 | bytes 16777216 | tf_op jit(solution)/shard_map/pack_edges/pallas_call | solution.py:118
  15.1 5.7 %collective-permute-done.4.dr_ref = f32[9,32,128]{2,1,0:T(8,128)S(1)} collective-permute-done((f32[9,32,128]{2,1,0:T(8,128)}, f32[9,32,128]{2,1,0:T(8,128)S(1)}, u32[]{:S(2)}, u32[]{:S(2)}) %collective-permute-start.4) | collective-permute-done | bytes 147488 | tf_op jit(solution)/shard_map/ppermute | solution.py:163
  23.9 5.2 %collective-permute-done.2.row_ref.row_k_ref = f32[9,4,32,128]{3,2,1,0:T(8,128)S(1)} collective-permute-done((f32[9,4,32,128]{3,2,1,0:T(8,128)}, f32[9,4,32,128]{3,2,1,0:T(8,128)S(1)}, u32[]{:S(2)}, u32[]{:S(2)}) %collective-permute-start.2) | collective-permute-done | bytes 589856 | tf_op jit(solution)/shard_map/ppermute | solution.py:159
  29.9 12.5 %forecast.2 = (f32[2,4,128,128]{3,2,1,0:T(8,128)}, f32[2,4,128,128]{3,2,1,0:T(8,128)}, f32[2,4,128,128]{3,2,1,0:T(8,128)}, f32[2,4,128,128]{3,2,1,0:T(8,128)}, f...) custom-call(s32[16]{0:T(128)} %stack.67.dest_ref, ...), custom_call_target="tpu_custom_call" | custom-call | flops 18874368 | bytes 8388608 | tf_op jit(solution)/shard_map/forecast/pallas_call | solution.py:283
  51.0 12.5 %forecast.3 = (f32[2,4,128,128]{3,2,1,0:T(8,128)}, f32[2,4,128,128]{3,2,1,0:T(8,128)}, f32[2,4,128,128]{3,2,1,0:T(8,128)}, f32[2,4,128,128]{3,2,1,0:T(8,128)}, f...) custom-call(s32[16]{0:T(128)} %stack.67.dest_ref, ...), custom_call_target="tpu_custom_call" | custom-call | flops 18874368 | bytes 8388608 | tf_op jit(solution)/shard_map/forecast/pallas_call | solution.py:283
  67.8 4.9 %collective-permute-done.9.refs_6_ = f32[2,4,128,128]{3,2,1,0:T(8,128)S(1)} collective-permute-done((f32[2,4,128,128]{3,2,1,0:T(8,128)}, f32[2,4,128,128]{3,2,1,0:T(8,128)S(1)}, u32[]{:S(2)}, u32[]{:S(2)}) %collective-permute-start.9) | collective-permute-done | bytes 524320 | tf_op jit(solution)/shard_map/ppermute | solution.py:462
  78.1 6.6 %collective-permute-done.12.refs_10_ = f32[2,4,128,128]{3,2,1,0:T(8,128)S(1)} collective-permute-done((f32[2,4,128,128]{3,2,1,0:T(8,128)}, f32[2,4,128,128]{3,2,1,0:T(8,128)S(1)}, u32[]{:S(2)}, u32[]{:S(2)}) %collective-permute-start.12) | collective-permute-done | bytes 524320 | tf_op jit(solution)/shard_map/ppermute | solution.py:462
  93.9 4.6 %collective-permute-start.14 = (f32[2,4,128,128]{3,2,1,0:T(8,128)}, f32[2,4,128,128]{3,2,1,0:T(8,128)S(1)}, u32[]{:S(2)}, u32[]{:S(2)}) collective-permute-start(f32[2,4,128,128]{3,2,1,0:T(8,128)} %pad_maximum_fusion.2), channel_id=1, source_target_pairs={{0,1},{1,0},{2,3},{3,2},{4,5},{5,4},{6,7},{7,6},{8,9},{9,8},{10,11... | collective-permute-start | bytes 1572872 | tf_op jit(solution)/shard_map/ppermute | solution.py:462
  99.4 6.9 %collective-permute-done.18.refs_2_ = f32[2,4,128,128]{3,2,1,0:T(8,128)} collective-permute-done((f32[2,4,128,128]{3,2,1,0:T(8,128)}, f32[2,4,128,128]{3,2,1,0:T(8,128)}, u32[]{:S(2)}, u32[]{:S(2)}) %collective-permute-start.18) | collective-permute-done | bytes 524320 | tf_op jit(solution)/shard_map/ppermute | solution.py:462
  112.9 9.3 %collective-permute-start.21 = (f32[2,4,128,128]{3,2,1,0:T(8,128)}, f32[2,4,128,128]{3,2,1,0:T(8,128)}, u32[]{:S(2)}, u32[]{:S(2)}) collective-permute-start(f32[2,4,128,128]{3,2,1,0:T(8,128)} %get-tuple-element.128), channel_id=1, source_target_pairs={{0,10},{1,11},{2,12},{3,13},{4,14},{5,15},{6,8},{7,9},{8,2},{9,3},... | collective-permute-start | bytes 1572872 | tf_op jit(solution)/shard_map/ppermute | solution.py:462
  124.1 5.3 %sample.1.raw_ref = f32[512,256]{1,0:T(8,128)} custom-call(s32[1,256]{1,0:T(1,128)} %fusion.5.place_ref, f32[2,4,128,128]{3,2,1,0:T(8,128)} %get-tuple-element.94.refs_0_, f32[1,4,128,128]{3,2,1,0:T(8,128)} %copy-done.42, f32[2,4,128,128]{3,2,1,0:T(8,128)} %copy-done.22, f32[2,4,128,128]{3,2,1,0:T(8,128)} %copy-done.9, f32[2,4,128,128]{3,2,1,0:T(8,128)} %copy-done.24, ...), custom_call_target="tpu_custom_call" | custom-call | flops 1610612736 | bytes 4194304 | tf_op jit(solution)/shard_map/sample/pallas_call | solution.py:365
  129.4 11.4 %mixing.1.mix_ref = f32[512,512]{1,0:T(8,128)} custom-call(s32[1]{0:T(128)} %bitcast.16.count_ref, f32[512,256]{1,0:T(8,128)} %sample.1.raw_ref, f32[1,256]{1,0:T(1,128)} %get-tuple-element.177.value_ref, f32[1,256]{1,0:T(1,128)} %get-tuple-element.178.precision_ref, s32[1,256]{1,0:T(1,128)} %fusion.4.class_ref), custom_call_target="tpu_custom_call" | custom-call | flops 4026531840 | bytes 1048576 | tf_op jit(solution)/shard_map/mixing/pallas_call | solution.py:544
  142.3 7.9 %transform.2 = (f32[2,4,128,128]{3,2,1,0:T(8,128)}, f32[2,4,128,128]{3,2,1,0:T(8,128)}, f32[2,4,128,128]{3,2,1,0:T(8,128)}, f32[2,4,128,128]{3,2,1,0:T(8,128)}, ...) custom-call(f32[512,512]{1,0:T(8,128)} %mixing.1.mix_ref, ...), custom_call_target="tpu_custom_call" | custom-call | flops 3221225472 | bytes 8388608 | tf_op jit(solution)/shard_map/transform/pallas_call | solution.py:408
  159.1 10.1 %collective-permute-done.27.refs_14_ = f32[2,4,128,128]{3,2,1,0:T(8,128)S(1)} collective-permute-done((f32[2,4,128,128]{3,2,1,0:T(8,128)S(1)}, f32[2,4,128,128]{3,2,1,0:T(8,128)S(1)}, u32[]{:S(2)}, u32[]{:S(2)}) %collective-permute-start.27) | collective-permute-done | bytes 524320 | tf_op jit(solution)/shard_map/ppermute | solution.py:462
  178.5 7.9 %transform.3 = (f32[2,4,128,128]{3,2,1,0:T(8,128)}, f32[2,4,128,128]{3,2,1,0:T(8,128)}, f32[2,4,128,128]{3,2,1,0:T(8,128)}, f32[2,4,128,128]{3,2,1,0:T(8,128)}, ...) custom-call(f32[512,512]{1,0:T(8,128)} %mixing.1.mix_ref, ...), custom_call_target="tpu_custom_call" | custom-call | flops 3221225472 | bytes 8388608 | tf_op jit(solution)/shard_map/transform/pallas_call | solution.py:408
  192.3 6.2 %collective-permute-done.40.refs_6_ = f32[2,4,128,128]{3,2,1,0:T(8,128)S(1)} collective-permute-done((f32[2,4,128,128]{3,2,1,0:T(8,128)}, f32[2,4,128,128]{3,2,1,0:T(8,128)S(1)}, u32[]{:S(2)}, u32[]{:S(2)}) %collective-permute-start.40) | collective-permute-done | bytes 524320 | tf_op jit(solution)/shard_map/ppermute | solution.py:462
  200.8 11.2 %collective-permute-done.43.refs_10_ = f32[2,4,128,128]{3,2,1,0:T(8,128)S(1)} collective-permute-done((f32[2,4,128,128]{3,2,1,0:T(8,128)}, f32[2,4,128,128]{3,2,1,0:T(8,128)S(1)}, u32[]{:S(2)}, u32[]{:S(2)}) %collective-permute-start.43) | collective-permute-done | bytes 524320 | tf_op jit(solution)/shard_map/ppermute | solution.py:462
  212.9 9.5 %collective-permute-done.46.refs_14_ = f32[2,4,128,128]{3,2,1,0:T(8,128)S(1)} collective-permute-done((f32[2,4,128,128]{3,2,1,0:T(8,128)}, f32[2,4,128,128]{3,2,1,0:T(8,128)S(1)}, u32[]{:S(2)}, u32[]{:S(2)}) %collective-permute-start.46) | collective-permute-done | bytes 524320 | tf_op jit(solution)/shard_map/ppermute | solution.py:462
  240.8 5.0 %collective-permute-start.51 = (f32[2,4,128,128]{3,2,1,0:T(8,128)S(1)}, f32[2,4,128,128]{3,2,1,0:T(8,128)S(1)}, u32[]{:S(2)}, u32[]{:S(2)}) collective-permute-start(f32[2,4,128,128]{3,2,1,0:T(8,128)S(1)} %copy-done.48), channel_id=1, source_target_pairs={{0,12},{1,13},{2,14},{3,15},{4,8},{5,9},{6,10},{7,11},{8,4},{9,5},... | collective-permute-start | bytes 1572872 | tf_op jit(solution)/shard_map/ppermute | solution.py:462
  246.6 5.5 %collective-permute-done.33.refs_6_ = f32[2,4,128,128]{3,2,1,0:T(8,128)S(1)} collective-permute-done((f32[2,4,128,128]{3,2,1,0:T(8,128)}, f32[2,4,128,128]{3,2,1,0:T(8,128)S(1)}, u32[]{:S(2)}, u32[]{:S(2)}) %collective-permute-start.33) | collective-permute-done | bytes 524320 | tf_op jit(solution)/shard_map/ppermute | solution.py:462
  254.5 10.9 %collective-permute-done.48.refs_10_ = f32[2,4,128,128]{3,2,1,0:T(8,128)S(1)} collective-permute-done((f32[2,4,128,128]{3,2,1,0:T(8,128)}, f32[2,4,128,128]{3,2,1,0:T(8,128)S(1)}, u32[]{:S(2)}, u32[]{:S(2)}) %collective-permute-start.48) | collective-permute-done | bytes 524320 | tf_op jit(solution)/shard_map/ppermute | solution.py:462
  267.8 8.7 %collective-permute-done.51.refs_14_ = f32[2,4,128,128]{3,2,1,0:T(8,128)S(1)} collective-permute-done((f32[2,4,128,128]{3,2,1,0:T(8,128)S(1)}, f32[2,4,128,128]{3,2,1,0:T(8,128)S(1)}, u32[]{:S(2)}, u32[]{:S(2)}) %collective-permute-start.51) | collective-permute-done | bytes 524320 | tf_op jit(solution)/shard_map/ppermute | solution.py:462
  278.4 4.8 %unpack.2.refs_16_ = f32[8,2048,128]{2,1,0:T(8,128)} custom-call(s32[16]{0:T(128)} %stack.67.dest_ref, f32[2,4,128,128]{3,2,1,0:T(8,128)} %get-tuple-element.158.refs_0_, f32[1,4,128,128]{3,2,1,0:T(8,128)} %copy-done.41, f32[2,4,128,128]{3,2,1,0:T(8,128)} %copy-done.17, f32[2,4,128,128]{3,2,1,0:T(8,128)} %copy-done.6, f32[2,4,128,128]{3,2,1,0:T(8,128)} %copy-done.19, ...), custom_call_target="tpu_custom_call" | custom-call | bytes 8388608 | tf_op jit(solution)/shard_map/unpack/pallas_call | solution.py:443
  285.0 4.8 %unpack.3 = f32[8,2048,128]{2,1,0:T(8,128)} custom-call(s32[16]{0:T(128)} %stack.67.dest_ref, f32[2,4,128,128]{3,2,1,0:T(8,128)} %get-tuple-element.153.refs_0_, f32[1,4,128,128]{3,2,1,0:T(8,128)} %collective-permute-done.29.refs_1_, f32[2,4,128,128]{3,2,1,0:T(8,128)} %copy-done.31, f32[2,4,128,128]{3,2,1,0:T(8,128)} %copy-done.12, ...), custom_call_target="tpu_custom_call", output_to_operand_aliasing={{}: (17, {})} | custom-call | bytes 8388608 | tf_op jit(solution)/shard_map/unpack/pallas_call | solution.py:443
  (252 shorter events, 104.7 us)
Async XLA Ops:
  42.4 23.7 %collective-permute-start.6 = (f32[2,4,128,128]{3,2,1,0:T(8,128)}, f32[2,4,128,128]{3,2,1,0:T(8,128)S(1)}, u32[]{:S(2)}, u32[]{:S(2)}) collective-permute-start(f32[2,4,128,128]{3,2,1,0:T(8,128)} %get-tuple-element.95), channel_id=1, source_target_pairs={{0,8},{1,9},{2,10},{3,11},{4,12},{5,13},{6,14},{7,15},{8,0},{9,1},... | collective-permute-start | bytes 1572872 | tf_op jit(solution)/shard_map/ppermute | solution.py:462
  48.5 24.2 %collective-permute-start.9 = (f32[2,4,128,128]{3,2,1,0:T(8,128)}, f32[2,4,128,128]{3,2,1,0:T(8,128)S(1)}, u32[]{:S(2)}, u32[]{:S(2)}) collective-permute-start(f32[2,4,128,128]{3,2,1,0:T(8,128)} %get-tuple-element.97), channel_id=1, source_target_pairs={{0,10},{1,11},{2,12},{3,13},{4,14},{5,15},{6,8},{7,9},{8,2},{9,3},... | collective-permute-start | bytes 1572872 | tf_op jit(solution)/shard_map/ppermute | solution.py:462
  48.7 27.0 %collective-permute-start.10 = (f32[2,4,128,128]{3,2,1,0:T(8,128)}, f32[2,4,128,128]{3,2,1,0:T(8,128)S(1)}, u32[]{:S(2)}, u32[]{:S(2)}) collective-permute-start(f32[2,4,128,128]{3,2,1,0:T(8,128)} %get-tuple-element.98), channel_id=1, source_target_pairs={{0,6},{1,7},{2,0},{3,1},{4,2},{5,3},{6,4},{7,5},{8,14},{9,15},{10,... | collective-permute-start | bytes 1572872 | tf_op jit(solution)/shard_map/ppermute | solution.py:462
  67.7 25.4 %collective-permute-start.15 = (f32[2,4,128,128]{3,2,1,0:T(8,128)S(1)}, f32[2,4,128,128]{3,2,1,0:T(8,128)S(1)}, u32[]{:S(2)}, u32[]{:S(2)}) collective-permute-start(f32[2,4,128,128]{3,2,1,0:T(8,128)S(1)} %copy-done.49), channel_id=1, source_target_pairs={{0,12},{1,13},{2,14},{3,15},{4,8},{5,9},{6,10},{7,11},{8,4},{9,5},... | collective-permute-start | bytes 1572872 | tf_op jit(solution)/shard_map/ppermute | solution.py:462
  72.7 33.7 %collective-permute-start.18 = (f32[2,4,128,128]{3,2,1,0:T(8,128)}, f32[2,4,128,128]{3,2,1,0:T(8,128)}, u32[]{:S(2)}, u32[]{:S(2)}) collective-permute-start(f32[2,4,128,128]{3,2,1,0:T(8,128)} %get-tuple-element.126), channel_id=1, source_target_pairs={{0,8},{1,9},{2,10},{3,11},{4,12},{5,13},{6,14},{7,15},{8,0},{9,1},... | collective-permute-start | bytes 1572872 | tf_op jit(solution)/shard_map/ppermute | solution.py:462
  75.7 31.1 %collective-permute-start.19 = (f32[2,4,128,128]{3,2,1,0:T(8,128)}, f32[2,4,128,128]{3,2,1,0:T(8,128)}, u32[]{:S(2)}, u32[]{:S(2)}) collective-permute-start(f32[2,4,128,128]{3,2,1,0:T(8,128)} %get-tuple-element.127), channel_id=1, source_target_pairs={{0,4},{1,5},{2,6},{3,7},{4,0},{5,1},{6,2},{7,3},{8,12},{9,13},{10,... | collective-permute-start | bytes 1572872 | tf_op jit(solution)/shard_map/ppermute | solution.py:462
  84.7 37.4 %collective-permute-start.8 = (f32[2,4,128,128]{3,2,1,0:T(8,128)}, f32[2,4,128,128]{3,2,1,0:T(8,128)S(1)}, u32[]{:S(2)}, u32[]{:S(2)}) collective-permute-start(f32[2,4,128,128]{3,2,1,0:T(8,128)} %pad_maximum_fusion), channel_id=1, source_target_pairs={{0,1},{1,0},{2,3},{3,2},{4,5},{5,4},{6,7},{7,6},{8,9},{9,8},{10,11... | collective-permute-start | bytes 1572872 | tf_op jit(solution)/shard_map/ppermute | solution.py:462
  87.8 34.4 %collective-permute-start.11 = (f32[2,4,128,128]{3,2,1,0:T(8,128)}, f32[2,4,128,128]{3,2,1,0:T(8,128)S(1)}, u32[]{:S(2)}, u32[]{:S(2)}) collective-permute-start(f32[2,4,128,128]{3,2,1,0:T(8,128)} %pad_maximum_fusion.1), channel_id=1, source_target_pairs={{0,1},{1,0},{2,3},{3,2},{4,5},{5,4},{6,7},{7,6},{8,9},{9,8},{10,11... | collective-permute-start | bytes 1572872 | tf_op jit(solution)/shard_map/ppermute | solution.py:462
  93.9 28.3 %collective-permute-start.14 = (f32[2,4,128,128]{3,2,1,0:T(8,128)}, f32[2,4,128,128]{3,2,1,0:T(8,128)S(1)}, u32[]{:S(2)}, u32[]{:S(2)}) collective-permute-start(f32[2,4,128,128]{3,2,1,0:T(8,128)} %pad_maximum_fusion.2), channel_id=1, source_target_pairs={{0,1},{1,0},{2,3},{3,2},{4,5},{5,4},{6,7},{7,6},{8,9},{9,8},{10,11... | collective-permute-start | bytes 1572872 | tf_op jit(solution)/shard_map/ppermute | solution.py:462
  112.9 41.5 %collective-permute-start.21 = (f32[2,4,128,128]{3,2,1,0:T(8,128)}, f32[2,4,128,128]{3,2,1,0:T(8,128)}, u32[]{:S(2)}, u32[]{:S(2)}) collective-permute-start(f32[2,4,128,128]{3,2,1,0:T(8,128)} %get-tuple-element.128), channel_id=1, source_target_pairs={{0,10},{1,11},{2,12},{3,13},{4,14},{5,15},{6,8},{7,9},{8,2},{9,3},... | collective-permute-start | bytes 1572872 | tf_op jit(solution)/shard_map/ppermute | solution.py:462
  122.1 34.5 %collective-permute-start.22 = (f32[2,4,128,128]{3,2,1,0:T(8,128)}, f32[2,4,128,128]{3,2,1,0:T(8,128)}, u32[]{:S(2)}, u32[]{:S(2)}) collective-permute-start(f32[2,4,128,128]{3,2,1,0:T(8,128)} %get-tuple-element.129), channel_id=1, source_target_pairs={{0,6},{1,7},{2,0},{3,1},{4,2},{5,3},{6,4},{7,5},{8,14},{9,15},{10,... | collective-permute-start | bytes 1572872 | tf_op jit(solution)/shard_map/ppermute | solution.py:462
  174.7 23.8 %collective-permute-start.40 = (f32[2,4,128,128]{3,2,1,0:T(8,128)}, f32[2,4,128,128]{3,2,1,0:T(8,128)S(1)}, u32[]{:S(2)}, u32[]{:S(2)}) collective-permute-start(f32[2,4,128,128]{3,2,1,0:T(8,128)} %get-tuple-element.161), channel_id=1, source_target_pairs={{0,14},{1,15},{2,8},{3,9},{4,10},{5,11},{6,12},{7,13},{8,6},{9,7},... | collective-permute-start | bytes 1572872 | tf_op jit(solution)/shard_map/ppermute | solution.py:462
  177.8 22.8 %collective-permute-start.41 = (f32[2,4,128,128]{3,2,1,0:T(8,128)}, f32[2,4,128,128]{3,2,1,0:T(8,128)S(1)}, u32[]{:S(2)}, u32[]{:S(2)}) collective-permute-start(f32[2,4,128,128]{3,2,1,0:T(8,128)} %get-tuple-element.162), channel_id=1, source_target_pairs={{0,2},{1,3},{2,4},{3,5},{4,6},{5,7},{6,0},{7,1},{8,10},{9,11},{10,... | collective-permute-start | bytes 1572872 | tf_op jit(solution)/shard_map/ppermute | solution.py:462
  186.4 25.6 %collective-permute-start.43 = (f32[2,4,128,128]{3,2,1,0:T(8,128)}, f32[2,4,128,128]{3,2,1,0:T(8,128)S(1)}, u32[]{:S(2)}, u32[]{:S(2)}) collective-permute-start(f32[2,4,128,128]{3,2,1,0:T(8,128)} %get-tuple-element.163), channel_id=1, source_target_pairs={{0,10},{1,11},{2,12},{3,13},{4,14},{5,15},{6,8},{7,9},{8,2},{9,3},... | collective-permute-start | bytes 1572872 | tf_op jit(solution)/shard_map/ppermute | solution.py:462
  187.3 25.4 %collective-permute-start.44 = (f32[2,4,128,128]{3,2,1,0:T(8,128)}, f32[2,4,128,128]{3,2,1,0:T(8,128)S(1)}, u32[]{:S(2)}, u32[]{:S(2)}) collective-permute-start(f32[2,4,128,128]{3,2,1,0:T(8,128)} %get-tuple-element.164), channel_id=1, source_target_pairs={{0,6},{1,7},{2,0},{3,1},{4,2},{5,3},{6,4},{7,5},{8,14},{9,15},{10,... | collective-permute-start | bytes 1572872 | tf_op jit(solution)/shard_map/ppermute | solution.py:462
  189.4 33.0 %collective-permute-start.46 = (f32[2,4,128,128]{3,2,1,0:T(8,128)}, f32[2,4,128,128]{3,2,1,0:T(8,128)S(1)}, u32[]{:S(2)}, u32[]{:S(2)}) collective-permute-start(f32[2,4,128,128]{3,2,1,0:T(8,128)} %get-tuple-element.165), channel_id=1, source_target_pairs={{0,12},{1,13},{2,14},{3,15},{4,8},{5,9},{6,10},{7,11},{8,4},{9,5},... | collective-permute-start | bytes 1572872 | tf_op jit(solution)/shard_map/ppermute | solution.py:462
  198.6 24.4 %collective-permute-start.36 = (f32[1,4,128,128]{3,2,1,0:T(8,128)S(1)}, f32[1,4,128,128]{3,2,1,0:T(8,128)S(1)}, u32[]{:S(2)}, u32[]{:S(2)}) collective-permute-start(f32[1,4,128,128]{3,2,1,0:T(8,128)S(1)} %slice.117), channel_id=1, source_target_pairs={{0,1},{1,0},{2,3},{3,2},{4,5},{5,4},{6,7},{7,6},{8,9},{9,8},{10,11... | collective-permute-start | bytes 786440 | tf_op jit(solution)/shard_map/ppermute | solution.py:462
  200.7 24.1 %collective-permute-start.39 = (f32[2,4,128,128]{3,2,1,0:T(8,128)S(1)}, f32[2,4,128,128]{3,2,1,0:T(8,128)S(1)}, u32[]{:S(2)}, u32[]{:S(2)}) collective-permute-start(f32[2,4,128,128]{3,2,1,0:T(8,128)S(1)} %pad_maximum_fusion.8), channel_id=1, source_target_pairs={{0,1},{1,0},{2,3},{3,2},{4,5},{5,4},{6,7},{7,6},{8,9},{9,8},{10,11... | collective-permute-start | bytes 1572872 | tf_op jit(solution)/shard_map/ppermute | solution.py:462
  227.7 24.4 %collective-permute-start.33 = (f32[2,4,128,128]{3,2,1,0:T(8,128)}, f32[2,4,128,128]{3,2,1,0:T(8,128)S(1)}, u32[]{:S(2)}, u32[]{:S(2)}) collective-permute-start(f32[2,4,128,128]{3,2,1,0:T(8,128)} %get-tuple-element.156), channel_id=1, source_target_pairs={{0,14},{1,15},{2,8},{3,9},{4,10},{5,11},{6,12},{7,13},{8,6},{9,7},... | collective-permute-start | bytes 1572872 | tf_op jit(solution)/shard_map/ppermute | solution.py:462
  231.1 34.3 %collective-permute-start.48 = (f32[2,4,128,128]{3,2,1,0:T(8,128)}, f32[2,4,128,128]{3,2,1,0:T(8,128)S(1)}, u32[]{:S(2)}, u32[]{:S(2)}) collective-permute-start(f32[2,4,128,128]{3,2,1,0:T(8,128)} %get-tuple-element.169), channel_id=1, source_target_pairs={{0,10},{1,11},{2,12},{3,13},{4,14},{5,15},{6,8},{7,9},{8,2},{9,3},... | collective-permute-start | bytes 1572872 | tf_op jit(solution)/shard_map/ppermute | solution.py:462
  235.7 29.8 %collective-permute-start.49 = (f32[2,4,128,128]{3,2,1,0:T(8,128)}, f32[2,4,128,128]{3,2,1,0:T(8,128)S(1)}, u32[]{:S(2)}, u32[]{:S(2)}) collective-permute-start(f32[2,4,128,128]{3,2,1,0:T(8,128)} %get-tuple-element.170), channel_id=1, source_target_pairs={{0,6},{1,7},{2,0},{3,1},{4,2},{5,3},{6,4},{7,5},{8,14},{9,15},{10,... | collective-permute-start | bytes 1572872 | tf_op jit(solution)/shard_map/ppermute | solution.py:462
  240.8 35.8 %collective-permute-start.51 = (f32[2,4,128,128]{3,2,1,0:T(8,128)S(1)}, f32[2,4,128,128]{3,2,1,0:T(8,128)S(1)}, u32[]{:S(2)}, u32[]{:S(2)}) collective-permute-start(f32[2,4,128,128]{3,2,1,0:T(8,128)S(1)} %copy-done.48), channel_id=1, source_target_pairs={{0,12},{1,13},{2,14},{3,15},{4,8},{5,9},{6,10},{7,11},{8,4},{9,5},... | collective-permute-start | bytes 1572872 | tf_op jit(solution)/shard_map/ppermute | solution.py:462
  252.1 31.1 %collective-permute-start.32 = (f32[2,4,128,128]{3,2,1,0:T(8,128)}, f32[2,4,128,128]{3,2,1,0:T(8,128)S(1)}, u32[]{:S(2)}, u32[]{:S(2)}) collective-permute-start(f32[2,4,128,128]{3,2,1,0:T(8,128)} %pad_maximum_fusion.6), channel_id=1, source_target_pairs={{0,1},{1,0},{2,3},{3,2},{4,5},{5,4},{6,7},{7,6},{8,9},{9,8},{10,11... | collective-permute-start | bytes 1572872 | tf_op jit(solution)/shard_map/ppermute | solution.py:462
  254.5 28.8 %collective-permute-start.35 = (f32[2,4,128,128]{3,2,1,0:T(8,128)}, f32[2,4,128,128]{3,2,1,0:T(8,128)S(1)}, u32[]{:S(2)}, u32[]{:S(2)}) collective-permute-start(f32[2,4,128,128]{3,2,1,0:T(8,128)} %pad_maximum_fusion.7), channel_id=1, source_target_pairs={{0,1},{1,0},{2,3},{3,2},{4,5},{5,4},{6,7},{7,6},{8,9},{9,8},{10,11... | collective-permute-start | bytes 1572872 | tf_op jit(solution)/shard_map/ppermute | solution.py:462
  (85 other events, 1630.3 us)

commit v2 on v1

--- a/solution.py
+++ b/solution.py
@@ -33,8 +33,8 @@
     return (z + dz) % 2 * 8 + (y + sign * dy + 4) % 4 * 2 + (core + dc) % 2
 
 
-def pair_spec(piece):
-    return pl.BlockSpec((2, 1, piece, LANES), lambda i: (0, i, 0, 0))
+def pair_spec(piece, count=2):
+    return pl.BlockSpec((count, 1, piece, LANES), lambda i, *_: (0, i, 0, 0))
 
 
 def piece_specs(pieces):
@@ -175,9 +175,9 @@
     return k[0] * centre + k[1] * west + k[2] * east + k[3] * south + k[4] * north
 
 
-def forecast_kernel(first, fields, rows, members, dest_ref, x_hbm, cx_ref, cy_ref, df_ref, own_ref, left_ref, right_ref, left_k_ref, right_k_ref, row_ref, row_k_ref, dl_ref, dr_ref, *refs):
+def forecast_kernel(first, fields, rows, members, outs, dest_ref, x_hbm, cx_ref, cy_ref, df_ref, own_ref, left_ref, right_ref, left_k_ref, right_k_ref, row_ref, row_k_ref, dl_ref, dr_ref, *refs):
     k_main, k_edge, k_row, edge_s, first_s, x_s, second_s, beside_s, held, sems = refs[-10:]
-    out_refs = refs[-10 - len(CHIPS) : -10]
+    out_refs = refs[-10 - outs : -10]
     step = pl.program_id(0)
     pitch = rows + PITCH
 
@@ -267,10 +267,13 @@
     for i in range(COUNT):
         base = dest_ref[i] * HEIGHT
         for r in range(HEIGHT):
-            out_refs[i // 2][i % 2, 0, r * members : (r + 1) * members, :] = second_s[base + r]
-
-
-def forecast(x, coefficients, edge, moved, dest, first, fields, after):
+            if outs == 1:
+                out_refs[0][i, 0, r * members : (r + 1) * members, :] = second_s[i * HEIGHT + r]
+            else:
+                out_refs[i // 2][i % 2, 0, r * members : (r + 1) * members, :] = second_s[base + r]
+
+
+def forecast(x, coefficients, edge, moved, dest, first, fields, after, outs):
     _, members, rows, _ = x.shape
     row, left, right, corner_l, corner_r = moved
     last = row.shape[0] - 1
@@ -281,7 +284,7 @@
     corner_spec = pl.BlockSpec((1, members, LANES), lambda i: (first + i, 0, 0))
     piece = HEIGHT * members
     return pl.pallas_call(
-        functools.partial(forecast_kernel, first, fields, rows, members),
+        functools.partial(forecast_kernel, first, fields, rows, members, outs),
         grid=(fields,),
         in_specs=[
             pl.BlockSpec(memory_space=pltpu.SMEM),
@@ -300,8 +303,11 @@
             corner_spec,
         ]
         + [pl.BlockSpec(memory_space=pl.ANY) for _ in after],
-        out_specs=[pair_spec(piece)] * len(CHIPS),
-        out_shape=[jax.ShapeDtypeStruct((2, fields, piece, LANES), jnp.float32)] * len(CHIPS),
+        out_specs=[pair_spec(piece, COUNT if outs == 1 else 2)] * outs,
+        out_shape=[
+            jax.ShapeDtypeStruct((COUNT if outs == 1 else 2, fields, piece, LANES), jnp.float32)
+        ]
+        * outs,
         scratch_shapes=[
             pltpu.VMEM((5, rows, LANES), jnp.float32),
             pltpu.VMEM((groups, 8, LANES), jnp.float32),
@@ -380,7 +386,7 @@
     )(place, *arrays(pieces), *after)
 
 
-def transform_kernel(mix_ref, *refs):
+def transform_kernel(places_ref, mix_ref, *refs):
     x_refs, out_refs, (high_s, low_s) = refs[:COUNT], refs[COUNT:-2], refs[-2:]
 
     @pl.when(pl.program_id(0) == 0)
@@ -402,19 +408,27 @@
                 ]
 
 
-def transform(pieces, mixing_t):
-    _, fields, piece, _ = pieces[0][0].shape
+def transform(pieces, mixing_t, places):
+    _, fields, piece, _ = pieces[0].shape
     members = mixing_t.shape[0]
+
+    def spec(i):
+        return pl.BlockSpec((1, 1, piece, LANES), lambda f, at: (at[i], f, 0, 0))
+
     return pl.pallas_call(
         transform_kernel,
-        grid=(fields,),
-        in_specs=[pl.BlockSpec((members, members), lambda i: (0, 0))] + piece_specs(pieces),
-        out_specs=[pair_spec(piece)] * len(CHIPS),
+        grid_spec=pltpu.PrefetchScalarGridSpec(
+            num_scalar_prefetch=1,
+            grid=(fields,),
+            in_specs=[pl.BlockSpec((members, members), lambda f, at: (0, 0))]
+            + [spec(i) for i in range(COUNT)],
+            out_specs=[pair_spec(piece)] * len(CHIPS),
+            scratch_shapes=[
+                pltpu.VMEM((members, members), jnp.bfloat16),
+                pltpu.VMEM((members, members), jnp.bfloat16),
+            ],
+        ),
         out_shape=[jax.ShapeDtypeStruct((2, fields, piece, LANES), jnp.float32)] * len(CHIPS),
-        scratch_shapes=[
-            pltpu.VMEM((members, members), jnp.bfloat16),
-            pltpu.VMEM((members, members), jnp.bfloat16),
-        ],
         compiler_params=pltpu.CompilerParams(vmem_limit_bytes=VMEM_LIMIT),
         cost_estimate=pl.CostEstimate(
             flops=fields * members * members * HEIGHT * LANES * 6,
@@ -422,7 +436,7 @@
             transcendentals=0,
         ),
         name="transform",
-    )(mixing_t, *arrays(pieces))
+    )(places, mixing_t, *pieces)
 
 
 def unpack_kernel(members, rows, dest_ref, *refs):
@@ -589,48 +603,48 @@
     dest = jnp.stack([shifted(tile, o) for o in OFFSETS]).astype(jnp.int32)
     half = total // 2
 
-    def fields_sent(first, after=()):
-        return list(
-            forecast(prior_members, coefficients, packed[0], moved, dest, first, half, after)
-        )
-
+    source = jnp.stack([shifted(tile, o, -1) for o in OFFSETS]).astype(jnp.int32)
     packed = pack(prior_members, coefficients, 0, total)
     moved = exchange(packed)
-    sent = fields_sent(0)
+
+    def fields_sent(first, after, outs):
+        return list(
+            forecast(prior_members, coefficients, packed[0], moved, dest, first, half, after, outs)
+        )
+
+    sent = fields_sent(0, (), len(CHIPS))
     arrived = travel(sent[:EARLY], 1)
     traded = [trade(arrived, GROUPS[0])]
-    following = fields_sent(half, sent[:1])
+    following = fields_sent(half, arrived[1:2], 1)
     following, sent[EARLY:] = lax.optimization_barrier((following, sent[EARLY:]))
     arrived += travel(sent[EARLY:], 1, EARLY)
+    following, arrived[1:] = lax.optimization_barrier((following, arrived[1:]))
     traded += [trade(arrived, group) for group in GROUPS[1:]]
-    sent = following
-    traded, sent[EARLY:] = lax.optimization_barrier((traded, sent[EARLY:]))
+    second = lax.all_to_all(following[0], "mem", split_axis=0, concat_axis=0, tiled=True)
     gathered = settled(arrived, traded)
 
     level, cell = own_row(report_level, tile), own_row(report_cell, tile)
     place = (level * (HEIGHT * LANES) + cell)[None, :]
     mixing_t = mixing_transposed(
-        sample(gathered, place, sent[:1]),
+        sample(gathered, place, following),
         own_row(report_value, tile),
         own_row(report_precision, tile),
         own_row(report_class, tile),
         own_row(report_count, tile),
     )
-    mixing_t, sent[EARLY:] = lax.optimization_barrier((mixing_t, sent[EARLY:]))
-    analysed = list(transform(gathered, mixing_t))
-    analysed, sent[LATE:] = lax.optimization_barrier((analysed, sent[LATE:]))
-    gathered = spread_out(sent, 1)
+    leads = jnp.array([p[1] for p in gathered], jnp.int32)
+    analysed = list(transform(arrays(gathered), mixing_t, leads))
 
     arrived = travel(analysed[:EARLY], -1)
     traded = [trade(arrived, GROUPS[0])]
-    ready = list(transform(gathered, mixing_t))
+    ready = list(transform([second] * COUNT, mixing_t, source))
     ready, analysed[EARLY:] = lax.optimization_barrier((ready, analysed[EARLY:]))
     arrived += travel(analysed[EARLY:], -1, EARLY)
     traded += [trade(arrived, group) for group in GROUPS[1:]]
     traded, ready[EARLY:] = lax.optimization_barrier((traded, ready[EARLY:]))
-    returned = [settled(arrived, traded), spread_out(ready, -1)]
-    result = unpack(returned[0], None, dest, 0, total, members, rows)
-    result = unpack(returned[1], result, dest, half, total, members, rows)
+    result = unpack(settled(arrived, traded), None, dest, 0, total, members, rows)
+    result, ready[LATE:] = lax.optimization_barrier((result, ready[LATE:]))
+    result = unpack(spread_out(ready, -1), result, dest, half, total, members, rows)
     return result.reshape(prior_members.shape)
 
 

time: 292 us -> 273 us (0.935)
  starting transfers between devices: 85.9 us -> 74.9 us
  waiting for transfers between devices: 105 us -> 98.8 us
    ppermute x48 -> x36, starting transfers between devices: 78.4 us -> 57.3 us  [hop(): lax.ppermute(value, 'mem', [(i, shifted(i, offset, sign)) for i in range(...]
    ppermute x48 -> x36, waiting for transfers between devices: 91.5 us -> 74.5 us  [hop(): lax.ppermute(value, 'mem', [(i, shifted(i, offset, sign)) for i in range(...]
    all_to_all x0 -> x1, waiting for transfers between devices: none -> 10.4 us  [on_device(): lax.all_to_all(following[0], 'mem', split_axis=0, concat_axis=0, tiled=True)]
    all_to_all x0 -> x1, starting transfers between devices: none -> 10.2 us  [on_device(): lax.all_to_all(following[0], 'mem', split_axis=0, concat_axis=0, tiled=True)]
    unnamed x112 -> x84, local copies, waits for them, and re-layouts: 6.83 us -> 5.91 us
    slice x32 -> x25, local copies, waits for them, and re-layouts: 6.85 us -> 6.84 us  [trade(): arrived[o][1:2]]
  transfers between devices with their start and end apart: 53 -> 42, of which waited for: 16 -> 17; matrix products, arithmetic and copies ran while one was open for 6% -> 6% of each run, Pallas kernels for 17% -> 19%
where the time goes in v2:
time: 273 us; the launch traced here: 272 us
  waiting for transfers between devices  98.8 us (36%)
  Pallas kernels  75.5 us (28%)
  starting transfers between devices  74.9 us (27%)
  local copies, waits for them, and re-layouts  16.6 us (6%)
  other arithmetic  4.94 us (2%)
    ppermute x36, waiting for transfers between devices, hop(): lax.ppermute(value, 'mem', [(i, shifted(i, offset, sign)) for i in range(...  74.5 us
    ppermute x36, starting transfers between devices, hop(): lax.ppermute(value, 'mem', [(i, shifted(i, offset, sign)) for i in range(...  57.3 us
    pallas_call x2, Pallas kernels, forecast(): pl.pallas_call(functools.partial(forecast_kernel, first, fields, rows, me...  24.3 us
    pallas_call x2, Pallas kernels, transform(): pl.pallas_call(transform_kernel, grid_spec=pltpu.PrefetchScalarGridSpec(n...  17.9 us
    pallas_call x1, Pallas kernels, mixing_transposed(): pl.pallas_call(mixing_kernel, in_specs=[pl.BlockSpec(memory_space=pltpu.S...  11.4 us
    all_to_all x1, waiting for transfers between devices, on_device(): lax.all_to_all(following[0], 'mem', split_axis=0, concat_axis=0, tiled=True)  10.4 us
    all_to_all x1, starting transfers between devices, on_device(): lax.all_to_all(following[0], 'mem', split_axis=0, concat_axis=0, tiled=True)  10.2 us
    pallas_call x2, Pallas kernels, unpack(): pl.pallas_call(functools.partial(unpack_kernel, members, rows), grid=(fie...  9.69 us
  transfers between devices with their start and end apart: 42, of which 17 were waited for; matrix products, arithmetic and copies ran while one was open for 6% of the time, Pallas kernels for 19%

profile of v2, /device:TPU:1, one launch (start us, length us, event | category | flops | bytes accessed | tf_op | source)
XLA Modules:
  0.0 271.5 jit_solution(2656006370794608304)
XLA Ops:
  0.0 6.9 %pack_edges.1 = (f32[9,2,32,128]{3,2,1,0:T(8,128)}, f32[9,4,32,128]{3,2,1,0:T(8,128)}, f32[9,32,128]{2,1,0:T(8,128)}) custom-call(f32[8,32,64,128]{3,2,1,0:T(8,128)} %x_hbm.3, f32[64,128]{1,0:T(8,128)} %cx_ref.5, f32[64,128]{1,0:T(8,128)} %cy_ref.5, f32[64,128]{1,0:T(8,128)} %df_ref.5), custom_call_target="tpu_custom_call" | custom-call | flops 4194304 | bytes 16777216 | tf_op jit(solution)/shard_map/pack_edges/pallas_call | solution.py:118
  15.1 5.7 %collective-permute-done.4.dr_ref = f32[9,32,128]{2,1,0:T(8,128)S(1)} collective-permute-done((f32[9,32,128]{2,1,0:T(8,128)}, f32[9,32,128]{2,1,0:T(8,128)S(1)}, u32[]{:S(2)}, u32[]{:S(2)}) %collective-permute-start.4) | collective-permute-done | bytes 147488 | tf_op jit(solution)/shard_map/ppermute | solution.py:163
  23.9 5.2 %collective-permute-done.2.row_ref.row_k_ref = f32[9,4,32,128]{3,2,1,0:T(8,128)S(1)} collective-permute-done((f32[9,4,32,128]{3,2,1,0:T(8,128)}, f32[9,4,32,128]{3,2,1,0:T(8,128)S(1)}, u32[]{:S(2)}, u32[]{:S(2)}) %collective-permute-start.2) | collective-permute-done | bytes 589856 | tf_op jit(solution)/shard_map/ppermute | solution.py:159
  29.9 12.4 %forecast.2 = (f32[2,4,128,128]{3,2,1,0:T(8,128)}, f32[2,4,128,128]{3,2,1,0:T(8,128)}, f32[2,4,128,128]{3,2,1,0:T(8,128)}, f32[2,4,128,128]{3,2,1,0:T(8,128)}, f...) custom-call(s32[16]{0:T(128)} %stack.110.dest_ref, ...), custom_call_target="tpu_custom_call" | custom-call | flops 18874368 | bytes 8388608 | tf_op jit(solution)/shard_map/forecast/pallas_call | solution.py:286
  50.9 5.6 %collective-permute-done.6.refs_0_.refs_2_ = f32[2,4,128,128]{3,2,1,0:T(8,128)S(1)} collective-permute-done((f32[2,4,128,128]{3,2,1,0:T(8,128)}, f32[2,4,128,128]{3,2,1,0:T(8,128)S(1)}, u32[]{:S(2)}, u32[]{:S(2)}) %collective-permute-start.6) | collective-permute-done | bytes 524320 | tf_op jit(solution)/shard_map/ppermute | solution.py:476
  57.3 11.9 %forecast.3.refs_16_ = f32[16,4,128,128]{3,2,1,0:T(8,128)} custom-call(s32[16]{0:T(128)} %stack.110.dest_ref, f32[8,32,64,128]{3,2,1,0:T(8,128)} %x_hbm.3, f32[64,128]{1,0:T(8,128)} %cx_ref.5, f32[64,128]{1,0:T(8,128)} %cy_ref.5, f32[64,128]{1,0:T(8,128)} %df_ref.5, f32[9,2,32,128]{3,2,1,0:T(8,128)} %get-tuple-element.65.own_ref, ...), custom_call_target="tpu_custom_call" | custom-call | flops 18874368 | bytes 8388608 | tf_op jit(solution)/shard_map/forecast/pallas_call | solution.py:286
  69.2 5.1 %collective-permute-start.10 = (f32[2,4,128,128]{3,2,1,0:T(8,128)}, f32[2,4,128,128]{3,2,1,0:T(8,128)S(1)}, u32[]{:S(2)}, u32[]{:S(2)}) collective-permute-start(f32[2,4,128,128]{3,2,1,0:T(8,128)} %get-tuple-element.77), channel_id=1, source_target_pairs={{0,14},{1,15},{2,8},{3,9},{4,10},{5,11},{6,12},{7,13},{8,6},{9,7},... | collective-permute-start | bytes 1572872 | tf_op jit(solution)/shard_map/ppermute | solution.py:476
  76.2 7.0 %collective-permute-done.10.refs_10_ = f32[2,4,128,128]{3,2,1,0:T(8,128)S(1)} collective-permute-done((f32[2,4,128,128]{3,2,1,0:T(8,128)}, f32[2,4,128,128]{3,2,1,0:T(8,128)S(1)}, u32[]{:S(2)}, u32[]{:S(2)}) %collective-permute-start.10) | collective-permute-done | bytes 524320 | tf_op jit(solution)/shard_map/ppermute | solution.py:476
  84.5 11.1 %collective-permute-done.12.refs_14_ = f32[2,4,128,128]{3,2,1,0:T(8,128)} collective-permute-done((f32[2,4,128,128]{3,2,1,0:T(8,128)S(1)}, f32[2,4,128,128]{3,2,1,0:T(8,128)}, u32[]{:S(2)}, u32[]{:S(2)}) %collective-permute-start.12) | collective-permute-done | bytes 524320 | tf_op jit(solution)/shard_map/ppermute | solution.py:476
  95.6 10.2 %all-to-all-start = ((f32[16,4,128,128]{3,2,1,0:T(8,128)}), f32[16,4,128,128]{3,2,1,0:T(8,128)}, u32[]{:S(2)}, u32[]{:S(2)}) async-start(f32[16,4,128,128]{3,2,1,0:T(8,128)} %forecast.3.refs_16_), calls=%async_computation | async-start | bytes 8388608 | tf_op jit(solution)/shard_map/all_to_all | solution.py:623
  117.6 5.3 %sample.1.raw_ref = f32[512,256]{1,0:T(8,128)} custom-call(s32[1,256]{1,0:T(1,128)} %fusion.5.place_ref, f32[2,4,128,128]{3,2,1,0:T(8,128)} %get-tuple-element.68.refs_0_, f32[1,4,128,128]{3,2,1,0:T(8,128)} %copy-done.38, f32[2,4,128,128]{3,2,1,0:T(8,128)} %copy-done.5, f32[2,4,128,128]{3,2,1,0:T(8,128)} %copy-done.12, f32[2,4,128,128]{3,2,1,0:T(8,128)} %copy-done.22, ...), custom_call_target="tpu_custom_call" | custom-call | flops 1610612736 | bytes 4194304 | tf_op jit(solution)/shard_map/sample/pallas_call | solution.py:371
  122.9 11.4 %mixing.1.mix_ref = f32[512,512]{1,0:T(8,128)} custom-call(s32[1]{0:T(128)} %bitcast.28.count_ref, f32[512,256]{1,0:T(8,128)} %sample.1.raw_ref, f32[1,256]{1,0:T(1,128)} %get-tuple-element.125.value_ref, f32[1,256]{1,0:T(1,128)} %get-tuple-element.126.precision_ref, s32[1,256]{1,0:T(1,128)} %fusion.4.class_ref), custom_call_target="tpu_custom_call" | custom-call | flops 4026531840 | bytes 1048576 | tf_op jit(solution)/shard_map/mixing/pallas_call | solution.py:558
  134.3 8.9 %transform.3 = (f32[2,4,128,128]{3,2,1,0:T(8,128)}, f32[2,4,128,128]{3,2,1,0:T(8,128)}, f32[2,4,128,128]{3,2,1,0:T(8,128)}, f32[2,4,128,128]{3,2,1,0:T(8,128)}, ...) custom-call(s32[16]{0:T(128)} %constant.553.clone.places_ref, ...), custom_call_target="tpu_custom_call" | custom-call | flops 3221225472 | bytes 8388608 | tf_op jit(solution)/shard_map/transform/pallas_call | solution.py:418
  151.2 10.4 %all-to-all-done.refs_0_.refs_1_.refs_2_.refs_3_.refs_4_.refs_5_.refs_6_.refs_7_.refs_8_.refs_9_.refs_10_.refs_11_.refs_12_.refs_13_.refs_14_.refs_15_ = f32[16,4,128,128]{3,2,1,0:T(8,128)} async-done(((f32[16,4,128,128]{3,2,1,0:T(8,128)}), f32[16,4,128,128]{3,2,1,0:T(8,128)}, u32[]{:S(2)}, u32[]{:S(2)}) %all-to-all-start) | async-done | bytes 4194336 | tf_op jit(solution)/shard_map/all_to_all | solution.py:623
  161.5 8.9 %transform.2 = (f32[2,4,128,128]{3,2,1,0:T(8,128)}, f32[2,4,128,128]{3,2,1,0:T(8,128)}, f32[2,4,128,128]{3,2,1,0:T(8,128)}, f32[2,4,128,128]{3,2,1,0:T(8,128)}, ...) custom-call(s32[16]{0:T(128)} %stack.123.places_ref, ...), custom_call_target="tpu_custom_call" | custom-call | flops 3221225472 | bytes 8388608 | tf_op jit(solution)/shard_map/transform/pallas_call | solution.py:418
  170.4 4.7 %collective-permute-start.31 = (f32[2,4,128,128]{3,2,1,0:T(8,128)}, f32[2,4,128,128]{3,2,1,0:T(8,128)S(1)}, u32[]{:S(2)}, u32[]{:S(2)}) collective-permute-start(f32[2,4,128,128]{3,2,1,0:T(8,128)} %get-tuple-element.109), channel_id=1, source_target_pairs={{0,10},{1,11},{2,12},{3,13},{4,14},{5,15},{6,8},{7,9},{8,2},{9,3},... | collective-permute-start | bytes 1572872 | tf_op jit(solution)/shard_map/ppermute | solution.py:476
  185.1 10.2 %collective-permute-done.31.refs_10_ = f32[2,4,128,128]{3,2,1,0:T(8,128)S(1)} collective-permute-done((f32[2,4,128,128]{3,2,1,0:T(8,128)}, f32[2,4,128,128]{3,2,1,0:T(8,128)S(1)}, u32[]{:S(2)}, u32[]{:S(2)}) %collective-permute-start.31) | collective-permute-done | bytes 524320 | tf_op jit(solution)/shard_map/ppermute | solution.py:476
  196.5 10.1 %collective-permute-done.34.refs_14_ = f32[2,4,128,128]{3,2,1,0:T(8,128)S(1)} collective-permute-done((f32[2,4,128,128]{3,2,1,0:T(8,128)}, f32[2,4,128,128]{3,2,1,0:T(8,128)S(1)}, u32[]{:S(2)}, u32[]{:S(2)}) %collective-permute-start.34) | collective-permute-done | bytes 524320 | tf_op jit(solution)/shard_map/ppermute | solution.py:476
  222.3 4.1 %collective-permute-done.19.refs_4_ = f32[2,4,128,128]{3,2,1,0:T(8,128)S(1)} collective-permute-done((f32[2,4,128,128]{3,2,1,0:T(8,128)}, f32[2,4,128,128]{3,2,1,0:T(8,128)S(1)}, u32[]{:S(2)}, u32[]{:S(2)}) %collective-permute-start.19) | collective-permute-done | bytes 524320 | tf_op jit(solution)/shard_map/ppermute | solution.py:476
  228.0 4.9 %unpack.2.refs_16_ = f32[8,2048,128]{2,1,0:T(8,128)} custom-call(s32[16]{0:T(128)} %stack.110.dest_ref, f32[2,4,128,128]{3,2,1,0:T(8,128)} %get-tuple-element.104.refs_0_, f32[1,4,128,128]{3,2,1,0:T(8,128)} %copy-done.34, f32[2,4,128,128]{3,2,1,0:T(8,128)} %copy-done.16, f32[2,4,128,128]{3,2,1,0:T(8,128)} %copy-done.6, f32[2,4,128,128]{3,2,1,0:T(8,128)} %copy-done.17, ...), custom_call_target="tpu_custom_call" | custom-call | bytes 8388608 | tf_op jit(solution)/shard_map/unpack/pallas_call | solution.py:457
  232.8 5.3 %collective-permute-start.39 = (f32[2,4,128,128]{3,2,1,0:T(8,128)}, f32[2,4,128,128]{3,2,1,0:T(8,128)S(1)}, u32[]{:S(2)}, u32[]{:S(2)}) collective-permute-start(f32[2,4,128,128]{3,2,1,0:T(8,128)} %get-tuple-element.123), channel_id=1, source_target_pairs={{0,12},{1,13},{2,14},{3,15},{4,8},{5,9},{6,10},{7,11},{8,4},{9,5},... | collective-permute-start | bytes 1572872 | tf_op jit(solution)/shard_map/ppermute | solution.py:476
  242.9 8.6 %collective-permute-done.36.refs_10_ = f32[2,4,128,128]{3,2,1,0:T(8,128)} collective-permute-done((f32[2,4,128,128]{3,2,1,0:T(8,128)}, f32[2,4,128,128]{3,2,1,0:T(8,128)}, u32[]{:S(2)}, u32[]{:S(2)}) %collective-permute-start.36) | collective-permute-done | bytes 524320 | tf_op jit(solution)/shard_map/ppermute | solution.py:476
  254.2 8.9 %collective-permute-done.39.refs_14_ = f32[2,4,128,128]{3,2,1,0:T(8,128)S(1)} collective-permute-done((f32[2,4,128,128]{3,2,1,0:T(8,128)}, f32[2,4,128,128]{3,2,1,0:T(8,128)S(1)}, u32[]{:S(2)}, u32[]{:S(2)}) %collective-permute-start.39) | collective-permute-done | bytes 524320 | tf_op jit(solution)/shard_map/ppermute | solution.py:476
  266.5 4.8 %unpack.3 = f32[8,2048,128]{2,1,0:T(8,128)} custom-call(s32[16]{0:T(128)} %stack.110.dest_ref, f32[2,4,128,128]{3,2,1,0:T(8,128)} %get-tuple-element.99.refs_0_, f32[1,4,128,128]{3,2,1,0:T(8,128)} %copy-done.36, f32[2,4,128,128]{3,2,1,0:T(8,128)} %copy-done.23, f32[2,4,128,128]{3,2,1,0:T(8,128)} %copy-done.11, ...), custom_call_target="tpu_custom_call", output_to_operand_aliasing={{}: (17, {})} | custom-call | bytes 8388608 | tf_op jit(solution)/shard_map/unpack/pallas_call | solution.py:457
  (193 shorter events, 83.4 us)
Async XLA Ops:
  6.9 22.1 %collective-permute-start.2 = (f32[9,4,32,128]{3,2,1,0:T(8,128)}, f32[9,4,32,128]{3,2,1,0:T(8,128)S(1)}, u32[]{:S(2)}, u32[]{:S(2)}) collective-permute-start(f32[9,4,32,128]{3,2,1,0:T(8,128)} %get-tuple-element.66), channel_id=1, source_target_pairs={{0,64},{64,0},{1,65},{65,1},{2,66},{66,2},{3,67},{67,3},{4,68},{68... | collective-permute-start | bytes 1769480 | tf_op jit(solution)/shard_map/ppermute | solution.py:159
  45.5 28.9 %collective-permute-start.7 = (f32[2,4,128,128]{3,2,1,0:T(8,128)}, f32[2,4,128,128]{3,2,1,0:T(8,128)S(1)}, u32[]{:S(2)}, u32[]{:S(2)}) collective-permute-start(f32[2,4,128,128]{3,2,1,0:T(8,128)} %get-tuple-element.74), channel_id=1, source_target_pairs={{0,4},{1,5},{2,6},{3,7},{4,0},{5,1},{6,2},{7,3},{8,12},{9,13},{10,... | collective-permute-start | bytes 1572872 | tf_op jit(solution)/shard_map/ppermute | solution.py:476
  48.4 27.8 %collective-permute-start.8 = (f32[2,4,128,128]{3,2,1,0:T(8,128)}, f32[2,4,128,128]{3,2,1,0:T(8,128)S(1)}, u32[]{:S(2)}, u32[]{:S(2)}) collective-permute-start(f32[2,4,128,128]{3,2,1,0:T(8,128)} %get-tuple-element.75), channel_id=1, source_target_pairs={{0,10},{1,11},{2,12},{3,13},{4,14},{5,15},{6,8},{7,9},{8,2},{9,3},... | collective-permute-start | bytes 1572872 | tf_op jit(solution)/shard_map/ppermute | solution.py:476
  48.6 27.6 %collective-permute-start.9 = (f32[2,4,128,128]{3,2,1,0:T(8,128)}, f32[2,4,128,128]{3,2,1,0:T(8,128)S(1)}, u32[]{:S(2)}, u32[]{:S(2)}) collective-permute-start(f32[2,4,128,128]{3,2,1,0:T(8,128)} %get-tuple-element.76), channel_id=1, source_target_pairs={{0,6},{1,7},{2,0},{3,1},{4,2},{5,3},{6,4},{7,5},{8,14},{9,15},{10,... | collective-permute-start | bytes 1572872 | tf_op jit(solution)/shard_map/ppermute | solution.py:476
  74.4 21.2 %collective-permute-start.12 = (f32[2,4,128,128]{3,2,1,0:T(8,128)S(1)}, f32[2,4,128,128]{3,2,1,0:T(8,128)}, u32[]{:S(2)}, u32[]{:S(2)}) collective-permute-start(f32[2,4,128,128]{3,2,1,0:T(8,128)S(1)} %copy-done.40), channel_id=1, source_target_pairs={{0,12},{1,13},{2,14},{3,15},{4,8},{5,9},{6,10},{7,11},{8,4},{9,5},... | collective-permute-start | bytes 1572872 | tf_op jit(solution)/shard_map/ppermute | solution.py:476
  95.6 66.0 %all-to-all-start = ((f32[16,4,128,128]{3,2,1,0:T(8,128)}), f32[16,4,128,128]{3,2,1,0:T(8,128)}, u32[]{:S(2)}, u32[]{:S(2)}) async-start(f32[16,4,128,128]{3,2,1,0:T(8,128)} %forecast.3.refs_16_), calls=%async_computation | async-start | bytes 8388608 | tf_op jit(solution)/shard_map/all_to_all | solution.py:623
  143.3 31.8 %collective-permute-start.25 = (f32[2,4,128,128]{3,2,1,0:T(8,128)}, f32[2,4,128,128]{3,2,1,0:T(8,128)S(1)}, u32[]{:S(2)}, u32[]{:S(2)}) collective-permute-start(f32[2,4,128,128]{3,2,1,0:T(8,128)} %get-tuple-element.105), channel_id=1, source_target_pairs={{0,8},{1,9},{2,10},{3,11},{4,12},{5,13},{6,14},{7,15},{8,0},{9,1},... | collective-permute-start | bytes 1572872 | tf_op jit(solution)/shard_map/ppermute | solution.py:476
  146.4 29.2 %collective-permute-start.26 = (f32[2,4,128,128]{3,2,1,0:T(8,128)}, f32[2,4,128,128]{3,2,1,0:T(8,128)S(1)}, u32[]{:S(2)}, u32[]{:S(2)}) collective-permute-start(f32[2,4,128,128]{3,2,1,0:T(8,128)} %get-tuple-element.106), channel_id=1, source_target_pairs={{0,4},{1,5},{2,6},{3,7},{4,0},{5,1},{6,2},{7,3},{8,12},{9,13},{10,... | collective-permute-start | bytes 1572872 | tf_op jit(solution)/shard_map/ppermute | solution.py:476
  149.7 30.2 %collective-permute-start.28 = (f32[2,4,128,128]{3,2,1,0:T(8,128)}, f32[2,4,128,128]{3,2,1,0:T(8,128)S(1)}, u32[]{:S(2)}, u32[]{:S(2)}) collective-permute-start(f32[2,4,128,128]{3,2,1,0:T(8,128)} %get-tuple-element.107), channel_id=1, source_target_pairs={{0,14},{1,15},{2,8},{3,9},{4,10},{5,11},{6,12},{7,13},{8,6},{9,7},... | collective-permute-start | bytes 1572872 | tf_op jit(solution)/shard_map/ppermute | solution.py:476
  150.6 33.5 %collective-permute-start.29 = (f32[2,4,128,128]{3,2,1,0:T(8,128)}, f32[2,4,128,128]{3,2,1,0:T(8,128)S(1)}, u32[]{:S(2)}, u32[]{:S(2)}) collective-permute-start(f32[2,4,128,128]{3,2,1,0:T(8,128)} %get-tuple-element.108), channel_id=1, source_target_pairs={{0,2},{1,3},{2,4},{3,5},{4,6},{5,7},{6,0},{7,1},{8,10},{9,11},{10,... | collective-permute-start | bytes 1572872 | tf_op jit(solution)/shard_map/ppermute | solution.py:476
  170.4 24.8 %collective-permute-start.31 = (f32[2,4,128,128]{3,2,1,0:T(8,128)}, f32[2,4,128,128]{3,2,1,0:T(8,128)S(1)}, u32[]{:S(2)}, u32[]{:S(2)}) collective-permute-start(f32[2,4,128,128]{3,2,1,0:T(8,128)} %get-tuple-element.109), channel_id=1, source_target_pairs={{0,10},{1,11},{2,12},{3,13},{4,14},{5,15},{6,8},{7,9},{8,2},{9,3},... | collective-permute-start | bytes 1572872 | tf_op jit(solution)/shard_map/ppermute | solution.py:476
  175.1 21.2 %collective-permute-start.32 = (f32[2,4,128,128]{3,2,1,0:T(8,128)}, f32[2,4,128,128]{3,2,1,0:T(8,128)S(1)}, u32[]{:S(2)}, u32[]{:S(2)}) collective-permute-start(f32[2,4,128,128]{3,2,1,0:T(8,128)} %get-tuple-element.110), channel_id=1, source_target_pairs={{0,6},{1,7},{2,0},{3,1},{4,2},{5,3},{6,4},{7,5},{8,14},{9,15},{10,... | collective-permute-start | bytes 1572872 | tf_op jit(solution)/shard_map/ppermute | solution.py:476
  175.6 30.9 %collective-permute-start.34 = (f32[2,4,128,128]{3,2,1,0:T(8,128)}, f32[2,4,128,128]{3,2,1,0:T(8,128)S(1)}, u32[]{:S(2)}, u32[]{:S(2)}) collective-permute-start(f32[2,4,128,128]{3,2,1,0:T(8,128)} %get-tuple-element.111), channel_id=1, source_target_pairs={{0,12},{1,13},{2,14},{3,15},{4,8},{5,9},{6,10},{7,11},{8,4},{9,5},... | collective-permute-start | bytes 1572872 | tf_op jit(solution)/shard_map/ppermute | solution.py:476
  179.9 30.3 %collective-permute-start.27 = (f32[2,4,128,128]{3,2,1,0:T(8,128)S(1)}, f32[2,4,128,128]{3,2,1,0:T(8,128)S(1)}, u32[]{:S(2)}, u32[]{:S(2)}) collective-permute-start(f32[2,4,128,128]{3,2,1,0:T(8,128)S(1)} %pad_maximum_fusion.5), channel_id=1, source_target_pairs={{0,1},{1,0},{2,3},{3,2},{4,5},{5,4},{6,7},{7,6},{8,9},{9,8},{10,11... | collective-permute-start | bytes 1572872 | tf_op jit(solution)/shard_map/ppermute | solution.py:476
  184.1 25.0 %collective-permute-start.24 = (f32[1,4,128,128]{3,2,1,0:T(8,128)S(1)}, f32[1,4,128,128]{3,2,1,0:T(8,128)S(1)}, u32[]{:S(2)}, u32[]{:S(2)}) collective-permute-start(f32[1,4,128,128]{3,2,1,0:T(8,128)S(1)} %slice.85), channel_id=1, source_target_pairs={{0,1},{1,0},{2,3},{3,2},{4,5},{5,4},{6,7},{7,6},{8,9},{9,8},{10,11... | collective-permute-start | bytes 786440 | tf_op jit(solution)/shard_map/ppermute | solution.py:476
  195.3 18.6 %collective-permute-start.30 = (f32[2,4,128,128]{3,2,1,0:T(8,128)S(1)}, f32[2,4,128,128]{3,2,1,0:T(8,128)S(1)}, u32[]{:S(2)}, u32[]{:S(2)}) collective-permute-start(f32[2,4,128,128]{3,2,1,0:T(8,128)S(1)} %pad_maximum_fusion.6), channel_id=1, source_target_pairs={{0,1},{1,0},{2,3},{3,2},{4,5},{5,4},{6,7},{7,6},{8,9},{9,8},{10,11... | collective-permute-start | bytes 1572872 | tf_op jit(solution)/shard_map/ppermute | solution.py:476
  196.4 21.4 %collective-permute-start.33 = (f32[2,4,128,128]{3,2,1,0:T(8,128)S(1)}, f32[2,4,128,128]{3,2,1,0:T(8,128)S(1)}, u32[]{:S(2)}, u32[]{:S(2)}) collective-permute-start(f32[2,4,128,128]{3,2,1,0:T(8,128)S(1)} %pad_maximum_fusion.7), channel_id=1, source_target_pairs={{0,1},{1,0},{2,3},{3,2},{4,5},{5,4},{6,7},{7,6},{8,9},{9,8},{10,11... | collective-permute-start | bytes 1572872 | tf_op jit(solution)/shard_map/ppermute | solution.py:476
  213.9 25.2 %collective-permute-start.21 = (f32[2,4,128,128]{3,2,1,0:T(8,128)}, f32[2,4,128,128]{3,2,1,0:T(8,128)}, u32[]{:S(2)}, u32[]{:S(2)}) collective-permute-start(f32[2,4,128,128]{3,2,1,0:T(8,128)} %get-tuple-element.102), channel_id=1, source_target_pairs={{0,14},{1,15},{2,8},{3,9},{4,10},{5,11},{6,12},{7,13},{8,6},{9,7},... | collective-permute-start | bytes 1572872 | tf_op jit(solution)/shard_map/ppermute | solution.py:476
  217.3 24.4 %collective-permute-start.22 = (f32[2,4,128,128]{3,2,1,0:T(8,128)}, f32[2,4,128,128]{3,2,1,0:T(8,128)}, u32[]{:S(2)}, u32[]{:S(2)}) collective-permute-start(f32[2,4,128,128]{3,2,1,0:T(8,128)} %get-tuple-element.103), channel_id=1, source_target_pairs={{0,2},{1,3},{2,4},{3,5},{4,6},{5,7},{6,0},{7,1},{8,10},{9,11},{10,... | collective-permute-start | bytes 1572872 | tf_op jit(solution)/shard_map/ppermute | solution.py:476
  217.8 33.7 %collective-permute-start.36 = (f32[2,4,128,128]{3,2,1,0:T(8,128)}, f32[2,4,128,128]{3,2,1,0:T(8,128)}, u32[]{:S(2)}, u32[]{:S(2)}) collective-permute-start(f32[2,4,128,128]{3,2,1,0:T(8,128)} %get-tuple-element.115), channel_id=1, source_target_pairs={{0,10},{1,11},{2,12},{3,13},{4,14},{5,15},{6,8},{7,9},{8,2},{9,3},... | collective-permute-start | bytes 1572872 | tf_op jit(solution)/shard_map/ppermute | solution.py:476
  221.0 31.4 %collective-permute-start.37 = (f32[2,4,128,128]{3,2,1,0:T(8,128)}, f32[2,4,128,128]{3,2,1,0:T(8,128)}, u32[]{:S(2)}, u32[]{:S(2)}) collective-permute-start(f32[2,4,128,128]{3,2,1,0:T(8,128)} %get-tuple-element.116), channel_id=1, source_target_pairs={{0,6},{1,7},{2,0},{3,1},{4,2},{5,3},{6,4},{7,5},{8,14},{9,15},{10,... | collective-permute-start | bytes 1572872 | tf_op jit(solution)/shard_map/ppermute | solution.py:476
  232.8 30.2 %collective-permute-start.39 = (f32[2,4,128,128]{3,2,1,0:T(8,128)}, f32[2,4,128,128]{3,2,1,0:T(8,128)S(1)}, u32[]{:S(2)}, u32[]{:S(2)}) collective-permute-start(f32[2,4,128,128]{3,2,1,0:T(8,128)} %get-tuple-element.123), channel_id=1, source_target_pairs={{0,12},{1,13},{2,14},{3,15},{4,8},{5,9},{6,10},{7,11},{8,4},{9,5},... | collective-permute-start | bytes 1572872 | tf_op jit(solution)/shard_map/ppermute | solution.py:476
  239.1 24.8 %collective-permute-start.20 = (f32[2,4,128,128]{3,2,1,0:T(8,128)S(1)}, f32[2,4,128,128]{3,2,1,0:T(8,128)S(1)}, u32[]{:S(2)}, u32[]{:S(2)}) collective-permute-start(f32[2,4,128,128]{3,2,1,0:T(8,128)S(1)} %pad_maximum_fusion.3), channel_id=1, source_target_pairs={{0,1},{1,0},{2,3},{3,2},{4,5},{5,4},{6,7},{7,6},{8,9},{9,8},{10,11... | collective-permute-start | bytes 1572872 | tf_op jit(solution)/shard_map/ppermute | solution.py:476
  242.8 21.1 %collective-permute-start.23 = (f32[2,4,128,128]{3,2,1,0:T(8,128)S(1)}, f32[2,4,128,128]{3,2,1,0:T(8,128)S(1)}, u32[]{:S(2)}, u32[]{:S(2)}) collective-permute-start(f32[2,4,128,128]{3,2,1,0:T(8,128)S(1)} %pad_maximum_fusion.4), channel_id=1, source_target_pairs={{0,1},{1,0},{2,3},{3,2},{4,5},{5,4},{6,7},{7,6},{8,9},{9,8},{10,11... | collective-permute-start | bytes 1572872 | tf_op jit(solution)/shard_map/ppermute | solution.py:476
  (61 other events, 991.0 us)

commit v3 on v2

--- a/solution.py
+++ b/solution.py
@@ -75,7 +75,7 @@
                 parts[i % 4] = jnp.where(lane // 4 == i, moved, parts[i % 4])
             packed.append((parts[0] + parts[1]) + (parts[2] + parts[3]))
             edge_ref[0, group, 0:tall, :] = packed[group]
-        corner_ref[0, 0:tall, :] = jnp.where(lane < LANES // 2, packed[0], packed[-1])
+        return packed
 
     for field in range(fields):
 
@@ -90,14 +90,19 @@
                     row_ref[0, picked.index(row)] = value
                 return value
 
-            gather(read, members)
+            packed = gather(read, members)
+            lane = iota((members, LANES), 1)
+            top = pltpu.roll(packed[0], 8 * field % LANES, 1)
+            bottom = pltpu.roll(packed[-1], (8 * field + 8) % LANES, 1)
+            corner = jnp.where(lane % 8 < 4, top, bottom)
+            before = jnp.zeros_like(corner) if field == 0 else corner_ref[...]
+            corner_ref[...] = jnp.where(lane // 8 == field, corner, before)
 
     @pl.when(step == fields)
     def _():
         sub = iota((8, LANES), 0)
         row_ref[0] = jnp.zeros((4, members, LANES), jnp.float32)
         edge_ref[0] = jnp.zeros((groups, members, LANES), jnp.float32)
-        corner_ref[0] = jnp.zeros((members, LANES), jnp.float32)
 
         def read(row):
             at = slice(row, row + 1)
@@ -123,12 +128,12 @@
         out_specs=[
             pl.BlockSpec((1, groups, members, LANES), lambda i: (i, 0, 0, 0)),
             pl.BlockSpec((1, 4, members, LANES), lambda i: (i, 0, 0, 0)),
-            pl.BlockSpec((1, members, LANES), lambda i: (i, 0, 0)),
+            pl.BlockSpec((members, LANES), lambda i: (0, 0)),
         ],
         out_shape=[
             jax.ShapeDtypeStruct((fields + 1, groups, members, LANES), jnp.float32),
             jax.ShapeDtypeStruct((fields + 1, 4, members, LANES), jnp.float32),
-            jax.ShapeDtypeStruct((fields + 1, members, LANES), jnp.float32),
+            jax.ShapeDtypeStruct((members, LANES), jnp.float32),
         ],
         scratch_shapes=[
             pltpu.VMEM((fields, members, rows + PITCH, LANES), jnp.float32),
@@ -216,7 +221,13 @@
                 k_row[side, i : i + 1, :] = w
 
     edges = [jnp.where(from_left, left_ref[0, g], right_ref[0, g]) for g in range(groups)]
-    corner = jnp.where(from_left, dl_ref[0], dr_ref[0])
+    corner = jnp.where(from_left, dl_ref[...], dr_ref[...])
+    turn = 8 * (first + step)
+    corner = jnp.where(
+        lane < LANES // 2,
+        pltpu.roll(corner, lax.rem(LANES - turn, LANES), 1),
+        pltpu.roll(corner, LANES - 8 - turn, 1),
+    )
     chain = [corner] + edges + [corner]
     up = [pltpu.roll(v, 4, 1) for v in chain]
     down = [pltpu.roll(v, LANES - 4, 1) for v in chain]
@@ -281,7 +292,7 @@
     small = pl.BlockSpec((rows, LANES), lambda i: (0, 0))
     edge_spec = pl.BlockSpec((1, groups, members, LANES), lambda i: (first + i, 0, 0, 0))
     edge_last = pl.BlockSpec((1, groups, members, LANES), lambda i: (last, 0, 0, 0))
-    corner_spec = pl.BlockSpec((1, members, LANES), lambda i: (first + i, 0, 0))
+    corner_spec = pl.BlockSpec((members, LANES), lambda i: (0, 0))
     piece = HEIGHT * members
     return pl.pallas_call(
         functools.partial(forecast_kernel, first, fields, rows, members, outs),
@@ -495,11 +506,6 @@
     return pieces
 
 
-def spread_out(sent, sign):
-    arrived = travel(sent, sign)
-    return settled(arrived, [trade(arrived, group) for group in GROUPS])
-
-
 def dot3(a, b, dims=(1, 0)):
     (ah, al), (bh, bl) = halves(a), halves(b)
 
@@ -615,7 +621,7 @@
     sent = fields_sent(0, (), len(CHIPS))
     arrived = travel(sent[:EARLY], 1)
     traded = [trade(arrived, GROUPS[0])]
-    following = fields_sent(half, arrived[1:2], 1)
+    following = fields_sent(half, traded, 1)
     following, sent[EARLY:] = lax.optimization_barrier((following, sent[EARLY:]))
     arrived += travel(sent[EARLY:], 1, EARLY)
     following, arrived[1:] = lax.optimization_barrier((following, arrived[1:]))
@@ -643,8 +649,10 @@
     traded += [trade(arrived, group) for group in GROUPS[1:]]
     traded, ready[EARLY:] = lax.optimization_barrier((traded, ready[EARLY:]))
     result = unpack(settled(arrived, traded), None, dest, 0, total, members, rows)
-    result, ready[LATE:] = lax.optimization_barrier((result, ready[LATE:]))
-    result = unpack(spread_out(ready, -1), result, dest, half, total, members, rows)
+    arrived = travel(ready, -1)
+    result, arrived[EARLY] = lax.optimization_barrier((result, arrived[EARLY]))
+    traded = [trade(arrived, group) for group in GROUPS]
+    result = unpack(settled(arrived, traded), result, dest, half, total, members, rows)
     return result.reshape(prior_members.shape)
 
 

time: 273 us -> 265 us (0.971)
  waiting for transfers between devices: 98.8 us -> 89.8 us
    ppermute x36, waiting for transfers between devices: 74.5 us -> 69.3 us  [hop(): lax.ppermute(value, 'mem', [(i, shifted(i, offset, sign)) for i in range(...]
    ppermute x36, starting transfers between devices: 57.3 us -> 61.7 us  [hop(): lax.ppermute(value, 'mem', [(i, shifted(i, offset, sign)) for i in range(...]
    ppermute x1, waiting for transfers between devices: 5.66 us -> 2.75 us  [exchange(): lax.ppermute(corner, ('gx', 'gy'), diagonal(-1))]
    slice x25 -> x24, local copies, waits for them, and re-layouts: 6.84 us -> 5.2 us  [trade(): arrived[o][1:2]]
    unnamed x84 -> x86, local copies, waits for them, and re-layouts: 5.91 us -> 5.86 us
  transfers between devices with their start and end apart: 42 -> 42, of which waited for: 17 -> 18; matrix products, arithmetic and copies ran while one was open for 6% -> 6% of each run, Pallas kernels for 19% -> 19%
where the time goes in v3:
time: 265 us; the launch traced here: 264 us
  waiting for transfers between devices  89.8 us (34%)
  starting transfers between devices  77.6 us (29%)
  Pallas kernels  75.2 us (28%)
  local copies, waits for them, and re-layouts  14.8 us (6%)
  other arithmetic  5.71 us (2%)
    ppermute x36, waiting for transfers between devices, hop(): lax.ppermute(value, 'mem', [(i, shifted(i, offset, sign)) for i in range(...  69.3 us
    ppermute x36, starting transfers between devices, hop(): lax.ppermute(value, 'mem', [(i, shifted(i, offset, sign)) for i in range(...  61.7 us
    pallas_call x2, Pallas kernels, forecast(): pl.pallas_call(functools.partial(forecast_kernel, first, fields, rows, me...  23.9 us
    pallas_call x2, Pallas kernels, transform(): pl.pallas_call(transform_kernel, grid_spec=pltpu.PrefetchScalarGridSpec(n...  17.9 us
    all_to_all x1, waiting for transfers between devices, on_device(): lax.all_to_all(following[0], 'mem', split_axis=0, concat_axis=0, tiled=True)  12.3 us
    pallas_call x1, Pallas kernels, mixing_transposed(): pl.pallas_call(mixing_kernel, in_specs=[pl.BlockSpec(memory_space=pltpu.S...  11.3 us
    pallas_call x2, Pallas kernels, unpack(): pl.pallas_call(functools.partial(unpack_kernel, members, rows), grid=(fie...  9.65 us
    all_to_all x1, starting transfers between devices, on_device(): lax.all_to_all(following[0], 'mem', split_axis=0, concat_axis=0, tiled=True)  8.42 us
  transfers between devices with their start and end apart: 42, of which 18 were waited for; matrix products, arithmetic and copies ran while one was open for 6% of the time, Pallas kernels for 19%

profile of v3, /device:TPU:1, one launch (start us, length us, event | category | flops | bytes accessed | tf_op | source)
XLA Modules:
  0.0 263.9 jit_solution(4661087970148516453)
XLA Ops:
  0.0 7.1 %pack_edges.1 = (f32[9,2,32,128]{3,2,1,0:T(8,128)}, f32[9,4,32,128]{3,2,1,0:T(8,128)}, f32[32,128]{1,0:T(8,128)}) custom-call(f32[8,32,64,128]{3,2,1,0:T(8,128)} %x_hbm.3, f32[64,128]{1,0:T(8,128)} %cx_ref.5, f32[64,128]{1,0:T(8,128)} %cy_ref.5, f32[64,128]{1,0:T(8,128)} %df_ref.5), custom_call_target="tpu_custom_call" | custom-call | flops 4194304 | bytes 16777216 | tf_op jit(solution)/shard_map/pack_edges/pallas_call | solution.py:123
  24.5 12.2 %forecast.2 = (f32[2,4,128,128]{3,2,1,0:T(8,128)}, f32[2,4,128,128]{3,2,1,0:T(8,128)}, f32[2,4,128,128]{3,2,1,0:T(8,128)}, f32[2,4,128,128]{3,2,1,0:T(8,128)}, f...) custom-call(s32[16]{0:T(128)} %stack.110.dest_ref, ...), custom_call_target="tpu_custom_call" | custom-call | flops 18874368 | bytes 8388608 | tf_op jit(solution)/shard_map/forecast/pallas_call | solution.py:297
  36.7 3.2 %collective-permute-start.6 = (f32[2,4,128,128]{3,2,1,0:T(8,128)}, f32[2,4,128,128]{3,2,1,0:T(8,128)S(1)}, u32[]{:S(2)}, u32[]{:S(2)}) collective-permute-start(f32[2,4,128,128]{3,2,1,0:T(8,128)} %get-tuple-element.73), channel_id=1, source_target_pairs={{0,8},{1,9},{2,10},{3,11},{4,12},{5,13},{6,14},{7,15},{8,0},{9,1},... | collective-permute-start | bytes 1572872 | tf_op jit(solution)/shard_map/ppermute | solution.py:487
  48.9 11.7 %forecast.3.refs_16_ = f32[16,4,128,128]{3,2,1,0:T(8,128)} custom-call(s32[16]{0:T(128)} %stack.110.dest_ref, f32[8,32,64,128]{3,2,1,0:T(8,128)} %x_hbm.3, f32[64,128]{1,0:T(8,128)} %cx_ref.5, f32[64,128]{1,0:T(8,128)} %cy_ref.5, f32[64,128]{1,0:T(8,128)} %df_ref.5, f32[9,2,32,128]{3,2,1,0:T(8,128)} %get-tuple-element.65.own_ref, ...), custom_call_target="tpu_custom_call" | custom-call | flops 18874368 | bytes 8388608 | tf_op jit(solution)/shard_map/forecast/pallas_call | solution.py:297
  66.6 10.8 %collective-permute-done.10.refs_10_ = f32[2,4,128,128]{3,2,1,0:T(8,128)S(1)} collective-permute-done((f32[2,4,128,128]{3,2,1,0:T(8,128)}, f32[2,4,128,128]{3,2,1,0:T(8,128)S(1)}, u32[]{:S(2)}, u32[]{:S(2)}) %collective-permute-start.10) | collective-permute-done | bytes 524320 | tf_op jit(solution)/shard_map/ppermute | solution.py:487
  78.4 10.5 %collective-permute-done.12.refs_14_ = f32[2,4,128,128]{3,2,1,0:T(8,128)} collective-permute-done((f32[2,4,128,128]{3,2,1,0:T(8,128)}, f32[2,4,128,128]{3,2,1,0:T(8,128)}, u32[]{:S(2)}, u32[]{:S(2)}) %collective-permute-start.12) | collective-permute-done | bytes 524320 | tf_op jit(solution)/shard_map/ppermute | solution.py:487
  88.9 8.4 %all-to-all-start = ((f32[16,4,128,128]{3,2,1,0:T(8,128)}), f32[16,4,128,128]{3,2,1,0:T(8,128)}, u32[]{:S(2)}, u32[]{:S(2)}) async-start(f32[16,4,128,128]{3,2,1,0:T(8,128)} %forecast.3.refs_16_), calls=%async_computation | async-start | bytes 8388608 | tf_op jit(solution)/shard_map/all_to_all | solution.py:629
  107.6 5.3 %sample.1.raw_ref = f32[512,256]{1,0:T(8,128)} custom-call(s32[1,256]{1,0:T(1,128)} %fusion.5.place_ref, f32[2,4,128,128]{3,2,1,0:T(8,128)} %get-tuple-element.68.refs_0_, f32[1,4,128,128]{3,2,1,0:T(8,128)} %copy-done.33, f32[2,4,128,128]{3,2,1,0:T(8,128)} %copy-done.21, f32[2,4,128,128]{3,2,1,0:T(8,128)} %copy-done.12, f32[2,4,128,128]{3,2,1,0:T(8,128)} %copy-done.23, ...), custom_call_target="tpu_custom_call" | custom-call | flops 1610612736 | bytes 4194304 | tf_op jit(solution)/shard_map/sample/pallas_call | solution.py:382
  113.0 11.3 %mixing.1.mix_ref = f32[512,512]{1,0:T(8,128)} custom-call(s32[1]{0:T(128)} %bitcast.28.count_ref, f32[512,256]{1,0:T(8,128)} %sample.1.raw_ref, f32[1,256]{1,0:T(1,128)} %get-tuple-element.125.value_ref, f32[1,256]{1,0:T(1,128)} %get-tuple-element.126.precision_ref, s32[1,256]{1,0:T(1,128)} %fusion.4.class_ref), custom_call_target="tpu_custom_call" | custom-call | flops 4026531840 | bytes 1048576 | tf_op jit(solution)/shard_map/mixing/pallas_call | solution.py:564
  124.3 9.0 %transform.3 = (f32[2,4,128,128]{3,2,1,0:T(8,128)}, f32[2,4,128,128]{3,2,1,0:T(8,128)}, f32[2,4,128,128]{3,2,1,0:T(8,128)}, f32[2,4,128,128]{3,2,1,0:T(8,128)}, ...) custom-call(s32[16]{0:T(128)} %constant.553.clone.places_ref, ...), custom_call_target="tpu_custom_call" | custom-call | flops 3221225472 | bytes 8388608 | tf_op jit(solution)/shard_map/transform/pallas_call | solution.py:429
  141.0 12.3 %all-to-all-done.refs_0_.refs_1_.refs_2_.refs_3_.refs_4_.refs_5_.refs_6_.refs_7_.refs_8_.refs_9_.refs_10_.refs_11_.refs_12_.refs_13_.refs_14_.refs_15_ = f32[16,4,128,128]{3,2,1,0:T(8,128)} async-done(((f32[16,4,128,128]{3,2,1,0:T(8,128)}), f32[16,4,128,128]{3,2,1,0:T(8,128)}, u32[]{:S(2)}, u32[]{:S(2)}) %all-to-all-start) | async-done | bytes 4194336 | tf_op jit(solution)/shard_map/all_to_all | solution.py:629
  153.2 8.9 %transform.2 = (f32[2,4,128,128]{3,2,1,0:T(8,128)}, f32[2,4,128,128]{3,2,1,0:T(8,128)}, f32[2,4,128,128]{3,2,1,0:T(8,128)}, f32[2,4,128,128]{3,2,1,0:T(8,128)}, ...) custom-call(s32[16]{0:T(128)} %stack.123.places_ref, ...), custom_call_target="tpu_custom_call" | custom-call | flops 3221225472 | bytes 8388608 | tf_op jit(solution)/shard_map/transform/pallas_call | solution.py:429
  162.2 4.6 %collective-permute-start.31 = (f32[2,4,128,128]{3,2,1,0:T(8,128)}, f32[2,4,128,128]{3,2,1,0:T(8,128)S(1)}, u32[]{:S(2)}, u32[]{:S(2)}) collective-permute-start(f32[2,4,128,128]{3,2,1,0:T(8,128)} %get-tuple-element.109), channel_id=1, source_target_pairs={{0,10},{1,11},{2,12},{3,13},{4,14},{5,15},{6,8},{7,9},{8,2},{9,3},... | collective-permute-start | bytes 1572872 | tf_op jit(solution)/shard_map/ppermute | solution.py:487
  176.7 10.3 %collective-permute-done.31.refs_10_ = f32[2,4,128,128]{3,2,1,0:T(8,128)S(1)} collective-permute-done((f32[2,4,128,128]{3,2,1,0:T(8,128)}, f32[2,4,128,128]{3,2,1,0:T(8,128)S(1)}, u32[]{:S(2)}, u32[]{:S(2)}) %collective-permute-start.31) | collective-permute-done | bytes 524320 | tf_op jit(solution)/shard_map/ppermute | solution.py:487
  187.0 7.8 %collective-permute-start.24 = (f32[1,4,128,128]{3,2,1,0:T(8,128)S(1)}, f32[1,4,128,128]{3,2,1,0:T(8,128)S(1)}, u32[]{:S(2)}, u32[]{:S(2)}) collective-permute-start(f32[1,4,128,128]{3,2,1,0:T(8,128)S(1)} %slice.85), channel_id=1, source_target_pairs={{0,1},{1,0},{2,3},{3,2},{4,5},{5,4},{6,7},{7,6},{8,9},{9,8},{10,11... | collective-permute-start | bytes 786440 | tf_op jit(solution)/shard_map/ppermute | solution.py:487
  201.6 3.9 %collective-permute-start.19 = (f32[2,4,128,128]{3,2,1,0:T(8,128)}, f32[2,4,128,128]{3,2,1,0:T(8,128)S(1)}, u32[]{:S(2)}, u32[]{:S(2)}) collective-permute-start(f32[2,4,128,128]{3,2,1,0:T(8,128)} %get-tuple-element.101), channel_id=1, source_target_pairs={{0,4},{1,5},{2,6},{3,7},{4,0},{5,1},{6,2},{7,3},{8,12},{9,13},{10,... | collective-permute-start | bytes 1572872 | tf_op jit(solution)/shard_map/ppermute | solution.py:487
  209.5 3.2 %collective-permute-done.18.refs_2_ = f32[2,4,128,128]{3,2,1,0:T(8,128)S(1)} collective-permute-done((f32[2,4,128,128]{3,2,1,0:T(8,128)}, f32[2,4,128,128]{3,2,1,0:T(8,128)S(1)}, u32[]{:S(2)}, u32[]{:S(2)}) %collective-permute-start.18) | collective-permute-done | bytes 524320 | tf_op jit(solution)/shard_map/ppermute | solution.py:487
  213.7 4.2 %collective-permute-done.19.refs_4_ = f32[2,4,128,128]{3,2,1,0:T(8,128)S(1)} collective-permute-done((f32[2,4,128,128]{3,2,1,0:T(8,128)}, f32[2,4,128,128]{3,2,1,0:T(8,128)S(1)}, u32[]{:S(2)}, u32[]{:S(2)}) %collective-permute-start.19) | collective-permute-done | bytes 524320 | tf_op jit(solution)/shard_map/ppermute | solution.py:487
  218.8 5.1 %collective-permute-start.39 = (f32[2,4,128,128]{3,2,1,0:T(8,128)}, f32[2,4,128,128]{3,2,1,0:T(8,128)}, u32[]{:S(2)}, u32[]{:S(2)}) collective-permute-start(f32[2,4,128,128]{3,2,1,0:T(8,128)} %get-tuple-element.123), channel_id=1, source_target_pairs={{0,12},{1,13},{2,14},{3,15},{4,8},{5,9},{6,10},{7,11},{8,4},{9,5},... | collective-permute-start | bytes 1572872 | tf_op jit(solution)/shard_map/ppermute | solution.py:487
  224.8 5.1 %collective-permute-done.21.refs_6_ = f32[2,4,128,128]{3,2,1,0:T(8,128)S(1)} collective-permute-done((f32[2,4,128,128]{3,2,1,0:T(8,128)}, f32[2,4,128,128]{3,2,1,0:T(8,128)S(1)}, u32[]{:S(2)}, u32[]{:S(2)}) %collective-permute-start.21) | collective-permute-done | bytes 524320 | tf_op jit(solution)/shard_map/ppermute | solution.py:487
  232.1 4.8 %unpack.2.refs_16_ = f32[8,2048,128]{2,1,0:T(8,128)} custom-call(s32[16]{0:T(128)} %stack.110.dest_ref, f32[2,4,128,128]{3,2,1,0:T(8,128)} %get-tuple-element.104.refs_0_, f32[1,4,128,128]{3,2,1,0:T(8,128)} %copy-done.34, f32[2,4,128,128]{3,2,1,0:T(8,128)} %copy-done.15, f32[2,4,128,128]{3,2,1,0:T(8,128)} %copy-done.5, f32[2,4,128,128]{3,2,1,0:T(8,128)} %copy-done.16, ...), custom_call_target="tpu_custom_call" | custom-call | bytes 8388608 | tf_op jit(solution)/shard_map/unpack/pallas_call | solution.py:468
  236.9 5.9 %collective-permute-done.36.refs_10_ = f32[2,4,128,128]{3,2,1,0:T(8,128)} collective-permute-done((f32[2,4,128,128]{3,2,1,0:T(8,128)}, f32[2,4,128,128]{3,2,1,0:T(8,128)}, u32[]{:S(2)}, u32[]{:S(2)}) %collective-permute-start.36) | collective-permute-done | bytes 524320 | tf_op jit(solution)/shard_map/ppermute | solution.py:487
  245.6 8.9 %collective-permute-done.39.refs_14_ = f32[2,4,128,128]{3,2,1,0:T(8,128)} collective-permute-done((f32[2,4,128,128]{3,2,1,0:T(8,128)}, f32[2,4,128,128]{3,2,1,0:T(8,128)}, u32[]{:S(2)}, u32[]{:S(2)}) %collective-permute-start.39) | collective-permute-done | bytes 524320 | tf_op jit(solution)/shard_map/ppermute | solution.py:487
  258.9 4.8 %unpack.3 = f32[8,2048,128]{2,1,0:T(8,128)} custom-call(s32[16]{0:T(128)} %stack.110.dest_ref, f32[2,4,128,128]{3,2,1,0:T(8,128)} %get-tuple-element.99.refs_0_, f32[1,4,128,128]{3,2,1,0:T(8,128)} %copy-done.36, f32[2,4,128,128]{3,2,1,0:T(8,128)} %copy-done.24, f32[2,4,128,128]{3,2,1,0:T(8,128)} %copy-done.8, ...), custom_call_target="tpu_custom_call", output_to_operand_aliasing={{}: (17, {})} | custom-call | bytes 8388608 | tf_op jit(solution)/shard_map/unpack/pallas_call | solution.py:468
  (194 shorter events, 83.7 us)
Async XLA Ops:
  7.1 16.5 %collective-permute-start.2 = (f32[9,4,32,128]{3,2,1,0:T(8,128)}, f32[9,4,32,128]{3,2,1,0:T(8,128)S(1)}, u32[]{:S(2)}, u32[]{:S(2)}) collective-permute-start(f32[9,4,32,128]{3,2,1,0:T(8,128)} %get-tuple-element.66), channel_id=1, source_target_pairs={{0,64},{64,0},{1,65},{65,1},{2,66},{66,2},{3,67},{67,3},{4,68},{68... | collective-permute-start | bytes 1769480 | tf_op jit(solution)/shard_map/ppermute | solution.py:164
  36.7 26.9 %collective-permute-start.6 = (f32[2,4,128,128]{3,2,1,0:T(8,128)}, f32[2,4,128,128]{3,2,1,0:T(8,128)S(1)}, u32[]{:S(2)}, u32[]{:S(2)}) collective-permute-start(f32[2,4,128,128]{3,2,1,0:T(8,128)} %get-tuple-element.73), channel_id=1, source_target_pairs={{0,8},{1,9},{2,10},{3,11},{4,12},{5,13},{6,14},{7,15},{8,0},{9,1},... | collective-permute-start | bytes 1572872 | tf_op jit(solution)/shard_map/ppermute | solution.py:487
  39.9 25.2 %collective-permute-start.7 = (f32[2,4,128,128]{3,2,1,0:T(8,128)}, f32[2,4,128,128]{3,2,1,0:T(8,128)S(1)}, u32[]{:S(2)}, u32[]{:S(2)}) collective-permute-start(f32[2,4,128,128]{3,2,1,0:T(8,128)} %get-tuple-element.74), channel_id=1, source_target_pairs={{0,4},{1,5},{2,6},{3,7},{4,0},{5,1},{6,2},{7,3},{8,12},{9,13},{10,... | collective-permute-start | bytes 1572872 | tf_op jit(solution)/shard_map/ppermute | solution.py:487
  46.0 20.6 %collective-permute-start.8 = (f32[2,4,128,128]{3,2,1,0:T(8,128)}, f32[2,4,128,128]{3,2,1,0:T(8,128)S(1)}, u32[]{:S(2)}, u32[]{:S(2)}) collective-permute-start(f32[2,4,128,128]{3,2,1,0:T(8,128)} %get-tuple-element.75), channel_id=1, source_target_pairs={{0,10},{1,11},{2,12},{3,13},{4,14},{5,15},{6,8},{7,9},{8,2},{9,3},... | collective-permute-start | bytes 1572872 | tf_op jit(solution)/shard_map/ppermute | solution.py:487
  46.0 20.6 %collective-permute-start.9 = (f32[2,4,128,128]{3,2,1,0:T(8,128)}, f32[2,4,128,128]{3,2,1,0:T(8,128)S(1)}, u32[]{:S(2)}, u32[]{:S(2)}) collective-permute-start(f32[2,4,128,128]{3,2,1,0:T(8,128)} %get-tuple-element.76), channel_id=1, source_target_pairs={{0,6},{1,7},{2,0},{3,1},{4,2},{5,3},{6,4},{7,5},{8,14},{9,15},{10,... | collective-permute-start | bytes 1572872 | tf_op jit(solution)/shard_map/ppermute | solution.py:487
  60.7 16.7 %collective-permute-start.10 = (f32[2,4,128,128]{3,2,1,0:T(8,128)}, f32[2,4,128,128]{3,2,1,0:T(8,128)S(1)}, u32[]{:S(2)}, u32[]{:S(2)}) collective-permute-start(f32[2,4,128,128]{3,2,1,0:T(8,128)} %get-tuple-element.77), channel_id=1, source_target_pairs={{0,14},{1,15},{2,8},{3,9},{4,10},{5,11},{6,12},{7,13},{8,6},{9,7},... | collective-permute-start | bytes 1572872 | tf_op jit(solution)/shard_map/ppermute | solution.py:487
  65.1 23.8 %collective-permute-start.12 = (f32[2,4,128,128]{3,2,1,0:T(8,128)}, f32[2,4,128,128]{3,2,1,0:T(8,128)}, u32[]{:S(2)}, u32[]{:S(2)}) collective-permute-start(f32[2,4,128,128]{3,2,1,0:T(8,128)} %get-tuple-element.79), channel_id=1, source_target_pairs={{0,12},{1,13},{2,14},{3,15},{4,8},{5,9},{6,10},{7,11},{8,4},{9,5},... | collective-permute-start | bytes 1572872 | tf_op jit(solution)/shard_map/ppermute | solution.py:487
  88.9 64.3 %all-to-all-start = ((f32[16,4,128,128]{3,2,1,0:T(8,128)}), f32[16,4,128,128]{3,2,1,0:T(8,128)}, u32[]{:S(2)}, u32[]{:S(2)}) async-start(f32[16,4,128,128]{3,2,1,0:T(8,128)} %forecast.3.refs_16_), calls=%async_computation | async-start | bytes 8388608 | tf_op jit(solution)/shard_map/all_to_all | solution.py:629
  133.2 33.5 %collective-permute-start.25 = (f32[2,4,128,128]{3,2,1,0:T(8,128)}, f32[2,4,128,128]{3,2,1,0:T(8,128)S(1)}, u32[]{:S(2)}, u32[]{:S(2)}) collective-permute-start(f32[2,4,128,128]{3,2,1,0:T(8,128)} %get-tuple-element.105), channel_id=1, source_target_pairs={{0,8},{1,9},{2,10},{3,11},{4,12},{5,13},{6,14},{7,15},{8,0},{9,1},... | collective-permute-start | bytes 1572872 | tf_op jit(solution)/shard_map/ppermute | solution.py:487
  136.2 30.9 %collective-permute-start.26 = (f32[2,4,128,128]{3,2,1,0:T(8,128)}, f32[2,4,128,128]{3,2,1,0:T(8,128)S(1)}, u32[]{:S(2)}, u32[]{:S(2)}) collective-permute-start(f32[2,4,128,128]{3,2,1,0:T(8,128)} %get-tuple-element.106), channel_id=1, source_target_pairs={{0,4},{1,5},{2,6},{3,7},{4,0},{5,1},{6,2},{7,3},{8,12},{9,13},{10,... | collective-permute-start | bytes 1572872 | tf_op jit(solution)/shard_map/ppermute | solution.py:487
  139.5 31.9 %collective-permute-start.28 = (f32[2,4,128,128]{3,2,1,0:T(8,128)}, f32[2,4,128,128]{3,2,1,0:T(8,128)S(1)}, u32[]{:S(2)}, u32[]{:S(2)}) collective-permute-start(f32[2,4,128,128]{3,2,1,0:T(8,128)} %get-tuple-element.107), channel_id=1, source_target_pairs={{0,14},{1,15},{2,8},{3,9},{4,10},{5,11},{6,12},{7,13},{8,6},{9,7},... | collective-permute-start | bytes 1572872 | tf_op jit(solution)/shard_map/ppermute | solution.py:487
  140.4 35.4 %collective-permute-start.29 = (f32[2,4,128,128]{3,2,1,0:T(8,128)}, f32[2,4,128,128]{3,2,1,0:T(8,128)S(1)}, u32[]{:S(2)}, u32[]{:S(2)}) collective-permute-start(f32[2,4,128,128]{3,2,1,0:T(8,128)} %get-tuple-element.108), channel_id=1, source_target_pairs={{0,2},{1,3},{2,4},{3,5},{4,6},{5,7},{6,0},{7,1},{8,10},{9,11},{10,... | collective-permute-start | bytes 1572872 | tf_op jit(solution)/shard_map/ppermute | solution.py:487
  162.2 24.8 %collective-permute-start.31 = (f32[2,4,128,128]{3,2,1,0:T(8,128)}, f32[2,4,128,128]{3,2,1,0:T(8,128)S(1)}, u32[]{:S(2)}, u32[]{:S(2)}) collective-permute-start(f32[2,4,128,128]{3,2,1,0:T(8,128)} %get-tuple-element.109), channel_id=1, source_target_pairs={{0,10},{1,11},{2,12},{3,13},{4,14},{5,15},{6,8},{7,9},{8,2},{9,3},... | collective-permute-start | bytes 1572872 | tf_op jit(solution)/shard_map/ppermute | solution.py:487
  166.8 28.0 %collective-permute-start.32 = (f32[2,4,128,128]{3,2,1,0:T(8,128)}, f32[2,4,128,128]{3,2,1,0:T(8,128)S(1)}, u32[]{:S(2)}, u32[]{:S(2)}) collective-permute-start(f32[2,4,128,128]{3,2,1,0:T(8,128)} %get-tuple-element.110), channel_id=1, source_target_pairs={{0,6},{1,7},{2,0},{3,1},{4,2},{5,3},{6,4},{7,5},{8,14},{9,15},{10,... | collective-permute-start | bytes 1572872 | tf_op jit(solution)/shard_map/ppermute | solution.py:487
  167.1 31.0 %collective-permute-start.34 = (f32[2,4,128,128]{3,2,1,0:T(8,128)S(1)}, f32[2,4,128,128]{3,2,1,0:T(8,128)S(1)}, u32[]{:S(2)}, u32[]{:S(2)}) collective-permute-start(f32[2,4,128,128]{3,2,1,0:T(8,128)S(1)} %copy-done.41), channel_id=1, source_target_pairs={{0,12},{1,13},{2,14},{3,15},{4,8},{5,9},{6,10},{7,11},{8,4},{9,5},... | collective-permute-start | bytes 1572872 | tf_op jit(solution)/shard_map/ppermute | solution.py:487
  171.4 30.2 %collective-permute-start.27 = (f32[2,4,128,128]{3,2,1,0:T(8,128)S(1)}, f32[2,4,128,128]{3,2,1,0:T(8,128)S(1)}, u32[]{:S(2)}, u32[]{:S(2)}) collective-permute-start(f32[2,4,128,128]{3,2,1,0:T(8,128)S(1)} %pad_maximum_fusion.5), channel_id=1, source_target_pairs={{0,1},{1,0},{2,3},{3,2},{4,5},{5,4},{6,7},{7,6},{8,9},{9,8},{10,11... | collective-permute-start | bytes 1572872 | tf_op jit(solution)/shard_map/ppermute | solution.py:487
  175.8 29.7 %collective-permute-start.30 = (f32[2,4,128,128]{3,2,1,0:T(8,128)S(1)}, f32[2,4,128,128]{3,2,1,0:T(8,128)S(1)}, u32[]{:S(2)}, u32[]{:S(2)}) collective-permute-start(f32[2,4,128,128]{3,2,1,0:T(8,128)S(1)} %pad_maximum_fusion.6), channel_id=1, source_target_pairs={{0,1},{1,0},{2,3},{3,2},{4,5},{5,4},{6,7},{7,6},{8,9},{9,8},{10,11... | collective-permute-start | bytes 1572872 | tf_op jit(solution)/shard_map/ppermute | solution.py:487
  205.5 24.4 %collective-permute-start.21 = (f32[2,4,128,128]{3,2,1,0:T(8,128)}, f32[2,4,128,128]{3,2,1,0:T(8,128)S(1)}, u32[]{:S(2)}, u32[]{:S(2)}) collective-permute-start(f32[2,4,128,128]{3,2,1,0:T(8,128)} %get-tuple-element.102), channel_id=1, source_target_pairs={{0,14},{1,15},{2,8},{3,9},{4,10},{5,11},{6,12},{7,13},{8,6},{9,7},... | collective-permute-start | bytes 1572872 | tf_op jit(solution)/shard_map/ppermute | solution.py:487
  208.6 22.2 %collective-permute-start.22 = (f32[2,4,128,128]{3,2,1,0:T(8,128)}, f32[2,4,128,128]{3,2,1,0:T(8,128)S(1)}, u32[]{:S(2)}, u32[]{:S(2)}) collective-permute-start(f32[2,4,128,128]{3,2,1,0:T(8,128)} %get-tuple-element.103), channel_id=1, source_target_pairs={{0,2},{1,3},{2,4},{3,5},{4,6},{5,7},{6,0},{7,1},{8,10},{9,11},{10,... | collective-permute-start | bytes 1572872 | tf_op jit(solution)/shard_map/ppermute | solution.py:487
  209.2 33.7 %collective-permute-start.36 = (f32[2,4,128,128]{3,2,1,0:T(8,128)}, f32[2,4,128,128]{3,2,1,0:T(8,128)}, u32[]{:S(2)}, u32[]{:S(2)}) collective-permute-start(f32[2,4,128,128]{3,2,1,0:T(8,128)} %get-tuple-element.120), channel_id=1, source_target_pairs={{0,10},{1,11},{2,12},{3,13},{4,14},{5,15},{6,8},{7,9},{8,2},{9,3},... | collective-permute-start | bytes 1572872 | tf_op jit(solution)/shard_map/ppermute | solution.py:487
  212.7 31.2 %collective-permute-start.37 = (f32[2,4,128,128]{3,2,1,0:T(8,128)}, f32[2,4,128,128]{3,2,1,0:T(8,128)}, u32[]{:S(2)}, u32[]{:S(2)}) collective-permute-start(f32[2,4,128,128]{3,2,1,0:T(8,128)} %get-tuple-element.122), channel_id=1, source_target_pairs={{0,6},{1,7},{2,0},{3,1},{4,2},{5,3},{6,4},{7,5},{8,14},{9,15},{10,... | collective-permute-start | bytes 1572872 | tf_op jit(solution)/shard_map/ppermute | solution.py:487
  218.8 35.7 %collective-permute-start.39 = (f32[2,4,128,128]{3,2,1,0:T(8,128)}, f32[2,4,128,128]{3,2,1,0:T(8,128)}, u32[]{:S(2)}, u32[]{:S(2)}) collective-permute-start(f32[2,4,128,128]{3,2,1,0:T(8,128)} %get-tuple-element.123), channel_id=1, source_target_pairs={{0,12},{1,13},{2,14},{3,15},{4,8},{5,9},{6,10},{7,11},{8,4},{9,5},... | collective-permute-start | bytes 1572872 | tf_op jit(solution)/shard_map/ppermute | solution.py:487
  229.9 26.3 %collective-permute-start.20 = (f32[2,4,128,128]{3,2,1,0:T(8,128)}, f32[2,4,128,128]{3,2,1,0:T(8,128)S(1)}, u32[]{:S(2)}, u32[]{:S(2)}) collective-permute-start(f32[2,4,128,128]{3,2,1,0:T(8,128)} %pad_maximum_fusion.3), channel_id=1, source_target_pairs={{0,1},{1,0},{2,3},{3,2},{4,5},{5,4},{6,7},{7,6},{8,9},{9,8},{10,11... | collective-permute-start | bytes 1572872 | tf_op jit(solution)/shard_map/ppermute | solution.py:487
  232.0 24.3 %collective-permute-start.23 = (f32[2,4,128,128]{3,2,1,0:T(8,128)}, f32[2,4,128,128]{3,2,1,0:T(8,128)S(1)}, u32[]{:S(2)}, u32[]{:S(2)}) collective-permute-start(f32[2,4,128,128]{3,2,1,0:T(8,128)} %pad_maximum_fusion.4), channel_id=1, source_target_pairs={{0,1},{1,0},{2,3},{3,2},{4,5},{5,4},{6,7},{7,6},{8,9},{9,8},{10,11... | collective-permute-start | bytes 1572872 | tf_op jit(solution)/shard_map/ppermute | solution.py:487
  (61 other events, 1008.2 us)

commit v4 on v3

--- a/solution.py
+++ b/solution.py
@@ -646,10 +646,11 @@
     ready = list(transform([second] * COUNT, mixing_t, source))
     ready, analysed[EARLY:] = lax.optimization_barrier((ready, analysed[EARLY:]))
     arrived += travel(analysed[EARLY:], -1, EARLY)
+    final = travel(ready[:EARLY], -1)
+    arrived[1:], final[1:] = lax.optimization_barrier((arrived[1:], final[1:]))
     traded += [trade(arrived, group) for group in GROUPS[1:]]
-    traded, ready[EARLY:] = lax.optimization_barrier((traded, ready[EARLY:]))
     result = unpack(settled(arrived, traded), None, dest, 0, total, members, rows)
-    arrived = travel(ready, -1)
+    arrived = final + travel(ready[EARLY:], -1, EARLY)
     result, arrived[EARLY] = lax.optimization_barrier((result, arrived[EARLY]))
     traded = [trade(arrived, group) for group in GROUPS]
     result = unpack(settled(arrived, traded), result, dest, half, total, members, rows)

time: 265 us -> 267 us (level)
  starting transfers between devices: 77.6 us -> 86.9 us
  waiting for transfers between devices: 89.8 us -> 81.2 us
    ppermute x36, starting transfers between devices: 61.7 us -> 71 us  [hop(): lax.ppermute(value, 'mem', [(i, shifted(i, offset, sign)) for i in range(...]
    ppermute x36, waiting for transfers between devices: 69.3 us -> 60.9 us  [hop(): lax.ppermute(value, 'mem', [(i, shifted(i, offset, sign)) for i in range(...]
    unnamed x86 -> x84, local copies, waits for them, and re-layouts: 5.86 us -> 6.75 us
  transfers between devices with their start and end apart: 42 -> 42, of which waited for: 18 -> 19; matrix products, arithmetic and copies ran while one was open for 6% -> 6% of each run, Pallas kernels for 19% -> 19%
where the time goes in v4:
time: 267 us; the launch traced here: 265 us
  starting transfers between devices  86.9 us (33%)
  waiting for transfers between devices  81.2 us (30%)
  Pallas kernels  75.3 us (28%)
  local copies, waits for them, and re-layouts  15.9 us (6%)
  other arithmetic  5.55 us (2%)
    ppermute x36, starting transfers between devices, hop(): lax.ppermute(value, 'mem', [(i, shifted(i, offset, sign)) for i in range(...  71 us
    ppermute x36, waiting for transfers between devices, hop(): lax.ppermute(value, 'mem', [(i, shifted(i, offset, sign)) for i in range(...  60.9 us
    pallas_call x2, Pallas kernels, forecast(): pl.pallas_call(functools.partial(forecast_kernel, first, fields, rows, me...  23.9 us
    pallas_call x2, Pallas kernels, transform(): pl.pallas_call(transform_kernel, grid_spec=pltpu.PrefetchScalarGridSpec(n...  17.9 us
    all_to_all x1, waiting for transfers between devices, on_device(): lax.all_to_all(following[0], 'mem', split_axis=0, concat_axis=0, tiled=True)  12 us
    pallas_call x1, Pallas kernels, mixing_transposed(): pl.pallas_call(mixing_kernel, in_specs=[pl.BlockSpec(memory_space=pltpu.S...  11.4 us
    pallas_call x2, Pallas kernels, unpack(): pl.pallas_call(functools.partial(unpack_kernel, members, rows), grid=(fie...  9.66 us
    all_to_all x1, starting transfers between devices, on_device(): lax.all_to_all(following[0], 'mem', split_axis=0, concat_axis=0, tiled=True)  8.42 us
  transfers between devices with their start and end apart: 42, of which 19 were waited for; matrix products, arithmetic and copies ran while one was open for 6% of the time, Pallas kernels for 19%

profile of v4, /device:TPU:1, one launch (start us, length us, event | category | flops | bytes accessed | tf_op | source)
XLA Modules:
  0.0 265.4 jit_solution(1024747543036172449)
XLA Ops:
  0.0 7.1 %pack_edges.1 = (f32[9,2,32,128]{3,2,1,0:T(8,128)}, f32[9,4,32,128]{3,2,1,0:T(8,128)}, f32[32,128]{1,0:T(8,128)}) custom-call(f32[8,32,64,128]{3,2,1,0:T(8,128)} %x_hbm.3, f32[64,128]{1,0:T(8,128)} %cx_ref.5, f32[64,128]{1,0:T(8,128)} %cy_ref.5, f32[64,128]{1,0:T(8,128)} %df_ref.5), custom_call_target="tpu_custom_call" | custom-call | flops 4194304 | bytes 16777216 | tf_op jit(solution)/shard_map/pack_edges/pallas_call | solution.py:123
  24.5 12.1 %forecast.2 = (f32[2,4,128,128]{3,2,1,0:T(8,128)}, f32[2,4,128,128]{3,2,1,0:T(8,128)}, f32[2,4,128,128]{3,2,1,0:T(8,128)}, f32[2,4,128,128]{3,2,1,0:T(8,128)}, f...) custom-call(s32[16]{0:T(128)} %stack.110.dest_ref, ...), custom_call_target="tpu_custom_call" | custom-call | flops 18874368 | bytes 8388608 | tf_op jit(solution)/shard_map/forecast/pallas_call | solution.py:297
  48.8 11.7 %forecast.3.refs_16_ = f32[16,4,128,128]{3,2,1,0:T(8,128)} custom-call(s32[16]{0:T(128)} %stack.110.dest_ref, f32[8,32,64,128]{3,2,1,0:T(8,128)} %x_hbm.3, f32[64,128]{1,0:T(8,128)} %cx_ref.5, f32[64,128]{1,0:T(8,128)} %cy_ref.5, f32[64,128]{1,0:T(8,128)} %df_ref.5, f32[9,2,32,128]{3,2,1,0:T(8,128)} %get-tuple-element.68.own_ref, ...), custom_call_target="tpu_custom_call" | custom-call | flops 18874368 | bytes 8388608 | tf_op jit(solution)/shard_map/forecast/pallas_call | solution.py:297
  66.5 10.8 %collective-permute-done.10.refs_10_ = f32[2,4,128,128]{3,2,1,0:T(8,128)S(1)} collective-permute-done((f32[2,4,128,128]{3,2,1,0:T(8,128)}, f32[2,4,128,128]{3,2,1,0:T(8,128)S(1)}, u32[]{:S(2)}, u32[]{:S(2)}) %collective-permute-start.10) | collective-permute-done | bytes 524320 | tf_op jit(solution)/shard_map/ppermute | solution.py:487
  78.3 10.5 %collective-permute-done.12.refs_14_ = f32[2,4,128,128]{3,2,1,0:T(8,128)} collective-permute-done((f32[2,4,128,128]{3,2,1,0:T(8,128)S(1)}, f32[2,4,128,128]{3,2,1,0:T(8,128)}, u32[]{:S(2)}, u32[]{:S(2)}) %collective-permute-start.12) | collective-permute-done | bytes 524320 | tf_op jit(solution)/shard_map/ppermute | solution.py:487
  88.8 8.4 %all-to-all-start = ((f32[16,4,128,128]{3,2,1,0:T(8,128)}), f32[16,4,128,128]{3,2,1,0:T(8,128)}, u32[]{:S(2)}, u32[]{:S(2)}) async-start(f32[16,4,128,128]{3,2,1,0:T(8,128)} %forecast.3.refs_16_), calls=%async_computation | async-start | bytes 8388608 | tf_op jit(solution)/shard_map/all_to_all | solution.py:629
  107.7 5.3 %sample.1.raw_ref = f32[512,256]{1,0:T(8,128)} custom-call(s32[1,256]{1,0:T(1,128)} %fusion.5.place_ref, f32[2,4,128,128]{3,2,1,0:T(8,128)} %get-tuple-element.71.refs_0_, f32[1,4,128,128]{3,2,1,0:T(8,128)} %copy-done.33, f32[2,4,128,128]{3,2,1,0:T(8,128)} %copy-done.26, f32[2,4,128,128]{3,2,1,0:T(8,128)} %copy-done.12, f32[2,4,128,128]{3,2,1,0:T(8,128)} %copy-done.28, ...), custom_call_target="tpu_custom_call" | custom-call | flops 1610612736 | bytes 4194304 | tf_op jit(solution)/shard_map/sample/pallas_call | solution.py:382
  113.0 11.4 %mixing.1.mix_ref = f32[512,512]{1,0:T(8,128)} custom-call(s32[1]{0:T(128)} %bitcast.28.count_ref, f32[512,256]{1,0:T(8,128)} %sample.1.raw_ref, f32[1,256]{1,0:T(1,128)} %get-tuple-element.131.value_ref, f32[1,256]{1,0:T(1,128)} %get-tuple-element.132.precision_ref, s32[1,256]{1,0:T(1,128)} %fusion.4.class_ref), custom_call_target="tpu_custom_call" | custom-call | flops 4026531840 | bytes 1048576 | tf_op jit(solution)/shard_map/mixing/pallas_call | solution.py:564
  124.4 8.9 %transform.3 = (f32[2,4,128,128]{3,2,1,0:T(8,128)}, f32[2,4,128,128]{3,2,1,0:T(8,128)}, f32[2,4,128,128]{3,2,1,0:T(8,128)}, f32[2,4,128,128]{3,2,1,0:T(8,128)}, ...) custom-call(s32[16]{0:T(128)} %constant.553.clone.places_ref, ...), custom_call_target="tpu_custom_call" | custom-call | flops 3221225472 | bytes 8388608 | tf_op jit(solution)/shard_map/transform/pallas_call | solution.py:429
  141.2 12.0 %all-to-all-done.refs_0_.refs_1_.refs_2_.refs_3_.refs_4_.refs_5_.refs_6_.refs_7_.refs_8_.refs_9_.refs_10_.refs_11_.refs_12_.refs_13_.refs_14_.refs_15_ = f32[16,4,128,128]{3,2,1,0:T(8,128)} async-done(((f32[16,4,128,128]{3,2,1,0:T(8,128)}), f32[16,4,128,128]{3,2,1,0:T(8,128)}, u32[]{:S(2)}, u32[]{:S(2)}) %all-to-all-start) | async-done | bytes 4194336 | tf_op jit(solution)/shard_map/all_to_all | solution.py:629
  153.1 8.9 %transform.2 = (f32[2,4,128,128]{3,2,1,0:T(8,128)}, f32[2,4,128,128]{3,2,1,0:T(8,128)}, f32[2,4,128,128]{3,2,1,0:T(8,128)}, f32[2,4,128,128]{3,2,1,0:T(8,128)}, ...) custom-call(s32[16]{0:T(128)} %stack.123.places_ref, ...), custom_call_target="tpu_custom_call" | custom-call | flops 3221225472 | bytes 8388608 | tf_op jit(solution)/shard_map/transform/pallas_call | solution.py:429
  162.1 4.6 %collective-permute-start.22 = (f32[2,4,128,128]{3,2,1,0:T(8,128)}, f32[2,4,128,128]{3,2,1,0:T(8,128)S(1)}, u32[]{:S(2)}, u32[]{:S(2)}) collective-permute-start(f32[2,4,128,128]{3,2,1,0:T(8,128)} %get-tuple-element.107), channel_id=1, source_target_pairs={{0,10},{1,11},{2,12},{3,13},{4,14},{5,15},{6,8},{7,9},{8,2},{9,3},... | collective-permute-start | bytes 1572872 | tf_op jit(solution)/shard_map/ppermute | solution.py:487
  171.8 3.8 %collective-permute-done.21.refs_8_ = f32[2,4,128,128]{3,2,1,0:T(8,128)} collective-permute-done((f32[2,4,128,128]{3,2,1,0:T(8,128)}, f32[2,4,128,128]{3,2,1,0:T(8,128)}, u32[]{:S(2)}, u32[]{:S(2)}) %collective-permute-start.21) | collective-permute-done | bytes 524320 | tf_op jit(solution)/shard_map/ppermute | solution.py:487
  175.7 6.6 %collective-permute-start.26 = (f32[2,4,128,128]{3,2,1,0:T(8,128)}, f32[2,4,128,128]{3,2,1,0:T(8,128)S(1)}, u32[]{:S(2)}, u32[]{:S(2)}) collective-permute-start(f32[2,4,128,128]{3,2,1,0:T(8,128)} %get-tuple-element.111), channel_id=1, source_target_pairs={{0,4},{1,5},{2,6},{3,7},{4,0},{5,1},{6,2},{7,3},{8,12},{9,13},{10,... | collective-permute-start | bytes 1572872 | tf_op jit(solution)/shard_map/ppermute | solution.py:487
  182.2 4.7 %collective-permute-done.22.refs_10_ = f32[2,4,128,128]{3,2,1,0:T(8,128)S(1)} collective-permute-done((f32[2,4,128,128]{3,2,1,0:T(8,128)}, f32[2,4,128,128]{3,2,1,0:T(8,128)S(1)}, u32[]{:S(2)}, u32[]{:S(2)}) %collective-permute-start.22) | collective-permute-done | bytes 524320 | tf_op jit(solution)/shard_map/ppermute | solution.py:487
  186.9 4.1 %collective-permute-start.28 = (f32[2,4,128,128]{3,2,1,0:T(8,128)}, f32[2,4,128,128]{3,2,1,0:T(8,128)S(1)}, u32[]{:S(2)}, u32[]{:S(2)}) collective-permute-start(f32[2,4,128,128]{3,2,1,0:T(8,128)} %get-tuple-element.113), channel_id=1, source_target_pairs={{0,2},{1,3},{2,4},{3,5},{4,6},{5,7},{6,0},{7,1},{8,10},{9,11},{10,... | collective-permute-start | bytes 1572872 | tf_op jit(solution)/shard_map/ppermute | solution.py:487
  191.1 7.2 %collective-permute-done.24.refs_14_ = f32[2,4,128,128]{3,2,1,0:T(8,128)S(1)} collective-permute-done((f32[2,4,128,128]{3,2,1,0:T(8,128)}, f32[2,4,128,128]{3,2,1,0:T(8,128)S(1)}, u32[]{:S(2)}, u32[]{:S(2)}) %collective-permute-start.24) | collective-permute-done | bytes 524320 | tf_op jit(solution)/shard_map/ppermute | solution.py:487
  199.5 6.2 %collective-permute-done.25.refs_2_ = f32[2,4,128,128]{3,2,1,0:T(8,128)S(1)} collective-permute-done((f32[2,4,128,128]{3,2,1,0:T(8,128)}, f32[2,4,128,128]{3,2,1,0:T(8,128)S(1)}, u32[]{:S(2)}, u32[]{:S(2)}) %collective-permute-start.25) | collective-permute-done | bytes 524320 | tf_op jit(solution)/shard_map/ppermute | solution.py:487
  211.0 9.8 %collective-permute-done.28.refs_8_ = f32[2,4,128,128]{3,2,1,0:T(8,128)S(1)} collective-permute-done((f32[2,4,128,128]{3,2,1,0:T(8,128)}, f32[2,4,128,128]{3,2,1,0:T(8,128)S(1)}, u32[]{:S(2)}, u32[]{:S(2)}) %collective-permute-start.28) | collective-permute-done | bytes 524320 | tf_op jit(solution)/shard_map/ppermute | solution.py:487
  225.1 3.7 %collective-permute-start.36 = (f32[2,4,128,128]{3,2,1,0:T(8,128)}, f32[2,4,128,128]{3,2,1,0:T(8,128)}, u32[]{:S(2)}, u32[]{:S(2)}) collective-permute-start(f32[2,4,128,128]{3,2,1,0:T(8,128)} %get-tuple-element.126), channel_id=1, source_target_pairs={{0,10},{1,11},{2,12},{3,13},{4,14},{5,15},{6,8},{7,9},{8,2},{9,3},... | collective-permute-start | bytes 1572872 | tf_op jit(solution)/shard_map/ppermute | solution.py:487
  230.5 8.2 %collective-permute-start.39 = (f32[2,4,128,128]{3,2,1,0:T(8,128)}, f32[2,4,128,128]{3,2,1,0:T(8,128)}, u32[]{:S(2)}, u32[]{:S(2)}) collective-permute-start(f32[2,4,128,128]{3,2,1,0:T(8,128)} %get-tuple-element.129), channel_id=1, source_target_pairs={{0,12},{1,13},{2,14},{3,15},{4,8},{5,9},{6,10},{7,11},{8,4},{9,5},... | collective-permute-start | bytes 1572872 | tf_op jit(solution)/shard_map/ppermute | solution.py:487
  242.7 4.8 %unpack.2.refs_16_ = f32[8,2048,128]{2,1,0:T(8,128)} custom-call(s32[16]{0:T(128)} %stack.110.dest_ref, f32[2,4,128,128]{3,2,1,0:T(8,128)} %get-tuple-element.118.refs_0_, f32[1,4,128,128]{3,2,1,0:T(8,128)} %copy-done.34, f32[2,4,128,128]{3,2,1,0:T(8,128)} %copy-done.15, f32[2,4,128,128]{3,2,1,0:T(8,128)} %copy-done.11, f32[2,4,128,128]{3,2,1,0:T(8,128)} %copy-done.18, ...), custom_call_target="tpu_custom_call" | custom-call | bytes 8388608 | tf_op jit(solution)/shard_map/unpack/pallas_call | solution.py:468
  248.6 7.1 %collective-permute-start.38 = (f32[2,4,128,128]{3,2,1,0:T(8,128)S(1)}, f32[2,4,128,128]{3,2,1,0:T(8,128)S(1)}, u32[]{:S(2)}, u32[]{:S(2)}) collective-permute-start(f32[2,4,128,128]{3,2,1,0:T(8,128)S(1)} %pad_maximum_fusion.8), channel_id=1, source_target_pairs={{0,1},{1,0},{2,3},{3,2},{4,5},{5,4},{6,7},{7,6},{8,9},{9,8},{10,11... | collective-permute-start | bytes 1572872 | tf_op jit(solution)/shard_map/ppermute | solution.py:487
  260.4 4.8 %unpack.3 = f32[8,2048,128]{2,1,0:T(8,128)} custom-call(s32[16]{0:T(128)} %stack.110.dest_ref, f32[2,4,128,128]{3,2,1,0:T(8,128)} %get-tuple-element.102.refs_0_, f32[1,4,128,128]{3,2,1,0:T(8,128)} %copy-done.35, f32[2,4,128,128]{3,2,1,0:T(8,128)} %copy-done.17, f32[2,4,128,128]{3,2,1,0:T(8,128)} %copy-done.8, ...), custom_call_target="tpu_custom_call", output_to_operand_aliasing={{}: (17, {})} | custom-call | bytes 8388608 | tf_op jit(solution)/shard_map/unpack/pallas_call | solution.py:468
  (193 shorter events, 81.9 us)
Async XLA Ops:
  36.6 26.9 %collective-permute-start.6 = (f32[2,4,128,128]{3,2,1,0:T(8,128)}, f32[2,4,128,128]{3,2,1,0:T(8,128)S(1)}, u32[]{:S(2)}, u32[]{:S(2)}) collective-permute-start(f32[2,4,128,128]{3,2,1,0:T(8,128)} %get-tuple-element.76), channel_id=1, source_target_pairs={{0,8},{1,9},{2,10},{3,11},{4,12},{5,13},{6,14},{7,15},{8,0},{9,1},... | collective-permute-start | bytes 1572872 | tf_op jit(solution)/shard_map/ppermute | solution.py:487
  39.8 25.2 %collective-permute-start.7 = (f32[2,4,128,128]{3,2,1,0:T(8,128)}, f32[2,4,128,128]{3,2,1,0:T(8,128)S(1)}, u32[]{:S(2)}, u32[]{:S(2)}) collective-permute-start(f32[2,4,128,128]{3,2,1,0:T(8,128)} %get-tuple-element.77), channel_id=1, source_target_pairs={{0,4},{1,5},{2,6},{3,7},{4,0},{5,1},{6,2},{7,3},{8,12},{9,13},{10,... | collective-permute-start | bytes 1572872 | tf_op jit(solution)/shard_map/ppermute | solution.py:487
  45.9 20.6 %collective-permute-start.8 = (f32[2,4,128,128]{3,2,1,0:T(8,128)}, f32[2,4,128,128]{3,2,1,0:T(8,128)S(1)}, u32[]{:S(2)}, u32[]{:S(2)}) collective-permute-start(f32[2,4,128,128]{3,2,1,0:T(8,128)} %get-tuple-element.78), channel_id=1, source_target_pairs={{0,10},{1,11},{2,12},{3,13},{4,14},{5,15},{6,8},{7,9},{8,2},{9,3},... | collective-permute-start | bytes 1572872 | tf_op jit(solution)/shard_map/ppermute | solution.py:487
  45.9 20.6 %collective-permute-start.9 = (f32[2,4,128,128]{3,2,1,0:T(8,128)}, f32[2,4,128,128]{3,2,1,0:T(8,128)S(1)}, u32[]{:S(2)}, u32[]{:S(2)}) collective-permute-start(f32[2,4,128,128]{3,2,1,0:T(8,128)} %get-tuple-element.79), channel_id=1, source_target_pairs={{0,6},{1,7},{2,0},{3,1},{4,2},{5,3},{6,4},{7,5},{8,14},{9,15},{10,... | collective-permute-start | bytes 1572872 | tf_op jit(solution)/shard_map/ppermute | solution.py:487
  65.0 23.8 %collective-permute-start.12 = (f32[2,4,128,128]{3,2,1,0:T(8,128)S(1)}, f32[2,4,128,128]{3,2,1,0:T(8,128)}, u32[]{:S(2)}, u32[]{:S(2)}) collective-permute-start(f32[2,4,128,128]{3,2,1,0:T(8,128)S(1)} %copy-done.40), channel_id=1, source_target_pairs={{0,12},{1,13},{2,14},{3,15},{4,8},{5,9},{6,10},{7,11},{8,4},{9,5},... | collective-permute-start | bytes 1572872 | tf_op jit(solution)/shard_map/ppermute | solution.py:487
  88.8 64.3 %all-to-all-start = ((f32[16,4,128,128]{3,2,1,0:T(8,128)}), f32[16,4,128,128]{3,2,1,0:T(8,128)}, u32[]{:S(2)}, u32[]{:S(2)}) async-start(f32[16,4,128,128]{3,2,1,0:T(8,128)} %forecast.3.refs_16_), calls=%async_computation | async-start | bytes 8388608 | tf_op jit(solution)/shard_map/all_to_all | solution.py:629
  133.4 33.3 %collective-permute-start.18 = (f32[2,4,128,128]{3,2,1,0:T(8,128)}, f32[2,4,128,128]{3,2,1,0:T(8,128)S(1)}, u32[]{:S(2)}, u32[]{:S(2)}) collective-permute-start(f32[2,4,128,128]{3,2,1,0:T(8,128)} %get-tuple-element.103), channel_id=1, source_target_pairs={{0,8},{1,9},{2,10},{3,11},{4,12},{5,13},{6,14},{7,15},{8,0},{9,1},... | collective-permute-start | bytes 1572872 | tf_op jit(solution)/shard_map/ppermute | solution.py:487
  137.0 29.9 %collective-permute-start.19 = (f32[2,4,128,128]{3,2,1,0:T(8,128)}, f32[2,4,128,128]{3,2,1,0:T(8,128)S(1)}, u32[]{:S(2)}, u32[]{:S(2)}) collective-permute-start(f32[2,4,128,128]{3,2,1,0:T(8,128)} %get-tuple-element.104), channel_id=1, source_target_pairs={{0,4},{1,5},{2,6},{3,7},{4,0},{5,1},{6,2},{7,3},{8,12},{9,13},{10,... | collective-permute-start | bytes 1572872 | tf_op jit(solution)/shard_map/ppermute | solution.py:487
  139.7 31.6 %collective-permute-start.20 = (f32[2,4,128,128]{3,2,1,0:T(8,128)}, f32[2,4,128,128]{3,2,1,0:T(8,128)S(1)}, u32[]{:S(2)}, u32[]{:S(2)}) collective-permute-start(f32[2,4,128,128]{3,2,1,0:T(8,128)} %get-tuple-element.105), channel_id=1, source_target_pairs={{0,14},{1,15},{2,8},{3,9},{4,10},{5,11},{6,12},{7,13},{8,6},{9,7},... | collective-permute-start | bytes 1572872 | tf_op jit(solution)/shard_map/ppermute | solution.py:487
  140.6 35.0 %collective-permute-start.21 = (f32[2,4,128,128]{3,2,1,0:T(8,128)}, f32[2,4,128,128]{3,2,1,0:T(8,128)}, u32[]{:S(2)}, u32[]{:S(2)}) collective-permute-start(f32[2,4,128,128]{3,2,1,0:T(8,128)} %get-tuple-element.106), channel_id=1, source_target_pairs={{0,2},{1,3},{2,4},{3,5},{4,6},{5,7},{6,0},{7,1},{8,10},{9,11},{10,... | collective-permute-start | bytes 1572872 | tf_op jit(solution)/shard_map/ppermute | solution.py:487
  162.1 24.9 %collective-permute-start.22 = (f32[2,4,128,128]{3,2,1,0:T(8,128)}, f32[2,4,128,128]{3,2,1,0:T(8,128)S(1)}, u32[]{:S(2)}, u32[]{:S(2)}) collective-permute-start(f32[2,4,128,128]{3,2,1,0:T(8,128)} %get-tuple-element.107), channel_id=1, source_target_pairs={{0,10},{1,11},{2,12},{3,13},{4,14},{5,15},{6,8},{7,9},{8,2},{9,3},... | collective-permute-start | bytes 1572872 | tf_op jit(solution)/shard_map/ppermute | solution.py:487
  166.7 20.3 %collective-permute-start.23 = (f32[2,4,128,128]{3,2,1,0:T(8,128)}, f32[2,4,128,128]{3,2,1,0:T(8,128)S(1)}, u32[]{:S(2)}, u32[]{:S(2)}) collective-permute-start(f32[2,4,128,128]{3,2,1,0:T(8,128)} %get-tuple-element.108), channel_id=1, source_target_pairs={{0,6},{1,7},{2,0},{3,1},{4,2},{5,3},{6,4},{7,5},{8,14},{9,15},{10,... | collective-permute-start | bytes 1572872 | tf_op jit(solution)/shard_map/ppermute | solution.py:487
  167.0 31.3 %collective-permute-start.24 = (f32[2,4,128,128]{3,2,1,0:T(8,128)}, f32[2,4,128,128]{3,2,1,0:T(8,128)S(1)}, u32[]{:S(2)}, u32[]{:S(2)}) collective-permute-start(f32[2,4,128,128]{3,2,1,0:T(8,128)} %get-tuple-element.109), channel_id=1, source_target_pairs={{0,12},{1,13},{2,14},{3,15},{4,8},{5,9},{6,10},{7,11},{8,4},{9,5},... | collective-permute-start | bytes 1572872 | tf_op jit(solution)/shard_map/ppermute | solution.py:487
  171.4 34.4 %collective-permute-start.25 = (f32[2,4,128,128]{3,2,1,0:T(8,128)}, f32[2,4,128,128]{3,2,1,0:T(8,128)S(1)}, u32[]{:S(2)}, u32[]{:S(2)}) collective-permute-start(f32[2,4,128,128]{3,2,1,0:T(8,128)} %get-tuple-element.110), channel_id=1, source_target_pairs={{0,8},{1,9},{2,10},{3,11},{4,12},{5,13},{6,14},{7,15},{8,0},{9,1},... | collective-permute-start | bytes 1572872 | tf_op jit(solution)/shard_map/ppermute | solution.py:487
  175.7 33.8 %collective-permute-start.26 = (f32[2,4,128,128]{3,2,1,0:T(8,128)}, f32[2,4,128,128]{3,2,1,0:T(8,128)S(1)}, u32[]{:S(2)}, u32[]{:S(2)}) collective-permute-start(f32[2,4,128,128]{3,2,1,0:T(8,128)} %get-tuple-element.111), channel_id=1, source_target_pairs={{0,4},{1,5},{2,6},{3,7},{4,0},{5,1},{6,2},{7,3},{8,12},{9,13},{10,... | collective-permute-start | bytes 1572872 | tf_op jit(solution)/shard_map/ppermute | solution.py:487
  186.9 24.0 %collective-permute-start.27 = (f32[2,4,128,128]{3,2,1,0:T(8,128)}, f32[2,4,128,128]{3,2,1,0:T(8,128)S(1)}, u32[]{:S(2)}, u32[]{:S(2)}) collective-permute-start(f32[2,4,128,128]{3,2,1,0:T(8,128)} %get-tuple-element.112), channel_id=1, source_target_pairs={{0,14},{1,15},{2,8},{3,9},{4,10},{5,11},{6,12},{7,13},{8,6},{9,7},... | collective-permute-start | bytes 1572872 | tf_op jit(solution)/shard_map/ppermute | solution.py:487
  186.9 33.8 %collective-permute-start.28 = (f32[2,4,128,128]{3,2,1,0:T(8,128)}, f32[2,4,128,128]{3,2,1,0:T(8,128)S(1)}, u32[]{:S(2)}, u32[]{:S(2)}) collective-permute-start(f32[2,4,128,128]{3,2,1,0:T(8,128)} %get-tuple-element.113), channel_id=1, source_target_pairs={{0,2},{1,3},{2,4},{3,5},{4,6},{5,7},{6,0},{7,1},{8,10},{9,11},{10,... | collective-permute-start | bytes 1572872 | tf_op jit(solution)/shard_map/ppermute | solution.py:487
  198.3 30.5 %collective-permute-start.37 = (f32[2,4,128,128]{3,2,1,0:T(8,128)}, f32[2,4,128,128]{3,2,1,0:T(8,128)S(1)}, u32[]{:S(2)}, u32[]{:S(2)}) collective-permute-start(f32[2,4,128,128]{3,2,1,0:T(8,128)} %get-tuple-element.128), channel_id=1, source_target_pairs={{0,6},{1,7},{2,0},{3,1},{4,2},{5,3},{6,4},{7,5},{8,14},{9,15},{10,... | collective-permute-start | bytes 1572872 | tf_op jit(solution)/shard_map/ppermute | solution.py:487
  205.7 19.3 %collective-permute-start.31 = (f32[1,4,128,128]{3,2,1,0:T(8,128)S(1)}, f32[1,4,128,128]{3,2,1,0:T(8,128)S(1)}, u32[]{:S(2)}, u32[]{:S(2)}) collective-permute-start(f32[1,4,128,128]{3,2,1,0:T(8,128)S(1)} %slice.85), channel_id=1, source_target_pairs={{0,1},{1,0},{2,3},{3,2},{4,5},{5,4},{6,7},{7,6},{8,9},{9,8},{10,11... | collective-permute-start | bytes 786440 | tf_op jit(solution)/shard_map/ppermute | solution.py:487
  221.9 18.6 %collective-permute-start.34 = (f32[2,4,128,128]{3,2,1,0:T(8,128)S(1)}, f32[2,4,128,128]{3,2,1,0:T(8,128)S(1)}, u32[]{:S(2)}, u32[]{:S(2)}) collective-permute-start(f32[2,4,128,128]{3,2,1,0:T(8,128)S(1)} %pad_maximum_fusion.7), channel_id=1, source_target_pairs={{0,1},{1,0},{2,3},{3,2},{4,5},{5,4},{6,7},{7,6},{8,9},{9,8},{10,11... | collective-permute-start | bytes 1572872 | tf_op jit(solution)/shard_map/ppermute | solution.py:487
  225.1 22.5 %collective-permute-start.36 = (f32[2,4,128,128]{3,2,1,0:T(8,128)}, f32[2,4,128,128]{3,2,1,0:T(8,128)}, u32[]{:S(2)}, u32[]{:S(2)}) collective-permute-start(f32[2,4,128,128]{3,2,1,0:T(8,128)} %get-tuple-element.126), channel_id=1, source_target_pairs={{0,10},{1,11},{2,12},{3,13},{4,14},{5,15},{6,8},{7,9},{8,2},{9,3},... | collective-permute-start | bytes 1572872 | tf_op jit(solution)/shard_map/ppermute | solution.py:487
  230.5 25.3 %collective-permute-start.39 = (f32[2,4,128,128]{3,2,1,0:T(8,128)}, f32[2,4,128,128]{3,2,1,0:T(8,128)}, u32[]{:S(2)}, u32[]{:S(2)}) collective-permute-start(f32[2,4,128,128]{3,2,1,0:T(8,128)} %get-tuple-element.129), channel_id=1, source_target_pairs={{0,12},{1,13},{2,14},{3,15},{4,8},{5,9},{6,10},{7,11},{8,4},{9,5},... | collective-permute-start | bytes 1572872 | tf_op jit(solution)/shard_map/ppermute | solution.py:487
  240.5 18.1 %collective-permute-start.30 = (f32[2,4,128,128]{3,2,1,0:T(8,128)}, f32[2,4,128,128]{3,2,1,0:T(8,128)S(1)}, u32[]{:S(2)}, u32[]{:S(2)}) collective-permute-start(f32[2,4,128,128]{3,2,1,0:T(8,128)} %pad_maximum_fusion.4), channel_id=1, source_target_pairs={{0,1},{1,0},{2,3},{3,2},{4,5},{5,4},{6,7},{7,6},{8,9},{9,8},{10,11... | collective-permute-start | bytes 1572872 | tf_op jit(solution)/shard_map/ppermute | solution.py:487
  241.1 17.4 %collective-permute-start.29 = (f32[2,4,128,128]{3,2,1,0:T(8,128)}, f32[2,4,128,128]{3,2,1,0:T(8,128)S(1)}, u32[]{:S(2)}, u32[]{:S(2)}) collective-permute-start(f32[2,4,128,128]{3,2,1,0:T(8,128)} %pad_maximum_fusion.3), channel_id=1, source_target_pairs={{0,1},{1,0},{2,3},{3,2},{4,5},{5,4},{6,7},{7,6},{8,9},{9,8},{10,11... | collective-permute-start | bytes 1572872 | tf_op jit(solution)/shard_map/ppermute | solution.py:487
  (61 other events, 1082.5 us)

commit v5 on v4

--- a/solution.py
+++ b/solution.py
@@ -647,8 +647,9 @@
     ready, analysed[EARLY:] = lax.optimization_barrier((ready, analysed[EARLY:]))
     arrived += travel(analysed[EARLY:], -1, EARLY)
     final = travel(ready[:EARLY], -1)
-    arrived[1:], final[1:] = lax.optimization_barrier((arrived[1:], final[1:]))
+    arrived[1:], final[1:3] = lax.optimization_barrier((arrived[1:], final[1:3]))
     traded += [trade(arrived, group) for group in GROUPS[1:]]
+    traded, ready[EARLY:] = lax.optimization_barrier((traded, ready[EARLY:]))
     result = unpack(settled(arrived, traded), None, dest, 0, total, members, rows)
     arrived = final + travel(ready[EARLY:], -1, EARLY)
     result, arrived[EARLY] = lax.optimization_barrier((result, arrived[EARLY]))

time: 267 us -> 268 us (level)
  waiting for transfers between devices: 81.2 us -> 97.3 us
  starting transfers between devices: 86.9 us -> 72.9 us
    ppermute x36, waiting for transfers between devices: 60.9 us -> 77 us  [hop(): lax.ppermute(value, 'mem', [(i, shifted(i, offset, sign)) for i in range(...]
    ppermute x36, starting transfers between devices: 71 us -> 57 us  [hop(): lax.ppermute(value, 'mem', [(i, shifted(i, offset, sign)) for i in range(...]
    unnamed x84 -> x88, local copies, waits for them, and re-layouts: 6.75 us -> 5.75 us
  transfers between devices with their start and end apart: 42 -> 42, of which waited for: 19 -> 19; matrix products, arithmetic and copies ran while one was open for 6% -> 5% of each run, Pallas kernels for 19% -> 19%
where the time goes in v5:
time: 268 us; the launch traced here: 267 us
  waiting for transfers between devices  97.3 us (36%)
  Pallas kernels  75.4 us (28%)
  starting transfers between devices  72.9 us (27%)
  local copies, waits for them, and re-layouts  14.8 us (6%)
  other arithmetic  5.61 us (2%)
    ppermute x36, waiting for transfers between devices, hop(): lax.ppermute(value, 'mem', [(i, shifted(i, offset, sign)) for i in range(...  77 us
    ppermute x36, starting transfers between devices, hop(): lax.ppermute(value, 'mem', [(i, shifted(i, offset, sign)) for i in range(...  57 us
    pallas_call x2, Pallas kernels, forecast(): pl.pallas_call(functools.partial(forecast_kernel, first, fields, rows, me...  23.9 us
    pallas_call x2, Pallas kernels, transform(): pl.pallas_call(transform_kernel, grid_spec=pltpu.PrefetchScalarGridSpec(n...  18 us
    all_to_all x1, waiting for transfers between devices, on_device(): lax.all_to_all(following[0], 'mem', split_axis=0, concat_axis=0, tiled=True)  12 us
    pallas_call x1, Pallas kernels, mixing_transposed(): pl.pallas_call(mixing_kernel, in_specs=[pl.BlockSpec(memory_space=pltpu.S...  11.4 us
    pallas_call x2, Pallas kernels, unpack(): pl.pallas_call(functools.partial(unpack_kernel, members, rows), grid=(fie...  9.69 us
    all_to_all x1, starting transfers between devices, on_device(): lax.all_to_all(following[0], 'mem', split_axis=0, concat_axis=0, tiled=True)  8.41 us
  transfers between devices with their start and end apart: 42, of which 19 were waited for; matrix products, arithmetic and copies ran while one was open for 5% of the time, Pallas kernels for 19%

profile of v5, /device:TPU:1, one launch (start us, length us, event | category | flops | bytes accessed | tf_op | source)
XLA Modules:
  0.0 266.8 jit_solution(9933185279589376995)
XLA Ops:
  0.0 7.1 %pack_edges.1 = (f32[9,2,32,128]{3,2,1,0:T(8,128)}, f32[9,4,32,128]{3,2,1,0:T(8,128)}, f32[32,128]{1,0:T(8,128)}) custom-call(f32[8,32,64,128]{3,2,1,0:T(8,128)} %x_hbm.3, f32[64,128]{1,0:T(8,128)} %cx_ref.5, f32[64,128]{1,0:T(8,128)} %cy_ref.5, f32[64,128]{1,0:T(8,128)} %df_ref.5), custom_call_target="tpu_custom_call" | custom-call | flops 4194304 | bytes 16777216 | tf_op jit(solution)/shard_map/pack_edges/pallas_call | solution.py:123
  24.5 12.2 %forecast.2 = (f32[2,4,128,128]{3,2,1,0:T(8,128)}, f32[2,4,128,128]{3,2,1,0:T(8,128)}, f32[2,4,128,128]{3,2,1,0:T(8,128)}, f32[2,4,128,128]{3,2,1,0:T(8,128)}, f...) custom-call(s32[16]{0:T(128)} %stack.110.dest_ref, ...), custom_call_target="tpu_custom_call" | custom-call | flops 18874368 | bytes 8388608 | tf_op jit(solution)/shard_map/forecast/pallas_call | solution.py:297
  48.8 11.7 %forecast.3.refs_16_ = f32[16,4,128,128]{3,2,1,0:T(8,128)} custom-call(s32[16]{0:T(128)} %stack.110.dest_ref, f32[8,32,64,128]{3,2,1,0:T(8,128)} %x_hbm.3, f32[64,128]{1,0:T(8,128)} %cx_ref.5, f32[64,128]{1,0:T(8,128)} %cy_ref.5, f32[64,128]{1,0:T(8,128)} %df_ref.5, f32[9,2,32,128]{3,2,1,0:T(8,128)} %get-tuple-element.74.own_ref, ...), custom_call_target="tpu_custom_call" | custom-call | flops 18874368 | bytes 8388608 | tf_op jit(solution)/shard_map/forecast/pallas_call | solution.py:297
  66.5 10.8 %collective-permute-done.10.refs_10_ = f32[2,4,128,128]{3,2,1,0:T(8,128)S(1)} collective-permute-done((f32[2,4,128,128]{3,2,1,0:T(8,128)}, f32[2,4,128,128]{3,2,1,0:T(8,128)S(1)}, u32[]{:S(2)}, u32[]{:S(2)}) %collective-permute-start.10) | collective-permute-done | bytes 524320 | tf_op jit(solution)/shard_map/ppermute | solution.py:487
  78.3 10.5 %collective-permute-done.12.refs_14_ = f32[2,4,128,128]{3,2,1,0:T(8,128)} collective-permute-done((f32[2,4,128,128]{3,2,1,0:T(8,128)}, f32[2,4,128,128]{3,2,1,0:T(8,128)}, u32[]{:S(2)}, u32[]{:S(2)}) %collective-permute-start.12) | collective-permute-done | bytes 524320 | tf_op jit(solution)/shard_map/ppermute | solution.py:487
  88.8 8.4 %all-to-all-start = ((f32[16,4,128,128]{3,2,1,0:T(8,128)}), f32[16,4,128,128]{3,2,1,0:T(8,128)}, u32[]{:S(2)}, u32[]{:S(2)}) async-start(f32[16,4,128,128]{3,2,1,0:T(8,128)} %forecast.3.refs_16_), calls=%async_computation | async-start | bytes 8388608 | tf_op jit(solution)/shard_map/all_to_all | solution.py:629
  107.7 5.3 %sample.1.raw_ref = f32[512,256]{1,0:T(8,128)} custom-call(s32[1,256]{1,0:T(1,128)} %fusion.5.place_ref, f32[2,4,128,128]{3,2,1,0:T(8,128)} %get-tuple-element.77.refs_0_, f32[1,4,128,128]{3,2,1,0:T(8,128)} %copy-done.33, f32[2,4,128,128]{3,2,1,0:T(8,128)} %copy-done.23, f32[2,4,128,128]{3,2,1,0:T(8,128)} %copy-done.12, f32[2,4,128,128]{3,2,1,0:T(8,128)} %copy-done.25, ...), custom_call_target="tpu_custom_call" | custom-call | flops 1610612736 | bytes 4194304 | tf_op jit(solution)/shard_map/sample/pallas_call | solution.py:382
  113.0 11.4 %mixing.1.mix_ref = f32[512,512]{1,0:T(8,128)} custom-call(s32[1]{0:T(128)} %bitcast.28.count_ref, f32[512,256]{1,0:T(8,128)} %sample.1.raw_ref, f32[1,256]{1,0:T(1,128)} %get-tuple-element.143.value_ref, f32[1,256]{1,0:T(1,128)} %get-tuple-element.144.precision_ref, s32[1,256]{1,0:T(1,128)} %fusion.4.class_ref), custom_call_target="tpu_custom_call" | custom-call | flops 4026531840 | bytes 1048576 | tf_op jit(solution)/shard_map/mixing/pallas_call | solution.py:564
  124.4 8.9 %transform.3 = (f32[2,4,128,128]{3,2,1,0:T(8,128)}, f32[2,4,128,128]{3,2,1,0:T(8,128)}, f32[2,4,128,128]{3,2,1,0:T(8,128)}, f32[2,4,128,128]{3,2,1,0:T(8,128)}, ...) custom-call(s32[16]{0:T(128)} %constant.553.clone.places_ref, ...), custom_call_target="tpu_custom_call" | custom-call | flops 3221225472 | bytes 8388608 | tf_op jit(solution)/shard_map/transform/pallas_call | solution.py:429
  141.1 12.0 %all-to-all-done.refs_0_.refs_1_.refs_2_.refs_3_.refs_4_.refs_5_.refs_6_.refs_7_.refs_8_.refs_9_.refs_10_.refs_11_.refs_12_.refs_13_.refs_14_.refs_15_ = f32[16,4,128,128]{3,2,1,0:T(8,128)} async-done(((f32[16,4,128,128]{3,2,1,0:T(8,128)}), f32[16,4,128,128]{3,2,1,0:T(8,128)}, u32[]{:S(2)}, u32[]{:S(2)}) %all-to-all-start) | async-done | bytes 4194336 | tf_op jit(solution)/shard_map/all_to_all | solution.py:629
  153.2 9.0 %transform.2 = (f32[2,4,128,128]{3,2,1,0:T(8,128)}, f32[2,4,128,128]{3,2,1,0:T(8,128)}, f32[2,4,128,128]{3,2,1,0:T(8,128)}, f32[2,4,128,128]{3,2,1,0:T(8,128)}, ...) custom-call(s32[16]{0:T(128)} %stack.123.places_ref, ...), custom_call_target="tpu_custom_call" | custom-call | flops 3221225472 | bytes 8388608 | tf_op jit(solution)/shard_map/transform/pallas_call | solution.py:429
  162.2 4.6 %collective-permute-start.22 = (f32[2,4,128,128]{3,2,1,0:T(8,128)}, f32[2,4,128,128]{3,2,1,0:T(8,128)S(1)}, u32[]{:S(2)}, u32[]{:S(2)}) collective-permute-start(f32[2,4,128,128]{3,2,1,0:T(8,128)} %get-tuple-element.113), channel_id=1, source_target_pairs={{0,10},{1,11},{2,12},{3,13},{4,14},{5,15},{6,8},{7,9},{8,2},{9,3},... | collective-permute-start | bytes 1572872 | tf_op jit(solution)/shard_map/ppermute | solution.py:487
  172.0 3.6 %collective-permute-done.21.refs_8_ = f32[2,4,128,128]{3,2,1,0:T(8,128)S(1)} collective-permute-done((f32[2,4,128,128]{3,2,1,0:T(8,128)}, f32[2,4,128,128]{3,2,1,0:T(8,128)S(1)}, u32[]{:S(2)}, u32[]{:S(2)}) %collective-permute-start.21) | collective-permute-done | bytes 524320 | tf_op jit(solution)/shard_map/ppermute | solution.py:487
  175.7 6.6 %collective-permute-start.26 = (f32[2,4,128,128]{3,2,1,0:T(8,128)}, f32[2,4,128,128]{3,2,1,0:T(8,128)S(1)}, u32[]{:S(2)}, u32[]{:S(2)}) collective-permute-start(f32[2,4,128,128]{3,2,1,0:T(8,128)} %get-tuple-element.117), channel_id=1, source_target_pairs={{0,4},{1,5},{2,6},{3,7},{4,0},{5,1},{6,2},{7,3},{8,12},{9,13},{10,... | collective-permute-start | bytes 1572872 | tf_op jit(solution)/shard_map/ppermute | solution.py:487
  182.2 4.7 %collective-permute-done.22.refs_10_ = f32[2,4,128,128]{3,2,1,0:T(8,128)S(1)} collective-permute-done((f32[2,4,128,128]{3,2,1,0:T(8,128)}, f32[2,4,128,128]{3,2,1,0:T(8,128)S(1)}, u32[]{:S(2)}, u32[]{:S(2)}) %collective-permute-start.22) | collective-permute-done | bytes 524320 | tf_op jit(solution)/shard_map/ppermute | solution.py:487
  186.9 11.1 %collective-permute-done.24.refs_14_ = f32[2,4,128,128]{3,2,1,0:T(8,128)S(1)} collective-permute-done((f32[2,4,128,128]{3,2,1,0:T(8,128)S(1)}, f32[2,4,128,128]{3,2,1,0:T(8,128)S(1)}, u32[]{:S(2)}, u32[]{:S(2)}) %collective-permute-start.24) | collective-permute-done | bytes 524320 | tf_op jit(solution)/shard_map/ppermute | solution.py:487
  198.1 7.3 %collective-permute-done.25.refs_2_ = f32[2,4,128,128]{3,2,1,0:T(8,128)S(1)} collective-permute-done((f32[2,4,128,128]{3,2,1,0:T(8,128)}, f32[2,4,128,128]{3,2,1,0:T(8,128)S(1)}, u32[]{:S(2)}, u32[]{:S(2)}) %collective-permute-start.25) | collective-permute-done | bytes 524320 | tf_op jit(solution)/shard_map/ppermute | solution.py:487
  205.3 4.1 %collective-permute-done.26.refs_4_ = f32[2,4,128,128]{3,2,1,0:T(8,128)S(1)} collective-permute-done((f32[2,4,128,128]{3,2,1,0:T(8,128)}, f32[2,4,128,128]{3,2,1,0:T(8,128)S(1)}, u32[]{:S(2)}, u32[]{:S(2)}) %collective-permute-start.26) | collective-permute-done | bytes 524320 | tf_op jit(solution)/shard_map/ppermute | solution.py:487
  218.4 3.6 %collective-permute-start.36 = (f32[2,4,128,128]{3,2,1,0:T(8,128)}, f32[2,4,128,128]{3,2,1,0:T(8,128)}, u32[]{:S(2)}, u32[]{:S(2)}) collective-permute-start(f32[2,4,128,128]{3,2,1,0:T(8,128)} %get-tuple-element.138), channel_id=1, source_target_pairs={{0,10},{1,11},{2,12},{3,13},{4,14},{5,15},{6,8},{7,9},{8,2},{9,3},... | collective-permute-start | bytes 1572872 | tf_op jit(solution)/shard_map/ppermute | solution.py:487
  222.0 8.4 %collective-permute-done.28.refs_6_ = f32[2,4,128,128]{3,2,1,0:T(8,128)S(1)} collective-permute-done((f32[2,4,128,128]{3,2,1,0:T(8,128)}, f32[2,4,128,128]{3,2,1,0:T(8,128)S(1)}, u32[]{:S(2)}, u32[]{:S(2)}) %collective-permute-start.28) | collective-permute-done | bytes 524320 | tf_op jit(solution)/shard_map/ppermute | solution.py:487
  232.6 3.8 %collective-permute-start.39 = (f32[2,4,128,128]{3,2,1,0:T(8,128)}, f32[2,4,128,128]{3,2,1,0:T(8,128)}, u32[]{:S(2)}, u32[]{:S(2)}) collective-permute-start(f32[2,4,128,128]{3,2,1,0:T(8,128)} %get-tuple-element.141), channel_id=1, source_target_pairs={{0,12},{1,13},{2,14},{3,15},{4,8},{5,9},{6,10},{7,11},{8,4},{9,5},... | collective-permute-start | bytes 1572872 | tf_op jit(solution)/shard_map/ppermute | solution.py:487
  240.9 4.9 %unpack.2.refs_16_ = f32[8,2048,128]{2,1,0:T(8,128)} custom-call(s32[16]{0:T(128)} %stack.110.dest_ref, f32[2,4,128,128]{3,2,1,0:T(8,128)} %get-tuple-element.122.refs_0_, f32[1,4,128,128]{3,2,1,0:T(8,128)} %copy-done.34, f32[2,4,128,128]{3,2,1,0:T(8,128)} %copy-done.15, f32[2,4,128,128]{3,2,1,0:T(8,128)} %copy-done.7, f32[2,4,128,128]{3,2,1,0:T(8,128)} %copy-done.16, ...), custom_call_target="tpu_custom_call" | custom-call | bytes 8388608 | tf_op jit(solution)/shard_map/unpack/pallas_call | solution.py:468
  248.5 8.2 %collective-permute-done.39.refs_14_ = f32[2,4,128,128]{3,2,1,0:T(8,128)} collective-permute-done((f32[2,4,128,128]{3,2,1,0:T(8,128)}, f32[2,4,128,128]{3,2,1,0:T(8,128)}, u32[]{:S(2)}, u32[]{:S(2)}) %collective-permute-start.39) | collective-permute-done | bytes 524320 | tf_op jit(solution)/shard_map/ppermute | solution.py:487
  261.7 4.8 %unpack.3 = f32[8,2048,128]{2,1,0:T(8,128)} custom-call(s32[16]{0:T(128)} %stack.110.dest_ref, f32[2,4,128,128]{3,2,1,0:T(8,128)} %get-tuple-element.108.refs_0_, f32[1,4,128,128]{3,2,1,0:T(8,128)} %copy-done.36, f32[2,4,128,128]{3,2,1,0:T(8,128)} %copy-done.20, f32[2,4,128,128]{3,2,1,0:T(8,128)} %copy-done.10, ...), custom_call_target="tpu_custom_call", output_to_operand_aliasing={{}: (17, {})} | custom-call | bytes 8388608 | tf_op jit(solution)/shard_map/unpack/pallas_call | solution.py:468
  (196 shorter events, 83.0 us)
Async XLA Ops:
  7.1 16.5 %collective-permute-start.2 = (f32[9,4,32,128]{3,2,1,0:T(8,128)}, f32[9,4,32,128]{3,2,1,0:T(8,128)S(1)}, u32[]{:S(2)}, u32[]{:S(2)}) collective-permute-start(f32[9,4,32,128]{3,2,1,0:T(8,128)} %get-tuple-element.75), channel_id=1, source_target_pairs={{0,64},{64,0},{1,65},{65,1},{2,66},{66,2},{3,67},{67,3},{4,68},{68... | collective-permute-start | bytes 1769480 | tf_op jit(solution)/shard_map/ppermute | solution.py:164
  36.7 26.9 %collective-permute-start.6 = (f32[2,4,128,128]{3,2,1,0:T(8,128)}, f32[2,4,128,128]{3,2,1,0:T(8,128)S(1)}, u32[]{:S(2)}, u32[]{:S(2)}) collective-permute-start(f32[2,4,128,128]{3,2,1,0:T(8,128)} %get-tuple-element.82), channel_id=1, source_target_pairs={{0,8},{1,9},{2,10},{3,11},{4,12},{5,13},{6,14},{7,15},{8,0},{9,1},... | collective-permute-start | bytes 1572872 | tf_op jit(solution)/shard_map/ppermute | solution.py:487
  39.8 25.2 %collective-permute-start.7 = (f32[2,4,128,128]{3,2,1,0:T(8,128)}, f32[2,4,128,128]{3,2,1,0:T(8,128)S(1)}, u32[]{:S(2)}, u32[]{:S(2)}) collective-permute-start(f32[2,4,128,128]{3,2,1,0:T(8,128)} %get-tuple-element.83), channel_id=1, source_target_pairs={{0,4},{1,5},{2,6},{3,7},{4,0},{5,1},{6,2},{7,3},{8,12},{9,13},{10,... | collective-permute-start | bytes 1572872 | tf_op jit(solution)/shard_map/ppermute | solution.py:487
  45.9 20.6 %collective-permute-start.8 = (f32[2,4,128,128]{3,2,1,0:T(8,128)}, f32[2,4,128,128]{3,2,1,0:T(8,128)S(1)}, u32[]{:S(2)}, u32[]{:S(2)}) collective-permute-start(f32[2,4,128,128]{3,2,1,0:T(8,128)} %get-tuple-element.84), channel_id=1, source_target_pairs={{0,10},{1,11},{2,12},{3,13},{4,14},{5,15},{6,8},{7,9},{8,2},{9,3},... | collective-permute-start | bytes 1572872 | tf_op jit(solution)/shard_map/ppermute | solution.py:487
  45.9 20.6 %collective-permute-start.9 = (f32[2,4,128,128]{3,2,1,0:T(8,128)}, f32[2,4,128,128]{3,2,1,0:T(8,128)S(1)}, u32[]{:S(2)}, u32[]{:S(2)}) collective-permute-start(f32[2,4,128,128]{3,2,1,0:T(8,128)} %get-tuple-element.85), channel_id=1, source_target_pairs={{0,6},{1,7},{2,0},{3,1},{4,2},{5,3},{6,4},{7,5},{8,14},{9,15},{10,... | collective-permute-start | bytes 1572872 | tf_op jit(solution)/shard_map/ppermute | solution.py:487
  60.6 16.8 %collective-permute-start.10 = (f32[2,4,128,128]{3,2,1,0:T(8,128)}, f32[2,4,128,128]{3,2,1,0:T(8,128)S(1)}, u32[]{:S(2)}, u32[]{:S(2)}) collective-permute-start(f32[2,4,128,128]{3,2,1,0:T(8,128)} %get-tuple-element.86), channel_id=1, source_target_pairs={{0,14},{1,15},{2,8},{3,9},{4,10},{5,11},{6,12},{7,13},{8,6},{9,7},... | collective-permute-start | bytes 1572872 | tf_op jit(solution)/shard_map/ppermute | solution.py:487
  65.0 23.8 %collective-permute-start.12 = (f32[2,4,128,128]{3,2,1,0:T(8,128)}, f32[2,4,128,128]{3,2,1,0:T(8,128)}, u32[]{:S(2)}, u32[]{:S(2)}) collective-permute-start(f32[2,4,128,128]{3,2,1,0:T(8,128)} %get-tuple-element.88), channel_id=1, source_target_pairs={{0,12},{1,13},{2,14},{3,15},{4,8},{5,9},{6,10},{7,11},{8,4},{9,5},... | collective-permute-start | bytes 1572872 | tf_op jit(solution)/shard_map/ppermute | solution.py:487
  88.8 64.3 %all-to-all-start = ((f32[16,4,128,128]{3,2,1,0:T(8,128)}), f32[16,4,128,128]{3,2,1,0:T(8,128)}, u32[]{:S(2)}, u32[]{:S(2)}) async-start(f32[16,4,128,128]{3,2,1,0:T(8,128)} %forecast.3.refs_16_), calls=%async_computation | async-start | bytes 8388608 | tf_op jit(solution)/shard_map/all_to_all | solution.py:629
  133.4 33.4 %collective-permute-start.18 = (f32[2,4,128,128]{3,2,1,0:T(8,128)}, f32[2,4,128,128]{3,2,1,0:T(8,128)S(1)}, u32[]{:S(2)}, u32[]{:S(2)}) collective-permute-start(f32[2,4,128,128]{3,2,1,0:T(8,128)} %get-tuple-element.109), channel_id=1, source_target_pairs={{0,8},{1,9},{2,10},{3,11},{4,12},{5,13},{6,14},{7,15},{8,0},{9,1},... | collective-permute-start | bytes 1572872 | tf_op jit(solution)/shard_map/ppermute | solution.py:487
  136.3 30.8 %collective-permute-start.19 = (f32[2,4,128,128]{3,2,1,0:T(8,128)}, f32[2,4,128,128]{3,2,1,0:T(8,128)S(1)}, u32[]{:S(2)}, u32[]{:S(2)}) collective-permute-start(f32[2,4,128,128]{3,2,1,0:T(8,128)} %get-tuple-element.110), channel_id=1, source_target_pairs={{0,4},{1,5},{2,6},{3,7},{4,0},{5,1},{6,2},{7,3},{8,12},{9,13},{10,... | collective-permute-start | bytes 1572872 | tf_op jit(solution)/shard_map/ppermute | solution.py:487
  139.0 32.3 %collective-permute-start.20 = (f32[2,4,128,128]{3,2,1,0:T(8,128)}, f32[2,4,128,128]{3,2,1,0:T(8,128)S(1)}, u32[]{:S(2)}, u32[]{:S(2)}) collective-permute-start(f32[2,4,128,128]{3,2,1,0:T(8,128)} %get-tuple-element.111), channel_id=1, source_target_pairs={{0,14},{1,15},{2,8},{3,9},{4,10},{5,11},{6,12},{7,13},{8,6},{9,7},... | collective-permute-start | bytes 1572872 | tf_op jit(solution)/shard_map/ppermute | solution.py:487
  139.9 35.7 %collective-permute-start.21 = (f32[2,4,128,128]{3,2,1,0:T(8,128)}, f32[2,4,128,128]{3,2,1,0:T(8,128)S(1)}, u32[]{:S(2)}, u32[]{:S(2)}) collective-permute-start(f32[2,4,128,128]{3,2,1,0:T(8,128)} %get-tuple-element.112), channel_id=1, source_target_pairs={{0,2},{1,3},{2,4},{3,5},{4,6},{5,7},{6,0},{7,1},{8,10},{9,11},{10,... | collective-permute-start | bytes 1572872 | tf_op jit(solution)/shard_map/ppermute | solution.py:487
  162.2 24.7 %collective-permute-start.22 = (f32[2,4,128,128]{3,2,1,0:T(8,128)}, f32[2,4,128,128]{3,2,1,0:T(8,128)S(1)}, u32[]{:S(2)}, u32[]{:S(2)}) collective-permute-start(f32[2,4,128,128]{3,2,1,0:T(8,128)} %get-tuple-element.113), channel_id=1, source_target_pairs={{0,10},{1,11},{2,12},{3,13},{4,14},{5,15},{6,8},{7,9},{8,2},{9,3},... | collective-permute-start | bytes 1572872 | tf_op jit(solution)/shard_map/ppermute | solution.py:487
  166.8 20.1 %collective-permute-start.23 = (f32[2,4,128,128]{3,2,1,0:T(8,128)S(1)}, f32[2,4,128,128]{3,2,1,0:T(8,128)S(1)}, u32[]{:S(2)}, u32[]{:S(2)}) collective-permute-start(f32[2,4,128,128]{3,2,1,0:T(8,128)S(1)} %copy-done.42), channel_id=1, source_target_pairs={{0,6},{1,7},{2,0},{3,1},{4,2},{5,3},{6,4},{7,5},{8,14},{9,15},{10,... | collective-permute-start | bytes 1572872 | tf_op jit(solution)/shard_map/ppermute | solution.py:487
  167.2 30.9 %collective-permute-start.24 = (f32[2,4,128,128]{3,2,1,0:T(8,128)S(1)}, f32[2,4,128,128]{3,2,1,0:T(8,128)S(1)}, u32[]{:S(2)}, u32[]{:S(2)}) collective-permute-start(f32[2,4,128,128]{3,2,1,0:T(8,128)S(1)} %copy-done.41), channel_id=1, source_target_pairs={{0,12},{1,13},{2,14},{3,15},{4,8},{5,9},{6,10},{7,11},{8,4},{9,5},... | collective-permute-start | bytes 1572872 | tf_op jit(solution)/shard_map/ppermute | solution.py:487
  171.4 34.0 %collective-permute-start.25 = (f32[2,4,128,128]{3,2,1,0:T(8,128)}, f32[2,4,128,128]{3,2,1,0:T(8,128)S(1)}, u32[]{:S(2)}, u32[]{:S(2)}) collective-permute-start(f32[2,4,128,128]{3,2,1,0:T(8,128)} %get-tuple-element.116), channel_id=1, source_target_pairs={{0,8},{1,9},{2,10},{3,11},{4,12},{5,13},{6,14},{7,15},{8,0},{9,1},... | collective-permute-start | bytes 1572872 | tf_op jit(solution)/shard_map/ppermute | solution.py:487
  175.7 33.7 %collective-permute-start.26 = (f32[2,4,128,128]{3,2,1,0:T(8,128)}, f32[2,4,128,128]{3,2,1,0:T(8,128)S(1)}, u32[]{:S(2)}, u32[]{:S(2)}) collective-permute-start(f32[2,4,128,128]{3,2,1,0:T(8,128)} %get-tuple-element.117), channel_id=1, source_target_pairs={{0,4},{1,5},{2,6},{3,7},{4,0},{5,1},{6,2},{7,3},{8,12},{9,13},{10,... | collective-permute-start | bytes 1572872 | tf_op jit(solution)/shard_map/ppermute | solution.py:487
  213.7 16.7 %collective-permute-start.28 = (f32[2,4,128,128]{3,2,1,0:T(8,128)}, f32[2,4,128,128]{3,2,1,0:T(8,128)S(1)}, u32[]{:S(2)}, u32[]{:S(2)}) collective-permute-start(f32[2,4,128,128]{3,2,1,0:T(8,128)} %get-tuple-element.120), channel_id=1, source_target_pairs={{0,14},{1,15},{2,8},{3,9},{4,10},{5,11},{6,12},{7,13},{8,6},{9,7},... | collective-permute-start | bytes 1572872 | tf_op jit(solution)/shard_map/ppermute | solution.py:487
  216.8 15.0 %collective-permute-start.29 = (f32[2,4,128,128]{3,2,1,0:T(8,128)}, f32[2,4,128,128]{3,2,1,0:T(8,128)S(1)}, u32[]{:S(2)}, u32[]{:S(2)}) collective-permute-start(f32[2,4,128,128]{3,2,1,0:T(8,128)} %get-tuple-element.121), channel_id=1, source_target_pairs={{0,2},{1,3},{2,4},{3,5},{4,6},{5,7},{6,0},{7,1},{8,10},{9,11},{10,... | collective-permute-start | bytes 1572872 | tf_op jit(solution)/shard_map/ppermute | solution.py:487
  218.4 27.4 %collective-permute-start.36 = (f32[2,4,128,128]{3,2,1,0:T(8,128)}, f32[2,4,128,128]{3,2,1,0:T(8,128)}, u32[]{:S(2)}, u32[]{:S(2)}) collective-permute-start(f32[2,4,128,128]{3,2,1,0:T(8,128)} %get-tuple-element.138), channel_id=1, source_target_pairs={{0,10},{1,11},{2,12},{3,13},{4,14},{5,15},{6,8},{7,9},{8,2},{9,3},... | collective-permute-start | bytes 1572872 | tf_op jit(solution)/shard_map/ppermute | solution.py:487
  222.0 24.8 %collective-permute-start.37 = (f32[2,4,128,128]{3,2,1,0:T(8,128)}, f32[2,4,128,128]{3,2,1,0:T(8,128)}, u32[]{:S(2)}, u32[]{:S(2)}) collective-permute-start(f32[2,4,128,128]{3,2,1,0:T(8,128)} %get-tuple-element.140), channel_id=1, source_target_pairs={{0,6},{1,7},{2,0},{3,1},{4,2},{5,3},{6,4},{7,5},{8,14},{9,15},{10,... | collective-permute-start | bytes 1572872 | tf_op jit(solution)/shard_map/ppermute | solution.py:487
  232.6 24.1 %collective-permute-start.39 = (f32[2,4,128,128]{3,2,1,0:T(8,128)}, f32[2,4,128,128]{3,2,1,0:T(8,128)}, u32[]{:S(2)}, u32[]{:S(2)}) collective-permute-start(f32[2,4,128,128]{3,2,1,0:T(8,128)} %get-tuple-element.141), channel_id=1, source_target_pairs={{0,12},{1,13},{2,14},{3,15},{4,8},{5,9},{6,10},{7,11},{8,4},{9,5},... | collective-permute-start | bytes 1572872 | tf_op jit(solution)/shard_map/ppermute | solution.py:487
  237.3 21.9 %collective-permute-start.30 = (f32[2,4,128,128]{3,2,1,0:T(8,128)}, f32[2,4,128,128]{3,2,1,0:T(8,128)S(1)}, u32[]{:S(2)}, u32[]{:S(2)}) collective-permute-start(f32[2,4,128,128]{3,2,1,0:T(8,128)} %pad_maximum_fusion.4), channel_id=1, source_target_pairs={{0,1},{1,0},{2,3},{3,2},{4,5},{5,4},{6,7},{7,6},{8,9},{9,8},{10,11... | collective-permute-start | bytes 1572872 | tf_op jit(solution)/shard_map/ppermute | solution.py:487
  240.9 18.3 %collective-permute-start.27 = (f32[2,4,128,128]{3,2,1,0:T(8,128)}, f32[2,4,128,128]{3,2,1,0:T(8,128)S(1)}, u32[]{:S(2)}, u32[]{:S(2)}) collective-permute-start(f32[2,4,128,128]{3,2,1,0:T(8,128)} %pad_maximum_fusion.3), channel_id=1, source_target_pairs={{0,1},{1,0},{2,3},{3,2},{4,5},{5,4},{6,7},{7,6},{8,9},{9,8},{10,11... | collective-permute-start | bytes 1572872 | tf_op jit(solution)/shard_map/ppermute | solution.py:487
  (62 other events, 1113.9 us)
